TPU v7x, 128 devices: a whole 4x4x4 slice. The times are simulated.
128 devices in a mesh: row: 16 (over y, x), col: 8 (over z, core).
Axes of the slice: x: 4, y: 4, z: 4, core: 2. Of those that a mesh axis runs over, the one named last changes fastest.
Arguments:
- matrix: float32 [16384, 16384], P('row', 'col'), as said below
Outputs:
- factored: float32 [16384, 16384], P('row', 'col')
Inputs may be any that keep to these rules, and one draw needn't show every extreme that they name: matrix, read as A by the first step, is symmetric and positive definite.
All inputs are finite; a program needn't handle non-finite values.
Results may differ from a plain program's by a relative error of at most 0.00028.
Values sent between devices are 32-bit elements; how exact they have to be, the bound alone decides.
No kernel may reach another device: no remote copies, remote signals or barrier semaphores. Data moves between devices by JAX's collectives and lax.ppermute only.
A program may use at most 128 MiB of HBM per device.

v0:
```python
import jax
import jax.numpy as jnp
from jax import lax
from jax.sharding import PartitionSpec as P

TILE = 256


def from_root(value, axis, source):
    kept = jnp.where(lax.axis_index(axis) == source, value, 0).astype(value.dtype)
    return lax.psum(kept, axis)


def factor_panel(column, panel_index, row_global, own_col):
    grid_rows = lax.axis_size("row")
    grid_cols = lax.axis_size("col")
    tile_rows = column.shape[0] // TILE
    local_row = panel_index // grid_rows
    diag_local = lax.slice_in_dim(column, local_row * TILE, (local_row + 1) * TILE, axis=0)
    diag = from_root(diag_local, "row", panel_index % grid_rows)
    identity = jnp.eye(TILE, dtype=jnp.float32)
    diag = jnp.where(own_col == panel_index % grid_cols, diag, identity)
    factor = jnp.linalg.cholesky(diag)
    solved = jax.scipy.linalg.solve_triangular(factor, column.T, lower=True).T
    below = jnp.where((row_global > panel_index)[:, None], solved, 0.0)
    stacked_factor = jnp.tile(factor, (tile_rows, 1))
    panel = jnp.where((row_global == panel_index)[:, None], stacked_factor, below)
    return from_root(panel, "col", panel_index % grid_cols)


def panel_columns(panel, own_col, tile_cols):
    grid_rows = lax.axis_size("row")
    grid_cols = lax.axis_size("col")
    tile_rows = panel.shape[0] // TILE
    whole = lax.all_gather(panel, "row", axis=0, tiled=True)
    ordered = whole.reshape(grid_rows, tile_rows, TILE, TILE).transpose(1, 0, 2, 3)
    ordered = ordered.reshape(tile_cols, grid_cols, TILE, TILE)
    picked = lax.dynamic_index_in_dim(ordered, own_col, axis=1, keepdims=False)
    return picked.reshape(tile_cols * TILE, TILE)


def apply_panel(block, panel, columns, panel_index, row_global, col_global):
    count = block.shape[1] // TILE
    left = jnp.where((row_global > panel_index)[:, None], panel, 0.0)
    right = jnp.where((col_global > panel_index)[:, None], columns, 0.0)
    block = block - jnp.dot(
        left, right.T, precision=lax.Precision.HIGHEST, preferred_element_type=jnp.float32
    )
    spread = jnp.tile(panel, (1, count))
    block = jnp.where((col_global == panel_index)[None, :], spread, block)
    upper = (row_global == panel_index)[:, None] & (col_global > panel_index)[None, :]
    return jnp.where(upper, 0.0, block)


def shards(matrix):
    grid_rows = lax.axis_size("row")
    grid_cols = lax.axis_size("col")
    own_row = lax.axis_index("row")
    own_col = lax.axis_index("col")
    tile_rows = matrix.shape[0] // TILE
    tile_cols = matrix.shape[1] // TILE
    row_global = jnp.repeat(jnp.arange(tile_rows, dtype=jnp.int32) * grid_rows + own_row, TILE)
    col_global = jnp.repeat(jnp.arange(tile_cols, dtype=jnp.int32) * grid_cols + own_col, TILE)
    current = matrix
    first_local = 0 // grid_cols
    panel_first = factor_panel(
        current[:, first_local * TILE : (first_local + 1) * TILE], 0, row_global, own_col
    )
    columns_first = panel_columns(panel_first, own_col, tile_cols)
    second_local = 1 // grid_cols
    current = apply_panel(current, panel_first, columns_first, 0, row_global, col_global)
    panel_second = factor_panel(
        current[:, second_local * TILE : (second_local + 1) * TILE], 1, row_global, own_col
    )
    columns_second = panel_columns(panel_second, own_col, tile_cols)
    return apply_panel(current, panel_second, columns_second, 1, row_global, col_global)


def solution(mesh):
    return jax.shard_map(
        shards,
        mesh=mesh,
        in_specs=(P("row", "col"),),
        out_specs=P("row", "col"),
        check_vma=False,
    )
```

profile of v0, /device:TPU:81, one launch (start us, length us, event | category | flops | bytes accessed | tf_op | source)
XLA Modules:
  0.0 793.3 jit_solution(10187298963584505124)
XLA Ops:
  6.5 9.2 %copy.11 = f32[1024,2048]{0,1:T(8,128)} copy(f32[1024,2048]{1,0:T(8,128)} %param.4) | data formatting | bytes 16777216 | tf_op args[0]
  15.8 1.7 slice_select_fusion.1
  19.0 81.3 %all-reduce.6.cloned.1.call-done = f32[256,256]{0,1:T(8,128)} async-done(((f32[256,256]{0,1:T(8,128)}), f32[256,256]{0,1:T(8,128)}) %all-reduce.6.cloned.1.call-update) | async-done | bytes 262160 | tf_op jit(solution)/shard_map/psum | solution.py:11
  100.5 11.7 %cholesky.130 = f32[128,128]{1,0:T(8,128)S(1)} custom-call(f32[128,128]{1,0:T(8,128)S(1)} %cholesky.194), custom_call_target="Cholesky" | custom-call | tf_op jit(solution)/shard_map/jit(cholesky)/cholesky | solution.py:23
  112.3 9.8 %custom-call.13 = f32[1,128,128]{1,2,0:T(8,128)S(1)} custom-call(f32[1,128,128]{2,1,0:T(8,128)S(1)} %get-tuple-element.54), custom_call_target="InvertDiagBlocksLowerTriangular" | custom-call | tf_op jit(solution)/shard_map/jit(cholesky)/cholesky | solution.py:23
  122.6 11.7 %cholesky.147 = f32[128,128]{1,0:T(8,128)S(1)} custom-call(f32[128,128]{1,0:T(8,128)S(1)} %convolution_subtract_fusion.3), custom_call_target="Cholesky" | custom-call | tf_op jit(solution)/shard_map/jit(cholesky)/cholesky | solution.py:23
  136.4 4.5 while.4
  137.6 1.3 bitcast_dynamic-update-slice_fusion.4
  139.6 1.3 bitcast_dynamic-update-slice_fusion.4
  140.9 19.7 %custom-call.14 = f32[2,128,128]{1,2,0:T(8,128)S(1)} custom-call(f32[2,128,128]{2,1,0:T(8,128)S(1)} %get-tuple-element.21), custom_call_target="InvertDiagBlocksLowerTriangular" | custom-call | tf_op jit(solution)/shard_map/jit(_solve_triangular)/triangular_solve | solution.py:24
  164.7 61.4 %all-reduce.8.cloned.1.call-done = f32[1024,256]{0,1:T(8,128)} async-done(((f32[1024,256]{0,1:T(8,128)}), f32[1024,256]{0,1:T(8,128)}) %all-reduce.8.cloned.1.call-update) | async-done | bytes 1048592 | tf_op jit(solution)/shard_map/psum | solution.py:11
  226.6 115.9 %all-gather.3.cloned.1.call-done = f32[16384,256]{0,1:T(8,128)} async-done(((f32[1024,256]{0,1:T(8,128)}), f32[16384,256]{0,1:T(8,128)}) %all-gather.3.cloned.1.call-update) | async-done | bytes 16777232 | tf_op jit(solution)/shard_map/all_gather | solution.py:35
  342.4 20.4 %reshape.119 = f32[16,4,256,256]{2,1,0,3:T(4,128)} reshape(f32[16384,256]{0,1:T(8,128)} %all-gather.3.cloned.1.call-done) | data formatting | bytes 33554432 | tf_op jit(solution)/shard_map/reshape | solution.py:36
  362.8 19.2 %copy.14 = f32[16,4,256,256]{3,2,0,1:T(8,128)} copy(f32[16,4,256,256]{2,1,0,3:T(4,128)} %reshape.119) | data formatting | bytes 33554432 | tf_op jit(solution)/shard_map/reshape | solution.py:36
  382.1 1.8 constant_dynamic-slice_fusion.3
  384.2 11.3 %fusion.1 = f32[1024,2048]{0,1:T(8,128)S(1)} fusion(f32[1024,2048]{0,1:T(8,128)} %copy.11, f32[2048,256]{1,0:T(8,128)S(1)} %bitcast_select_fusion.3, f32[1024,256]{0,1:T(8,128)S(1)} %copy-done.1, pred[2048]{0:T(1024)(128)(4,1)S(1)} %eq.75, pred[1024]{0:T(1024)(128)(4,1)S(1)} %eq.73, pred[2048]{0:T(1024)(128)(4,1)S(1)} %gt.59, pred[1024]{0:T(1024)(128)(4,1)S(1)} %gt.61), kind=kOutput, calls=%fused_computation.7 | convolution fusion | flops 6451101696 | bytes 19929088 | tf_op jit(solution)/shard_map/dot_general | solution.py:46
  395.5 3.4 copy-done
  401.2 79.6 %all-reduce.10.cloned.1.call-done = f32[256,256]{0,1:T(8,128)} async-done(((f32[256,256]{0,1:T(8,128)}), f32[256,256]{0,1:T(8,128)}) %all-reduce.10.cloned.1.call-update) | async-done | bytes 262160 | tf_op jit(solution)/shard_map/psum | solution.py:11
  481.1 11.7 %cholesky.164 = f32[128,128]{1,0:T(8,128)S(1)} custom-call(f32[128,128]{1,0:T(8,128)S(1)} %cholesky.197), custom_call_target="Cholesky" | custom-call | tf_op jit(solution)/shard_map/jit(cholesky)/cholesky | solution.py:23
  492.8 9.8 %custom-call.15 = f32[1,128,128]{1,2,0:T(8,128)S(1)} custom-call(f32[1,128,128]{2,1,0:T(8,128)S(1)} %get-tuple-element.50), custom_call_target="InvertDiagBlocksLowerTriangular" | custom-call | tf_op jit(solution)/shard_map/jit(cholesky)/cholesky | solution.py:23
  503.1 11.7 %cholesky.181 = f32[128,128]{1,0:T(8,128)S(1)} custom-call(f32[128,128]{1,0:T(8,128)S(1)} %convolution_subtract_fusion.2), custom_call_target="Cholesky" | custom-call | tf_op jit(solution)/shard_map/jit(cholesky)/cholesky | solution.py:23
  517.6 4.2 while.5
  518.4 1.3 bitcast_dynamic-update-slice_fusion.5
  520.5 1.3 bitcast_dynamic-update-slice_fusion.5
  521.8 19.7 %custom-call.16 = f32[2,128,128]{1,2,0:T(8,128)S(1)} custom-call(f32[2,128,128]{2,1,0:T(8,128)S(1)} %get-tuple-element.22), custom_call_target="InvertDiagBlocksLowerTriangular" | custom-call | tf_op jit(solution)/shard_map/jit(_solve_triangular)/triangular_solve | solution.py:24
  545.1 61.4 %all-reduce.12.cloned.1.call-done = f32[1024,256]{0,1:T(8,128)} async-done(((f32[1024,256]{0,1:T(8,128)}), f32[1024,256]{0,1:T(8,128)}) %all-reduce.12.cloned.1.call-update) | async-done | bytes 1048592 | tf_op jit(solution)/shard_map/psum | solution.py:11
  606.8 115.7 %all-gather.5.cloned.1.call-done = f32[16384,256]{0,1:T(8,128)} async-done(((f32[1024,256]{0,1:T(8,128)}), f32[16384,256]{0,1:T(8,128)}) %all-gather.5.cloned.1.call-update) | async-done | bytes 16777232 | tf_op jit(solution)/shard_map/all_gather | solution.py:35
  722.5 20.4 %reshape.122 = f32[16,4,256,256]{2,1,0,3:T(4,128)} reshape(f32[16384,256]{0,1:T(8,128)} %all-gather.5.cloned.1.call-done) | data formatting | bytes 33554432 | tf_op jit(solution)/shard_map/reshape | solution.py:36
  742.9 19.2 %copy.19 = f32[16,4,256,256]{3,2,0,1:T(8,128)} copy(f32[16,4,256,256]{2,1,0,3:T(4,128)} %reshape.122) | data formatting | bytes 33554432 | tf_op jit(solution)/shard_map/reshape | solution.py:36
  762.1 1.8 constant_dynamic-slice_fusion.2
  764.3 12.8 %fusion = f32[1024,2048]{0,1:T(8,128)} fusion(f32[1024,2048]{0,1:T(8,128)} %copy-done, f32[2048,256]{1,0:T(8,128)S(1)} %bitcast_select_fusion.2, f32[1024,256]{0,1:T(8,128)S(1)} %copy-done.2, pred[2048]{0:T(1024)(128)(4,1)S(1)} %eq.69, pred[1024]{0:T(1024)(128)(4,1)S(1)} %eq.67, pred[2048]{0:T(1024)(128)(4,1)S(1)} %gt.57, pred[1024]{0:T(1024)(128)(4,1)S(1)} %gt.63), kind=kOutput, calls=%fused_computation.5 | convolution fusion | flops 6451101696 | bytes 19929088 | tf_op jit(solution)/shard_map/dot_general | solution.py:46
  777.1 9.1 %copy.21 = f32[1024,2048]{1,0:T(8,128)} copy(f32[1024,2048]{0,1:T(8,128)} %fusion) | data formatting | bytes 16777216 | tf_op jit(solution)/shard_map/jit(_where)/select_n | solution.py:52
  (91 shorter events, 19.1 us)
Async XLA Ops:
  6.5 93.7 %all-reduce.6.cloned.1.call-start = ((), (), s32[]{:S(2)}) async-start(), calls=%async_computation | async-start | bytes 524288 | tf_op jit(solution)/shard_map/psum | solution.py:11
  17.5 208.6 %all-reduce.8.cloned.1.call-start = ((), (), s32[]{:S(2)}) async-start(), calls=%async_computation.1 | async-start | bytes 2097152 | tf_op jit(solution)/shard_map/psum | solution.py:11
  164.6 177.8 %all-gather.3.cloned.1.call-start = ((), (), s32[]{:S(2)}) async-start(), calls=%async_computation.2 | async-start | bytes 17825792 | tf_op jit(solution)/shard_map/all_gather | solution.py:35
  226.1 254.7 %all-reduce.10.cloned.1.call-start = ((), (), s32[]{:S(2)}) async-start(), calls=%async_computation.3 | async-start | bytes 524288 | tf_op jit(solution)/shard_map/psum | solution.py:11
  382.1 2.2 copy-start.1
  395.5 3.4 copy-start
  399.7 206.9 %all-reduce.12.cloned.1.call-start = ((), (), s32[]{:S(2)}) async-start(), calls=%async_computation.4 | async-start | bytes 2097152 | tf_op jit(solution)/shard_map/psum | solution.py:11
  545.1 177.4 %all-gather.5.cloned.1.call-start = ((), (), s32[]{:S(2)}) async-start(), calls=%async_computation.5 | async-start | bytes 17825792 | tf_op jit(solution)/shard_map/all_gather | solution.py:35
  762.1 2.2 copy-start.2
Sparse Core Ops, SparseCore 0:
  17.6 82.6 all-reduce.5
  164.8 61.3 all-reduce.7
  228.5 113.8 all-gather.2
  399.8 80.9 all-reduce.9
  545.2 61.3 all-reduce.11
  608.6 113.8 all-gather.4
where the time goes:
time: 805 us; the launch traced here: 793 us
  waiting for transfers between devices  515 us (64%)
  local copies, waits for them, and re-layouts  117 us (15%)
  other arithmetic  114 us (14%)
  matrix products  29.1 us (4%)
  between operations  16.6 us (2%)
    psum x4, waiting for transfers between devices, from_root(): return lax.psum(kept, axis)  284 us
    all_gather x2, waiting for transfers between devices, panel_columns(): whole = lax.all_gather(panel, 'row', axis=0, tiled=True)  232 us
    reshape x4, local copies, waits for them, and re-layouts, panel_columns(): whole.reshape(grid_rows, tile_rows, TILE, TILE).transpose(1, 0, 2, 3)  79.3 us
    another operation x13, other arithmetic, factor_panel(): factor = jnp.linalg.cholesky(diag)  68.7 us
    another operation x5, other arithmetic, factor_panel(): solved = jax.scipy.linalg.solve_triangular(factor, column.T, lower=True).T  39.4 us
    dot_general x2, matrix products, apply_panel(): jnp.dot(left, right.T, precision=lax.Precision.HIGHEST, preferred_element...  24.1 us
  transfers between devices with their start and end apart: 6, of which 6 were waited for; matrix products, arithmetic and copies ran while one was open for 0% of the time, Pallas kernels for 0%

commit v1 on v0

v1 whole, which is shorter than its diff:
```python
import jax
import jax.numpy as jnp
from jax import lax
from jax.experimental import pallas as pl
from jax.experimental.pallas import tpu as pltpu
from jax.sharding import PartitionSpec as P

TILE = 256
BLOCK = 128
F32 = jnp.float32
BF16 = jnp.bfloat16
HIGHEST = lax.Precision.HIGHEST


def device_id(y, x, z, c):
    return ((4 * y + x) * 4 + z) * 2 + c


def pairs(moves):
    return [(device_id(*a), device_id(*b)) for a, b in moves]


R4 = range(4)
R2 = range(2)


def send(value, moves):
    return lax.ppermute(value, ("row", "col"), pairs(moves))


def split3(x):
    hi = x.astype(BF16).astype(F32)
    rest = x - hi
    mid = rest.astype(BF16).astype(F32)
    return hi, mid, rest - mid


def stacked(x, left):
    hi, mid, lo = split3(x)
    parts = [hi, hi, mid, hi, lo, mid] if left else [hi, mid, hi, lo, hi, mid]
    return jnp.concatenate(parts, axis=0).astype(BF16)


def dot_tn(a, b, precision=None):
    return lax.dot_general(
        a, b, (((0,), (0,)), ((), ())), precision=precision, preferred_element_type=F32
    )


def spread(x):
    return jnp.broadcast_to(x, (8, BLOCK))


def factor_block(rows):
    groups = BLOCK // 8
    sub = lax.broadcasted_iota(jnp.int32, (8, BLOCK), 0)
    lane = lax.broadcasted_iota(jnp.int32, (8, BLOCK), 1)
    a = list(rows)
    w = [jnp.where(lane == sub + 8 * g, 1.0, 0.0).astype(F32) for g in range(groups)]
    upper, inverse = [], []
    for g in range(groups):
        r, v = a[g], w[g]
        cols = [spread(r[:, 8 * g + i : 8 * g + i + 1]) for i in range(8)]
        pivots = None
        for i in range(8):
            p = spread(cols[i][i : i + 1, :])
            pivots = p if pivots is None else jnp.where(sub == i, p, pivots)
            if i == 7:
                break
            m = jnp.where(sub > i, cols[i] / p, 0.0)
            r = r - m * spread(r[i : i + 1, :])
            v = v - m * spread(v[i : i + 1, :])
            for j in range(i + 1, 8):
                cols[j] = cols[j] - m * spread(cols[j][i : i + 1, :])
        s = lax.rsqrt(pivots)
        s = s * (1.5 - 0.5 * pivots * s * s)
        r = jnp.where(lane >= sub + 8 * g, r * s, 0.0)
        v = v * s
        upper.append(r)
        inverse.append(v)
        if g < groups - 1:
            t = dot_tn(stacked(r, True), stacked(jnp.concatenate([r, v], axis=1), False))
            for h in range(g + 1, groups):
                a[h] = a[h] - t[8 * h : 8 * h + 8, :BLOCK]
                w[h] = w[h] - t[8 * h : 8 * h + 8, BLOCK:]
    return jnp.concatenate(upper, axis=0), jnp.concatenate(inverse, axis=0)


def factor_kernel(d00, d10, d11, v_ref, l00, l11, m):
    n, b = 2 * TILE, BLOCK
    count = n // b
    m[0:TILE, 0:TILE] = d00[...]
    m[0:TILE, TILE:n] = d10[...].T
    m[TILE:n, TILE:n] = d11[...]
    v_ref[...] = jnp.zeros((n, n), F32)
    for k in range(count):
        o = k * b
        e = o + b
        uk, vk = factor_block([m[o + 8 * g : o + 8 * g + 8, o:e] for g in range(b // 8)])
        m[o:e, o:e] = uk
        if k > 0:
            v_ref[o:e, 0:o] = jnp.dot(
                vk, v_ref[o:e, 0:o], precision=HIGHEST, preferred_element_type=F32
            )
        v_ref[o:e, o:e] = vk
        if k < count - 1:
            row = jnp.dot(vk, m[o:e, e:n], precision=HIGHEST, preferred_element_type=F32)
            m[o:e, e:n] = row
            for j in range(k + 1, count):
                s = j * b
                t = s + b
                left = row[:, s - e : t - e]
                m[s:t, s:n] = m[s:t, s:n] - dot_tn(left, row[:, s - e :], HIGHEST)
                v_ref[s:t, 0:e] = v_ref[s:t, 0:e] - dot_tn(left, v_ref[o:e, 0:e], HIGHEST)
    r = lax.broadcasted_iota(jnp.int32, (TILE, TILE), 0)
    c = lax.broadcasted_iota(jnp.int32, (TILE, TILE), 1)
    l00[...] = jnp.where(r >= c, m[0:TILE, 0:TILE].T, 0.0)
    l11[...] = jnp.where(r >= c, m[TILE:n, TILE:n].T, 0.0)


def factor(d00, d10, d11):
    n = 2 * TILE
    vmem = pl.BlockSpec(memory_space=pltpu.VMEM)
    return pl.pallas_call(
        factor_kernel,
        out_shape=[
            jax.ShapeDtypeStruct((n, n), F32),
            jax.ShapeDtypeStruct((TILE, TILE), F32),
            jax.ShapeDtypeStruct((TILE, TILE), F32),
        ],
        in_specs=[vmem] * 3,
        out_specs=[vmem] * 3,
        scratch_shapes=[pltpu.VMEM((n, n), F32)],
        compiler_params=pltpu.CompilerParams(vmem_limit_bytes=16 * 2**20),
        cost_estimate=pl.CostEstimate(
            flops=15 * 10**9, bytes_accessed=3 * 2**20, transcendentals=0
        ),
    )(d00, d10, d11)


def halves(x):
    hi = x.astype(BF16)
    return hi, (x - hi.astype(F32)).astype(BF16)


def dot3(a, b, dims):
    ah, al = a
    bh, bl = b
    d = (dims, ((), ()))
    out = lax.dot_general(ah, bh, d, preferred_element_type=F32)
    out = out + lax.dot_general(ah, bl, d, preferred_element_type=F32)
    return out + lax.dot_general(al, bh, d, preferred_element_type=F32)


NT = ((1,), (1,))
NN = ((1,), (0,))
CHUNK = 512


def update_kernel(
    place, mat, v_hbm, l00, l11, mine_a, mine_b, other_a, other_b,
    x0, x1, x2, x3, y0, y1, y2, y3, out,
    m, o, ap, dq, v, lp, lph, lpl, lqh, lql, in_sem, piece_sem, out_sem,
):
    row, col = place[0], place[1]
    y, x = row // 4, row % 4
    c = col % 2
    rows, cols = mat.shape
    chunks = cols // CHUNK
    copies = []

    def fetch(src, dst):
        copy = pltpu.make_async_copy(src, dst, piece_sem.at[len(copies)])
        copy.start()
        copies.append(copy)

    half = rows // 2
    fetch(v_hbm, v)
    for ref, which, at in ((mine_a, c, 0), (mine_b, c, half), (other_a, 1 - c, 0), (other_b, 1 - c, half)):
        fetch(ref, ap.at[which, pl.ds(at, half), :])
    for k, ref in enumerate((x0, x1, x2, x3)):
        source = lax.rem(x + 4 - k, 4)
        second = jnp.logical_or(source == 1, source == 2).astype(jnp.int32)
        start = pl.multiple_of((source // 2) * 512, 512)
        fetch(ref, dq.at[second, :, pl.ds(start, 512)])
    for k, ref in enumerate((y0, y1, y2, y3)):
        source = lax.rem(y + 4 - k, 4)
        start = pl.multiple_of(1024 + source * 256, 256)
        fetch(ref, dq.at[:, :, pl.ds(start, 256)])
    loads = []
    for j in range(chunks):
        copy = pltpu.make_async_copy(
            mat.at[:, pl.ds(j * CHUNK, CHUNK)], m.at[:, pl.ds(j * CHUNK, CHUNK)], in_sem.at[j]
        )
        copy.start()
        loads.append(copy)

    for copy in copies[:5]:
        copy.wait()
    v00 = halves(v[0:TILE, 0:TILE])
    v10 = halves(v[TILE:, 0:TILE])
    v11 = halves(v[TILE:, TILE:])
    for i in range(rows // TILE):
        at = pl.ds(i * TILE, TILE)
        a0 = halves(ap[0, at, :])
        a1 = halves(ap[1, at, :])
        first = dot3(a0, v00, NT)
        second = dot3(a0, v10, NT) + dot3(a1, v11, NT)
        lp[at, 0:TILE] = first
        lp[at, TILE:] = second
        lph[at, 0:TILE], lpl[at, 0:TILE] = halves(first)
        lph[at, TILE:], lpl[at, TILE:] = halves(second)
    for copy in copies[5:]:
        copy.wait()
    stores = []
    for j in range(chunks):
        at = pl.ds(j * CHUNK, CHUNK)
        d0 = halves(dq[0, :, at])
        d1 = halves(dq[1, :, at])
        lqh[0:TILE, :], lql[0:TILE, :] = halves(dot3(v00, d0, NN))
        lqh[TILE:, :], lql[TILE:, :] = halves(dot3(v10, d0, NN) + dot3(v11, d1, NN))
        loads[j].wait()
        for i in range(rows // TILE):
            r = pl.ds(i * TILE, TILE)
            o[r, at] = m[r, at] - dot3(
                (lph[r, :], lpl[r, :]), (lqh[...], lql[...]), NN
            )

        @pl.when(row < 2)
        def _():
            o[0:TILE, at] = jnp.zeros((TILE, CHUNK), F32)

        if j == 0:
            @pl.when(col == 0)
            def _():
                o[:, 0:TILE] = lp[:, 0:TILE]

                @pl.when(row == 0)
                def _():
                    o[0:TILE, 0:TILE] = l00[...]

            @pl.when(col == 1)
            def _():
                o[:, 0:TILE] = lp[:, TILE:]

                @pl.when(row == 0)
                def _():
                    o[0:TILE, 0:TILE] = jnp.zeros((TILE, TILE), F32)

                @pl.when(row == 1)
                def _():
                    o[0:TILE, 0:TILE] = l11[...]

        copy = pltpu.make_async_copy(o.at[:, at], out.at[:, at], out_sem.at[j])
        copy.start()
        stores.append(copy)
    for copy in stores:
        copy.wait()


def update(place, mat, v, l00, l11, mine, other, xs, ys):
    rows, cols = mat.shape
    n = 2 * TILE
    chunks = cols // CHUNK
    hbm = pl.BlockSpec(memory_space=pl.ANY)
    vmem = pl.BlockSpec(memory_space=pltpu.VMEM)
    smem = pl.BlockSpec(memory_space=pltpu.SMEM)
    return pl.pallas_call(
        update_kernel,
        out_shape=jax.ShapeDtypeStruct((rows, cols), F32),
        in_specs=[smem, hbm, hbm, vmem, vmem] + [hbm] * 12,
        out_specs=hbm,
        scratch_shapes=[
            pltpu.VMEM((rows, cols), F32),
            pltpu.VMEM((rows, cols), F32),
            pltpu.VMEM((2, rows, TILE), F32),
            pltpu.VMEM((2, TILE, cols), F32),
            pltpu.VMEM((n, n), F32),
            pltpu.VMEM((rows, n), F32),
            pltpu.VMEM((rows, n), BF16),
            pltpu.VMEM((rows, n), BF16),
            pltpu.VMEM((n, CHUNK), BF16),
            pltpu.VMEM((n, CHUNK), BF16),
            pltpu.SemaphoreType.DMA((chunks,)),
            pltpu.SemaphoreType.DMA((13,)),
            pltpu.SemaphoreType.DMA((chunks,)),
        ],
        compiler_params=pltpu.CompilerParams(vmem_limit_bytes=48 * 2**20),
        cost_estimate=pl.CostEstimate(
            flops=10 * 10**9, bytes_accessed=24 * 2**20, transcendentals=0
        ),
    )(place, mat, v, l00, l11, *mine, *other, *xs, *ys)


def along(axis, table, cores=R2, fixed=None):
    fixed = fixed or {}
    names = "yxzc"
    ranges = [fixed.get(k, R4 if k != "c" else cores) for k in names]
    moves = []
    at = names.index(axis)
    for a, b in table:
        spans = list(ranges)
        spans[at] = (a,)
        for y in spans[0]:
            for x in spans[1]:
                for z in spans[2]:
                    for c in spans[3]:
                        src = [y, x, z, c]
                        dst = list(src)
                        dst[at] = b
                        moves.append((tuple(src), tuple(dst)))
    return moves


def spread_chain(value, core, order, root):
    fixed = {k: (root[k],) for k in "yxz"}
    for axis in order:
        s = root[axis]
        near, far, opposite = (s + 1) % 4, (s + 3) % 4, (s + 2) % 4
        first = send(value, along(axis, [(s, near)], (core,), fixed))
        value = value + first
        second = send(value, along(axis, [(s, far), (near, opposite)], (core,), fixed))
        value = value + second
        fixed[axis] = R4
    return value


def swap_cores(value):
    return send(value, [((y, x, z, c), (y, x, z, 1 - c)) for y in R4 for x in R4 for z in R4 for c in R2])


def shards(matrix):
    row = lax.axis_index("row")
    col = lax.axis_index("col")
    y, x = row // 4, row % 4
    z, c = col // 2, col % 2
    tile = matrix[0:TILE, 0:TILE]

    at_first = (row == 0) & (col == 0)
    at_second = (row == 1) & (col == 1)
    t00 = spread_chain(jnp.where(at_first, tile, 0.0), 0, "xyz", {"y": 0, "x": 0, "z": 0})
    t10 = send(tile, [((0, 1, 0, 0), (0, 1, 0, 1))])
    pair = jnp.where(at_second, jnp.stack([t10, tile]), 0.0)
    pair = spread_chain(pair, 1, "zyx", {"y": 0, "x": 1, "z": 0})
    t00 = t00 + send(t00, [((a, b, d, 0), (a, b, d, 1)) for a in R4 for b in R4 for d in R4])
    pair = pair + send(pair, [((a, b, d, 1), (a, b, d, 0)) for a in R4 for b in R4 for d in R4])
    v, l00, l11 = factor(t00, pair[0], pair[1])

    strip = matrix[:, 0:TILE]
    half = strip.shape[0] // 2
    own_a, own_b = strip[:half], strip[half:]
    at_zero = z == 0
    a1 = send(own_a, along("z", [(0, 1)]))
    b1 = send(own_b, along("z", [(0, 3)]))
    a2 = send(jnp.where(at_zero, own_a, a1), along("z", [(0, 3), (1, 2)]))
    b2 = send(jnp.where(at_zero, own_b, b1), along("z", [(0, 1), (3, 2)]))
    mine_a = jnp.where(at_zero, own_a, a1 + a2)
    mine_b = jnp.where(at_zero, own_b, b1 + b2)
    other_a = swap_cores(mine_a)
    other_b = swap_cores(mine_b)

    near = matrix[0:TILE, 0:512]
    far = matrix[0:TILE, 512:1024]
    moved = send(far, along("x", [(0, 3), (1, 2)], fixed={"y": (0,)}))
    quarter = jnp.where(x < 2, near, moved)
    top = y == 0
    qa, qb = quarter[:, :256], quarter[:, 256:]
    qa1 = send(qa, along("y", [(0, 1)]))
    qb1 = send(qb, along("y", [(0, 3)]))
    qa2 = send(jnp.where(top, qa, qa1), along("y", [(0, 3), (1, 2)]))
    qb2 = send(jnp.where(top, qb, qb1), along("y", [(0, 1), (3, 2)]))
    quarter = jnp.where(top, quarter, jnp.concatenate([qa1 + qa2, qb1 + qb2], axis=1))
    xs = [quarter] + [send(quarter, along("x", [(i, (i + k) % 4) for i in R4])) for k in (1, 2, 3)]

    parts = [matrix[0:TILE, 1024 + 256 * i : 1280 + 256 * i] for i in R4]
    got = [send(parts[k], along("y", [(0, k)], fixed={"x": (0, 1)})) for k in (1, 2, 3)]
    base = jnp.where(top, parts[0], got[0] + got[1] + got[2])
    e1 = send(base, along("x", [(0, 1), (1, 0)]))
    e2 = send(base, along("x", [(0, 3), (1, 2)]))
    e3 = send(e2, along("x", [(3, 2), (2, 3)]))
    kept = jnp.where(x < 2, base, e2)
    came = e1 + e3
    first_mine = (x == 0) | (x == 3)
    both = jnp.stack([jnp.where(first_mine, kept, came), jnp.where(first_mine, came, kept)])
    ys = [both] + [send(both, along("y", [(i, (i + k) % 4) for i in R4])) for k in (1, 2, 3)]

    place = jnp.stack([row, col]).astype(jnp.int32)
    return update(place, matrix, v, l00, l11, (mine_a, mine_b), (other_a, other_b), xs, ys)


def solution(mesh):
    return jax.shard_map(
        shards,
        mesh=mesh,
        in_specs=(P("row", "col"),),
        out_specs=P("row", "col"),
        check_vma=False,
    )
```

time: 805 us -> 181 us (0.22)
  the two profiles are of different devices: /device:TPU:81 before, /device:TPU:1 now
where the time goes in v1:
time: 181 us; the launch traced here: 180 us
  starting transfers between devices  90.6 us (50%)
  Pallas kernels  42.2 us (23%)
  waiting for transfers between devices  28.8 us (16%)
  other arithmetic  11.9 us (7%)
  local copies, waits for them, and re-layouts  6.01 us (3%)
    ppermute x38, starting transfers between devices, send(): return lax.ppermute(value, ('row', 'col'), pairs(moves))  90.6 us
    ppermute x38, waiting for transfers between devices, send(): return lax.ppermute(value, ('row', 'col'), pairs(moves))  28.8 us
    pallas_call x1, Pallas kernels, factor(): pl.pallas_call(factor_kernel, out_shape=[jax.ShapeDtypeStruct((n, n), F32...  25.5 us
    pallas_call x1, Pallas kernels, update(): pl.pallas_call(update_kernel, out_shape=jax.ShapeDtypeStruct((rows, cols)...  16.7 us
  transfers between devices with their start and end apart: 38, of which 6 were waited for; matrix products, arithmetic and copies ran while one was open for 8% of the time, Pallas kernels for 14%

profile of v1, /device:TPU:1, one launch (start us, length us, event | category | flops | bytes accessed | tf_op | source)
XLA Modules:
  0.0 180.3 jit_solution(16957787567913619751)
XLA Ops:
  1.2 5.7 %collective-permute-start.30 = (f32[256,256]{1,0:T(8,128)S(1)}, f32[256,256]{1,0:T(8,128)S(1)}, u32[]{:S(2)}, u32[]{:S(2)}) collective-permute-start(f32[256,256]{1,0:T(8,128)S(1)} %get-tuple-element.15), channel_id=1, source_target_pairs={{0,64},{1,65},{2,66},{3,67},{4,68},{5,69},{6,70},{7,71},{8,72},{9,... | collective-permute-start | bytes 786440 | tf_op jit(solution)/shard_map/ppermute | solution.py:28
  6.8 1.3 collective-permute-start.29
  8.2 1.3 collective-permute-start.31
  9.5 2.3 %collective-permute-done.30 = f32[256,256]{1,0:T(8,128)S(1)} collective-permute-done((f32[256,256]{1,0:T(8,128)S(1)}, f32[256,256]{1,0:T(8,128)S(1)}, u32[]{:S(2)}, u32[]{:S(2)}) %collective-permute-start.30) | collective-permute-done | bytes 262176 | tf_op jit(solution)/shard_map/ppermute | solution.py:28
  11.8 5.6 %collective-permute-done.29 = f32[256,256]{1,0:T(8,128)S(1)} collective-permute-done((f32[256,256]{1,0:T(8,128)S(1)}, f32[256,256]{1,0:T(8,128)S(1)}, u32[]{:S(2)}, u32[]{:S(2)}) %collective-permute-start.29) | collective-permute-done | bytes 262176 | tf_op jit(solution)/shard_map/ppermute | solution.py:28
  20.8 1.9 %slice.46 = f32[512,256]{1,0:T(8,128)} slice(f32[1024,2048]{1,0:T(8,128)} %mat.1), slice={[512:1024], [0:256]} | slice | bytes 1048576 | tf_op jit(solution)/shard_map/slice | solution.py:351
  22.7 5.7 %collective-permute-start.17 = (f32[512,256]{1,0:T(8,128)}, f32[512,256]{1,0:T(8,128)S(1)}, u32[]{:S(2)}, u32[]{:S(2)}) collective-permute-start(f32[512,256]{1,0:T(8,128)} %slice.46), channel_id=1, source_target_pairs={{0,6},{1,7},{8,14},{9,15},{16,22},{17,23},{24,30},{25,31},{32,38},... | collective-permute-start | bytes 1572872 | tf_op jit(solution)/shard_map/ppermute | solution.py:28
  28.3 1.9 %slice.48 = f32[256,512]{1,0:T(8,128)} slice(f32[1024,2048]{1,0:T(8,128)} %mat.1), slice={[0:256], [512:1024]} | slice | bytes 1048576 | tf_op jit(solution)/shard_map/slice | solution.py:363
  30.2 2.1 %collective-permute-start.21 = (f32[256,512]{1,0:T(8,128)}, f32[256,512]{1,0:T(8,128)}, u32[]{:S(2)}, u32[]{:S(2)}) collective-permute-start(f32[256,512]{1,0:T(8,128)} %slice.48), channel_id=1, source_target_pairs={{0,24},{1,25},{2,26},{3,27},{4,28},{5,29},{6,30},{7,31},{8,16},{9,... | collective-permute-start | bytes 1572872 | tf_op jit(solution)/shard_map/ppermute | solution.py:28
  33.9 4.4 %collective-permute-done.17 = f32[512,256]{1,0:T(8,128)S(1)} collective-permute-done((f32[512,256]{1,0:T(8,128)}, f32[512,256]{1,0:T(8,128)S(1)}, u32[]{:S(2)}, u32[]{:S(2)}) %collective-permute-start.17) | collective-permute-done | bytes 524320 | tf_op jit(solution)/shard_map/ppermute | solution.py:28
  39.4 2.1 %collective-permute-start.18 = (f32[512,256]{1,0:T(8,128)S(1)}, f32[512,256]{1,0:T(8,128)}, u32[]{:S(2)}, u32[]{:S(2)}) collective-permute-start(f32[512,256]{1,0:T(8,128)S(1)} %broadcast_select_fusion), channel_id=1, source_target_pairs={{0,2},{1,3},{8,10},{9,11},{16,18},{17,19},{24,26},{25,27},{32,34},... | collective-permute-start | bytes 1572872 | tf_op jit(solution)/shard_map/ppermute | solution.py:28
  41.5 2.0 %collective-permute-start.32 = (f32[256,256]{1,0:T(8,128)S(1)}, f32[256,256]{1,0:T(8,128)}, u32[]{:S(2)}, u32[]{:S(2)}) collective-permute-start(f32[256,256]{1,0:T(8,128)S(1)} %get-tuple-element.11), channel_id=1, source_target_pairs={{0,24},{1,25},{2,26},{3,27},{4,28},{5,29},{6,30},{7,31},{32,56},{3... | collective-permute-start | bytes 786440 | tf_op jit(solution)/shard_map/ppermute | solution.py:28
  46.2 4.1 %collective-permute-start.22 = (f32[256,256]{1,0:T(8,128)S(1)}, f32[256,256]{1,0:T(8,128)S(1)}, u32[]{:S(2)}, u32[]{:S(2)}) collective-permute-start(f32[256,256]{1,0:T(8,128)S(1)} %slice.57), channel_id=1, source_target_pairs={{0,32},{1,33},{2,34},{3,35},{4,36},{5,37},{6,38},{7,39},{8,40},{9,... | collective-permute-start | bytes 786440 | tf_op jit(solution)/shard_map/ppermute | solution.py:28
  51.0 2.3 %add_select_fusion = (f32[512,256]{1,0:T(8,128)S(1)}, f32[512,256]{1,0:T(8,128)}) fusion(f32[512,256]{1,0:T(8,128)S(1)} %collective-permute-done.17, f32[512,256]{1,0:T(8,128)} %collective-permute-done.18, pred[]{:T(512)S(6)} %eq.30, f32[1024,2048]{1,0:T(8,128)} %mat.1), kind=kLoop, calls=%fused_computation.4 | loop fusion | flops 262144 | bytes 3145729 | tf_op jit(solution)/shard_map/jit(_where)/select_n | solution.py:358
  53.3 2.9 %collective-permute-start.15 = (f32[512,256]{1,0:T(8,128)}, f32[512,256]{1,0:T(8,128)S(1)}, u32[]{:S(2)}, u32[]{:S(2)}) collective-permute-start(f32[512,256]{1,0:T(8,128)} %get-tuple-element.19), channel_id=1, source_target_pairs={{0,2},{1,3},{8,10},{9,11},{16,18},{17,19},{24,26},{25,27},{32,34},... | collective-permute-start | bytes 1572872 | tf_op jit(solution)/shard_map/ppermute | solution.py:28
  57.0 1.5 collective-permute-start.12
  59.3 2.3 %collective-permute-start.24 = (f32[256,256]{1,0:T(8,128)}, f32[256,256]{1,0:T(8,128)S(1)}, u32[]{:S(2)}, u32[]{:S(2)}) collective-permute-start(f32[256,256]{1,0:T(8,128)} %get-tuple-element.23), channel_id=1, source_target_pairs={{0,96},{1,97},{2,98},{3,99},{4,100},{5,101},{6,102},{7,103},{8,104... | collective-permute-start | bytes 786440 | tf_op jit(solution)/shard_map/ppermute | solution.py:28
  61.7 1.4 collective-permute-start.4
  63.1 10.9 %collective-permute-start.33 = (f32[256,256]{1,0:T(8,128)S(1)}, f32[256,256]{1,0:T(8,128)S(1)}, u32[]{:S(2)}, u32[]{:S(2)}) collective-permute-start(f32[256,256]{1,0:T(8,128)S(1)} %get-tuple-element.11), channel_id=1, source_target_pairs={{0,8},{1,9},{2,10},{3,11},{4,12},{5,13},{6,14},{7,15},{32,40},{33,... | collective-permute-start | bytes 786440 | tf_op jit(solution)/shard_map/ppermute | solution.py:28
  74.7 1.3 collective-permute-start.23
  81.3 1.3 collective-permute-start.25
  82.7 4.9 %collective-permute-start.16 = (f32[512,256]{1,0:T(8,128)S(1)}, f32[512,256]{1,0:T(8,128)S(1)}, u32[]{:S(2)}, u32[]{:S(2)}) collective-permute-start(f32[512,256]{1,0:T(8,128)S(1)} %broadcast_select_fusion.1), channel_id=1, source_target_pairs={{0,6},{1,7},{8,14},{9,15},{16,22},{17,23},{24,30},{25,31},{32,38},... | collective-permute-start | bytes 1572872 | tf_op jit(solution)/shard_map/ppermute | solution.py:28
  87.6 1.3 collective-permute-start.6
  89.1 11.8 %collective-permute-start.37 = (f32[2,256,256]{2,1,0:T(8,128)S(1)}, f32[2,256,256]{2,1,0:T(8,128)S(1)}, u32[]{:S(2)}, u32[]{:S(2)}) collective-permute-start(f32[2,256,256]{2,1,0:T(8,128)S(1)} %pad_maximum_fusion.y0), channel_id=1, source_target_pairs={{0,96},{1,97},{2,98},{3,99},{4,100},{5,101},{6,102},{7,103},{8,104... | collective-permute-start | bytes 1572872 | tf_op jit(solution)/shard_map/ppermute | solution.py:28
  100.9 9.0 %collective-permute-start.36 = (f32[2,256,256]{2,1,0:T(8,128)S(1)}, f32[2,256,256]{2,1,0:T(8,128)S(1)}, u32[]{:S(2)}, u32[]{:S(2)}) collective-permute-start(f32[2,256,256]{2,1,0:T(8,128)S(1)} %pad_maximum_fusion.y0), channel_id=1, source_target_pairs={{0,64},{1,65},{2,66},{3,67},{4,68},{5,69},{6,70},{7,71},{8,72},{9,... | collective-permute-start | bytes 1572872 | tf_op jit(solution)/shard_map/ppermute | solution.py:28
  110.0 1.5 collective-permute-start.35
  111.5 2.6 %collective-permute-start.14 = (f32[2,256,256]{2,1,0:T(8,128)S(1)}, f32[2,256,256]{2,1,0:T(8,128)S(1)}, u32[]{:S(2)}, u32[]{:S(2)}) collective-permute-start(f32[2,256,256]{2,1,0:T(8,128)S(1)} %add.81), channel_id=1, source_target_pairs={{1,0},{3,2},{5,4},{7,6},{9,8},{11,10},{13,12},{15,14},{17,16},{19,... | collective-permute-start | bytes 1572872 | tf_op jit(solution)/shard_map/ppermute | solution.py:28
  115.6 2.4 %collective-permute-start.28 = (f32[256,512]{1,0:T(8,128)S(1)}, f32[256,512]{1,0:T(8,128)S(1)}, u32[]{:S(2)}, u32[]{:S(2)}) collective-permute-start(f32[256,512]{1,0:T(8,128)S(1)} %maximum_select_fusion.1.x0), channel_id=1, source_target_pairs={{0,24},{1,25},{2,26},{3,27},{4,28},{5,29},{6,30},{7,31},{32,56},{3... | collective-permute-start | bytes 1572872 | tf_op jit(solution)/shard_map/ppermute | solution.py:28
  118.8 6.1 %collective-permute-done.36.y2 = f32[2,256,256]{2,1,0:T(8,128)S(1)} collective-permute-done((f32[2,256,256]{2,1,0:T(8,128)S(1)}, f32[2,256,256]{2,1,0:T(8,128)S(1)}, u32[]{:S(2)}, u32[]{:S(2)}) %collective-permute-start.36) | collective-permute-done | bytes 524320 | tf_op jit(solution)/shard_map/ppermute | solution.py:28
  126.0 10.2 %collective-permute-done.35.y1 = f32[2,256,256]{2,1,0:T(8,128)S(1)} collective-permute-done((f32[2,256,256]{2,1,0:T(8,128)S(1)}, f32[2,256,256]{2,1,0:T(8,128)S(1)}, u32[]{:S(2)}, u32[]{:S(2)}) %collective-permute-start.35) | collective-permute-done | bytes 524320 | tf_op jit(solution)/shard_map/ppermute | solution.py:28
  136.8 25.5 %shard_map.17 = (f32[512,512]{1,0:T(8,128)S(1)}, f32[256,256]{1,0:T(8,128)S(1)}, f32[256,256]{1,0:T(8,128)S(1)}) custom-call(f32[256,256]{1,0:T(8,128)S(1)} %add.75.d00, f32[256,256]{1,0:T(8,128)S(1)} %get-tuple-element.25.d10, f32[256,256]{1,0:T(8,128)S(1)} %get-tuple-element.24.d11), custom_call_target="tpu_custom_call" | custom-call | flops 15000000512 | bytes 3145728 | tf_op jit(solution)/shard_map/pallas_call | solution.py:124
  163.4 16.7 %shard_map.18 = f32[1024,2048]{1,0:T(8,128)} custom-call(s32[2]{0:T(128)S(1)} %pad_add_fusion.place, f32[1024,2048]{1,0:T(8,128)} %mat.1, f32[512,512]{1,0:T(8,128)} %copy-done, f32[256,256]{1,0:T(8,128)S(1)} %get-tuple-element.9.l00, f32[256,256]{1,0:T(8,128)S(1)} %get-tuple-element.10.l11, f32[512,256]{1,0:T(8,128)S(1)} %add_select_fusion.1.mine_a, ...), custom_call_target="tpu_custom_call" | custom-call | flops 10000000000 | bytes 25165824 | tf_op jit(solution)/shard_map/pallas_call | solution.py:268
  (86 shorter events, 23.3 us)
Async XLA Ops:
  1.2 10.6 %collective-permute-start.30 = (f32[256,256]{1,0:T(8,128)S(1)}, f32[256,256]{1,0:T(8,128)S(1)}, u32[]{:S(2)}, u32[]{:S(2)}) collective-permute-start(f32[256,256]{1,0:T(8,128)S(1)} %get-tuple-element.15), channel_id=1, source_target_pairs={{0,64},{1,65},{2,66},{3,67},{4,68},{5,69},{6,70},{7,71},{8,72},{9,... | collective-permute-start | bytes 786440 | tf_op jit(solution)/shard_map/ppermute | solution.py:28
  6.8 10.6 %collective-permute-start.29 = (f32[256,256]{1,0:T(8,128)S(1)}, f32[256,256]{1,0:T(8,128)S(1)}, u32[]{:S(2)}, u32[]{:S(2)}) collective-permute-start(f32[256,256]{1,0:T(8,128)S(1)} %get-tuple-element.16), channel_id=1, source_target_pairs={{0,32},{1,33},{2,34},{3,35},{4,36},{5,37},{6,38},{7,39},{8,40},{9,... | collective-permute-start | bytes 786440 | tf_op jit(solution)/shard_map/ppermute | solution.py:28
  8.2 9.2 %collective-permute-start.31 = (f32[256,256]{1,0:T(8,128)S(1)}, f32[256,256]{1,0:T(8,128)S(1)}, u32[]{:S(2)}, u32[]{:S(2)}) collective-permute-start(f32[256,256]{1,0:T(8,128)S(1)} %get-tuple-element.17), channel_id=1, source_target_pairs={{0,96},{1,97},{2,98},{3,99},{4,100},{5,101},{6,102},{7,103},{8,104... | collective-permute-start | bytes 786440 | tf_op jit(solution)/shard_map/ppermute | solution.py:28
  20.1 12.3 %collective-permute-start.9 = (f32[2,256,256]{2,1,0:T(8,128)S(1)}, f32[2,256,256]{2,1,0:T(8,128)S(1)}, u32[]{:S(2)}, u32[]{:S(2)}) collective-permute-start(f32[2,256,256]{2,1,0:T(8,128)S(1)} %fusion.1), channel_id=1, source_target_pairs={{9,15},{11,13}} | collective-permute-start | bytes 1572872 | tf_op jit(solution)/shard_map/ppermute | solution.py:28
  22.7 15.6 %collective-permute-start.17 = (f32[512,256]{1,0:T(8,128)}, f32[512,256]{1,0:T(8,128)S(1)}, u32[]{:S(2)}, u32[]{:S(2)}) collective-permute-start(f32[512,256]{1,0:T(8,128)} %slice.46), channel_id=1, source_target_pairs={{0,6},{1,7},{8,14},{9,15},{16,22},{17,23},{24,30},{25,31},{32,38},... | collective-permute-start | bytes 1572872 | tf_op jit(solution)/shard_map/ppermute | solution.py:28
  30.2 14.7 %collective-permute-start.21 = (f32[256,512]{1,0:T(8,128)}, f32[256,512]{1,0:T(8,128)}, u32[]{:S(2)}, u32[]{:S(2)}) collective-permute-start(f32[256,512]{1,0:T(8,128)} %slice.48), channel_id=1, source_target_pairs={{0,24},{1,25},{2,26},{3,27},{4,28},{5,29},{6,30},{7,31},{8,16},{9,... | collective-permute-start | bytes 1572872 | tf_op jit(solution)/shard_map/ppermute | solution.py:28
  32.5 11.7 %collective-permute-start.10 = (f32[2,256,256]{2,1,0:T(8,128)S(1)}, f32[2,256,256]{2,1,0:T(8,128)S(1)}, u32[]{:S(2)}, u32[]{:S(2)}) collective-permute-start(f32[2,256,256]{2,1,0:T(8,128)S(1)} %fusion.2), channel_id=1, source_target_pairs={{9,41},{11,43},{13,45},{15,47}} | collective-permute-start | bytes 1572872 | tf_op jit(solution)/shard_map/ppermute | solution.py:28
  33.2 10.3 %collective-permute-start = (f32[256,256]{1,0:T(8,128)S(1)}, f32[256,256]{1,0:T(8,128)S(1)}, u32[]{:S(2)}, u32[]{:S(2)}) collective-permute-start(f32[256,256]{1,0:T(8,128)S(1)} %get-tuple-element.12), channel_id=1, source_target_pairs={{0,8}} | collective-permute-start | bytes 786440 | tf_op jit(solution)/shard_map/ppermute | solution.py:28
  39.4 11.6 %collective-permute-start.18 = (f32[512,256]{1,0:T(8,128)S(1)}, f32[512,256]{1,0:T(8,128)}, u32[]{:S(2)}, u32[]{:S(2)}) collective-permute-start(f32[512,256]{1,0:T(8,128)S(1)} %broadcast_select_fusion), channel_id=1, source_target_pairs={{0,2},{1,3},{8,10},{9,11},{16,18},{17,19},{24,26},{25,27},{32,34},... | collective-permute-start | bytes 1572872 | tf_op jit(solution)/shard_map/ppermute | solution.py:28
  41.5 21.6 %collective-permute-start.32 = (f32[256,256]{1,0:T(8,128)S(1)}, f32[256,256]{1,0:T(8,128)}, u32[]{:S(2)}, u32[]{:S(2)}) collective-permute-start(f32[256,256]{1,0:T(8,128)S(1)} %get-tuple-element.11), channel_id=1, source_target_pairs={{0,24},{1,25},{2,26},{3,27},{4,28},{5,29},{6,30},{7,31},{32,56},{3... | collective-permute-start | bytes 786440 | tf_op jit(solution)/shard_map/ppermute | solution.py:28
  43.5 6.8 %collective-permute-start.1 = (f32[256,256]{1,0:T(8,128)S(1)}, f32[256,256]{1,0:T(8,128)S(1)}, u32[]{:S(2)}, u32[]{:S(2)}) collective-permute-start(f32[256,256]{1,0:T(8,128)S(1)} %add.69), channel_id=1, source_target_pairs={{0,24},{8,16}} | collective-permute-start | bytes 786440 | tf_op jit(solution)/shard_map/ppermute | solution.py:28
  44.3 12.7 %collective-permute-start.11 = (f32[2,256,256]{2,1,0:T(8,128)S(1)}, f32[2,256,256]{2,1,0:T(8,128)S(1)}, u32[]{:S(2)}, u32[]{:S(2)}) collective-permute-start(f32[2,256,256]{2,1,0:T(8,128)S(1)} %add.78), channel_id=1, source_target_pairs={{9,105},{11,107},{13,109},{15,111},{41,73},{43,75},{45,77},{47,79}} | collective-permute-start | bytes 1572872 | tf_op jit(solution)/shard_map/ppermute | solution.py:28
  46.2 12.4 %collective-permute-start.22 = (f32[256,256]{1,0:T(8,128)S(1)}, f32[256,256]{1,0:T(8,128)S(1)}, u32[]{:S(2)}, u32[]{:S(2)}) collective-permute-start(f32[256,256]{1,0:T(8,128)S(1)} %slice.57), channel_id=1, source_target_pairs={{0,32},{1,33},{2,34},{3,35},{4,36},{5,37},{6,38},{7,39},{8,40},{9,... | collective-permute-start | bytes 786440 | tf_op jit(solution)/shard_map/ppermute | solution.py:28
  53.3 25.5 %collective-permute-start.15 = (f32[512,256]{1,0:T(8,128)}, f32[512,256]{1,0:T(8,128)S(1)}, u32[]{:S(2)}, u32[]{:S(2)}) collective-permute-start(f32[512,256]{1,0:T(8,128)} %get-tuple-element.19), channel_id=1, source_target_pairs={{0,2},{1,3},{8,10},{9,11},{16,18},{17,19},{24,26},{25,27},{32,34},... | collective-permute-start | bytes 1572872 | tf_op jit(solution)/shard_map/ppermute | solution.py:28
  57.0 20.0 %collective-permute-start.12 = (f32[2,256,256]{2,1,0:T(8,128)S(1)}, f32[2,256,256]{2,1,0:T(8,128)}, u32[]{:S(2)}, u32[]{:S(2)}) collective-permute-start(f32[2,256,256]{2,1,0:T(8,128)S(1)} %add.79), channel_id=1, source_target_pairs={{9,17},{11,19},{13,21},{15,23},{41,49},{43,51},{45,53},{47,55},{73... | collective-permute-start | bytes 1572872 | tf_op jit(solution)/shard_map/ppermute | solution.py:28
  59.3 14.7 %collective-permute-start.24 = (f32[256,256]{1,0:T(8,128)}, f32[256,256]{1,0:T(8,128)S(1)}, u32[]{:S(2)}, u32[]{:S(2)}) collective-permute-start(f32[256,256]{1,0:T(8,128)} %get-tuple-element.23), channel_id=1, source_target_pairs={{0,96},{1,97},{2,98},{3,99},{4,100},{5,101},{6,102},{7,103},{8,104... | collective-permute-start | bytes 786440 | tf_op jit(solution)/shard_map/ppermute | solution.py:28
  61.7 13.1 %collective-permute-start.4 = (f32[256,256]{1,0:T(8,128)S(1)}, f32[256,256]{1,0:T(8,128)}, u32[]{:S(2)}, u32[]{:S(2)}) collective-permute-start(f32[256,256]{1,0:T(8,128)S(1)} %add.72), channel_id=1, source_target_pairs={{0,2},{8,10},{16,18},{24,26},{32,34},{40,42},{48,50},{56,58},{64,6... | collective-permute-start | bytes 786440 | tf_op jit(solution)/shard_map/ppermute | solution.py:28
  63.1 19.5 %collective-permute-start.33 = (f32[256,256]{1,0:T(8,128)S(1)}, f32[256,256]{1,0:T(8,128)S(1)}, u32[]{:S(2)}, u32[]{:S(2)}) collective-permute-start(f32[256,256]{1,0:T(8,128)S(1)} %get-tuple-element.11), channel_id=1, source_target_pairs={{0,8},{1,9},{2,10},{3,11},{4,12},{5,13},{6,14},{7,15},{32,40},{33,... | collective-permute-start | bytes 786440 | tf_op jit(solution)/shard_map/ppermute | solution.py:28
  74.0 13.6 %collective-permute-start.34 = (f32[256,256]{1,0:T(8,128)}, f32[256,256]{1,0:T(8,128)S(1)}, u32[]{:S(2)}, u32[]{:S(2)}) collective-permute-start(f32[256,256]{1,0:T(8,128)} %collective-permute-done.32), channel_id=1, source_target_pairs={{24,16},{25,17},{26,18},{27,19},{28,20},{29,21},{30,22},{31,23},{5... | collective-permute-start | bytes 786440 | tf_op jit(solution)/shard_map/ppermute | solution.py:28
  74.7 14.3 %collective-permute-start.23 = (f32[256,256]{1,0:T(8,128)S(1)}, f32[256,256]{1,0:T(8,128)S(1)}, u32[]{:S(2)}, u32[]{:S(2)}) collective-permute-start(f32[256,256]{1,0:T(8,128)S(1)} %get-tuple-element.22), channel_id=1, source_target_pairs={{0,96},{1,97},{2,98},{3,99},{4,100},{5,101},{6,102},{7,103},{8,104... | collective-permute-start | bytes 786440 | tf_op jit(solution)/shard_map/ppermute | solution.py:28
  78.9 31.1 %collective-permute-start.13 = (f32[2,256,256]{2,1,0:T(8,128)S(1)}, f32[2,256,256]{2,1,0:T(8,128)S(1)}, u32[]{:S(2)}, u32[]{:S(2)}) collective-permute-start(f32[2,256,256]{2,1,0:T(8,128)S(1)} %add.80), channel_id=1, source_target_pairs={{9,1},{11,3},{13,5},{15,7},{41,33},{43,35},{45,37},{47,39},{73,65}... | collective-permute-start | bytes 1572872 | tf_op jit(solution)/shard_map/ppermute | solution.py:28
  81.3 19.6 %collective-permute-start.25 = (f32[256,256]{1,0:T(8,128)S(1)}, f32[256,256]{1,0:T(8,128)S(1)}, u32[]{:S(2)}, u32[]{:S(2)}) collective-permute-start(f32[256,256]{1,0:T(8,128)S(1)} %broadcast_select_fusion.4), channel_id=1, source_target_pairs={{0,32},{1,33},{2,34},{3,35},{4,36},{5,37},{6,38},{7,39},{8,40},{9,... | collective-permute-start | bytes 786440 | tf_op jit(solution)/shard_map/ppermute | solution.py:28
  82.7 31.6 %collective-permute-start.16 = (f32[512,256]{1,0:T(8,128)S(1)}, f32[512,256]{1,0:T(8,128)S(1)}, u32[]{:S(2)}, u32[]{:S(2)}) collective-permute-start(f32[512,256]{1,0:T(8,128)S(1)} %broadcast_select_fusion.1), channel_id=1, source_target_pairs={{0,6},{1,7},{8,14},{9,15},{16,22},{17,23},{24,30},{25,31},{32,38},... | collective-permute-start | bytes 1572872 | tf_op jit(solution)/shard_map/ppermute | solution.py:28
  87.6 23.9 %collective-permute-start.6 = (f32[256,256]{1,0:T(8,128)S(1)}, f32[256,256]{1,0:T(8,128)S(1)}, u32[]{:S(2)}, u32[]{:S(2)}) collective-permute-start(f32[256,256]{1,0:T(8,128)S(1)} %add.74), channel_id=1, source_target_pairs={{0,1},{2,3},{4,5},{6,7},{8,9},{10,11},{12,13},{14,15},{16,17},{18,... | collective-permute-start | bytes 786440 | tf_op jit(solution)/shard_map/ppermute | solution.py:28
  89.1 29.0 %collective-permute-start.37 = (f32[2,256,256]{2,1,0:T(8,128)S(1)}, f32[2,256,256]{2,1,0:T(8,128)S(1)}, u32[]{:S(2)}, u32[]{:S(2)}) collective-permute-start(f32[2,256,256]{2,1,0:T(8,128)S(1)} %pad_maximum_fusion.y0), channel_id=1, source_target_pairs={{0,96},{1,97},{2,98},{3,99},{4,100},{5,101},{6,102},{7,103},{8,104... | collective-permute-start | bytes 1572872 | tf_op jit(solution)/shard_map/ppermute | solution.py:28
  100.9 23.9 %collective-permute-start.36 = (f32[2,256,256]{2,1,0:T(8,128)S(1)}, f32[2,256,256]{2,1,0:T(8,128)S(1)}, u32[]{:S(2)}, u32[]{:S(2)}) collective-permute-start(f32[2,256,256]{2,1,0:T(8,128)S(1)} %pad_maximum_fusion.y0), channel_id=1, source_target_pairs={{0,64},{1,65},{2,66},{3,67},{4,68},{5,69},{6,70},{7,71},{8,72},{9,... | collective-permute-start | bytes 1572872 | tf_op jit(solution)/shard_map/ppermute | solution.py:28
  110.0 26.3 %collective-permute-start.35 = (f32[2,256,256]{2,1,0:T(8,128)S(1)}, f32[2,256,256]{2,1,0:T(8,128)S(1)}, u32[]{:S(2)}, u32[]{:S(2)}) collective-permute-start(f32[2,256,256]{2,1,0:T(8,128)S(1)} %pad_maximum_fusion.y0), channel_id=1, source_target_pairs={{0,32},{1,33},{2,34},{3,35},{4,36},{5,37},{6,38},{7,39},{8,40},{9,... | collective-permute-start | bytes 1572872 | tf_op jit(solution)/shard_map/ppermute | solution.py:28
  114.2 49.2 %collective-permute-start.20 = (f32[512,256]{1,0:T(8,128)S(1)}, f32[512,256]{1,0:T(8,128)S(1)}, u32[]{:S(2)}, u32[]{:S(2)}) collective-permute-start(f32[512,256]{1,0:T(8,128)S(1)} %get-tuple-element.18.mine_b), channel_id=1, source_target_pairs={{0,1},{1,0},{2,3},{3,2},{4,5},{5,4},{6,7},{7,6},{8,9},{9,8},{10,11... | collective-permute-start | bytes 1572872 | tf_op jit(solution)/shard_map/ppermute | solution.py:28
  115.6 47.8 %collective-permute-start.28 = (f32[256,512]{1,0:T(8,128)S(1)}, f32[256,512]{1,0:T(8,128)S(1)}, u32[]{:S(2)}, u32[]{:S(2)}) collective-permute-start(f32[256,512]{1,0:T(8,128)S(1)} %maximum_select_fusion.1.x0), channel_id=1, source_target_pairs={{0,24},{1,25},{2,26},{3,27},{4,28},{5,29},{6,30},{7,31},{32,56},{3... | collective-permute-start | bytes 1572872 | tf_op jit(solution)/shard_map/ppermute | solution.py:28
  118.1 45.3 %collective-permute-start.27 = (f32[256,512]{1,0:T(8,128)S(1)}, f32[256,512]{1,0:T(8,128)S(1)}, u32[]{:S(2)}, u32[]{:S(2)}) collective-permute-start(f32[256,512]{1,0:T(8,128)S(1)} %maximum_select_fusion.1.x0), channel_id=1, source_target_pairs={{0,16},{1,17},{2,18},{3,19},{4,20},{5,21},{6,22},{7,23},{32,48},{3... | collective-permute-start | bytes 1572872 | tf_op jit(solution)/shard_map/ppermute | solution.py:28
  124.9 38.5 %collective-permute-start.26 = (f32[256,512]{1,0:T(8,128)S(1)}, f32[256,512]{1,0:T(8,128)S(1)}, u32[]{:S(2)}, u32[]{:S(2)}) collective-permute-start(f32[256,512]{1,0:T(8,128)S(1)} %maximum_select_fusion.1.x0), channel_id=1, source_target_pairs={{0,8},{1,9},{2,10},{3,11},{4,12},{5,13},{6,14},{7,15},{32,40},{33,... | collective-permute-start | bytes 1572872 | tf_op jit(solution)/shard_map/ppermute | solution.py:28
  136.2 27.2 %collective-permute-start.19 = (f32[512,256]{1,0:T(8,128)S(1)}, f32[512,256]{1,0:T(8,128)S(1)}, u32[]{:S(2)}, u32[]{:S(2)}) collective-permute-start(f32[512,256]{1,0:T(8,128)S(1)} %add_select_fusion.1.mine_a), channel_id=1, source_target_pairs={{0,1},{1,0},{2,3},{3,2},{4,5},{5,4},{6,7},{7,6},{8,9},{9,8},{10,11... | collective-permute-start | bytes 1572872 | tf_op jit(solution)/shard_map/ppermute | solution.py:28
  (9 other events, 103.7 us)

commit v2 on v1

v2 whole, which is shorter than its diff:
```python
import jax
import jax.numpy as jnp
from jax import lax
from jax.experimental import pallas as pl
from jax.experimental.pallas import tpu as pltpu
from jax.sharding import PartitionSpec as P

TILE = 256
BLOCK = 128
F32 = jnp.float32
BF16 = jnp.bfloat16
HIGHEST = lax.Precision.HIGHEST


def device_id(y, x, z, c):
    return ((4 * y + x) * 4 + z) * 2 + c


def pairs(moves):
    return [(device_id(*a), device_id(*b)) for a, b in moves]


R4 = range(4)
R2 = range(2)


def send(value, moves):
    return lax.ppermute(value, ("row", "col"), pairs(moves))


def split3(x):
    hi = x.astype(BF16).astype(F32)
    rest = x - hi
    mid = rest.astype(BF16).astype(F32)
    return hi, mid, rest - mid


def stacked(x, left):
    hi, mid, lo = split3(x)
    parts = [hi, hi, mid, hi, lo, mid] if left else [hi, mid, hi, lo, hi, mid]
    return jnp.concatenate(parts, axis=0).astype(BF16)


def dot_tn(a, b, precision=None):
    return lax.dot_general(
        a, b, (((0,), (0,)), ((), ())), precision=precision, preferred_element_type=F32
    )


def spread(x):
    return jnp.broadcast_to(x, (8, BLOCK))


def factor_block(rows):
    groups = BLOCK // 8
    sub = lax.broadcasted_iota(jnp.int32, (8, BLOCK), 0)
    lane = lax.broadcasted_iota(jnp.int32, (8, BLOCK), 1)
    a = list(rows)
    w = [jnp.where(lane == sub + 8 * g, 1.0, 0.0).astype(F32) for g in range(groups)]
    upper, inverse = [], []
    for g in range(groups):
        r, v = a[g], w[g]
        cols = [spread(r[:, 8 * g + i : 8 * g + i + 1]) for i in range(8)]
        pivots = None
        for i in range(8):
            p = spread(cols[i][i : i + 1, :])
            pivots = p if pivots is None else jnp.where(sub == i, p, pivots)
            if i == 7:
                break
            m = jnp.where(sub > i, cols[i] / p, 0.0)
            r = r - m * spread(r[i : i + 1, :])
            v = v - m * spread(v[i : i + 1, :])
            for j in range(i + 1, 8):
                cols[j] = cols[j] - m * spread(cols[j][i : i + 1, :])
        s = lax.rsqrt(pivots)
        s = s * (1.5 - 0.5 * pivots * s * s)
        r = jnp.where(lane >= sub + 8 * g, r * s, 0.0)
        v = v * s
        upper.append(r)
        inverse.append(v)
        if g < groups - 1:
            t = dot_tn(stacked(r, True), stacked(jnp.concatenate([r, v], axis=1), False))
            for h in range(g + 1, groups):
                a[h] = a[h] - t[8 * h : 8 * h + 8, :BLOCK]
                w[h] = w[h] - t[8 * h : 8 * h + 8, BLOCK:]
    return jnp.concatenate(upper, axis=0), jnp.concatenate(inverse, axis=0)


def factor_tile(m, v_ref, l_ref):
    b = BLOCK
    u0, v0 = factor_block([m[8 * g : 8 * g + 8, 0:b] for g in range(b // 8)])
    u01 = jnp.dot(v0, m[0:b, b:], precision=HIGHEST, preferred_element_type=F32)
    m[b:, b:] = m[b:, b:] - dot_tn(u01, u01, HIGHEST)
    u1, v1 = factor_block([m[b + 8 * g : b + 8 * g + 8, b:] for g in range(b // 8)])
    w = dot_tn(u01, v0, HIGHEST)
    zeros = jnp.zeros((b, b), F32)
    v_ref[0:b, 0:b] = v0
    v_ref[0:b, b:] = zeros
    v_ref[b:, 0:b] = -jnp.dot(v1, w, precision=HIGHEST, preferred_element_type=F32)
    v_ref[b:, b:] = v1
    l_ref[0:b, 0:b] = u0.T
    l_ref[0:b, b:] = zeros
    l_ref[b:, 0:b] = u01.T
    l_ref[b:, b:] = u1.T


def first_kernel(d00, v00, l00, m):
    m[...] = d00[...]
    factor_tile(m, v00, l00)


def second_kernel(d10, d11, v00, v10, v11, l11, m):
    u01 = lax.dot_general(
        v00[...], d10[...], (((1,), (1,)), ((), ())), precision=HIGHEST, preferred_element_type=F32
    )
    m[...] = d11[...] - dot_tn(u01, u01, HIGHEST)
    factor_tile(m, v11, l11)
    w = dot_tn(u01, v00[...], HIGHEST)
    v10[...] = -jnp.dot(v11[...], w, precision=HIGHEST, preferred_element_type=F32)


def factor_call(kernel, outs, *args):
    vmem = pl.BlockSpec(memory_space=pltpu.VMEM)
    return pl.pallas_call(
        kernel,
        out_shape=[jax.ShapeDtypeStruct((TILE, TILE), F32)] * outs,
        in_specs=[vmem] * len(args),
        out_specs=[vmem] * outs,
        scratch_shapes=[pltpu.VMEM((TILE, TILE), F32)],
        compiler_params=pltpu.CompilerParams(vmem_limit_bytes=16 * 2**20),
        cost_estimate=pl.CostEstimate(
            flops=10 * 10**9, bytes_accessed=2**20, transcendentals=0
        ),
    )(*args)


def halves(x):
    hi = x.astype(BF16)
    return hi, (x - hi.astype(F32)).astype(BF16)


def dot3(a, b, dims):
    ah, al = a
    bh, bl = b
    d = (dims, ((), ()))
    out = lax.dot_general(ah, bh, d, preferred_element_type=F32)
    out = out + lax.dot_general(ah, bl, d, preferred_element_type=F32)
    return out + lax.dot_general(al, bh, d, preferred_element_type=F32)


NT = ((1,), (1,))
NN = ((1,), (0,))
CHUNK = 512


def update_kernel(
    place, mat, v00_ref, v10_ref, v11_ref, l00, l11, mine, other, g0, g1, g2, g3, out,
    m, o, ap, dq, lp, lph, lpl, lqh, lql, in_sem, piece_sem, out_sem,
):
    row, col = place[0], place[1]
    y, x = row // 4, row % 4
    c = col % 2
    rows, cols = mat.shape
    chunks = cols // CHUNK
    copies = []

    def fetch(src, dst):
        copy = pltpu.make_async_copy(src, dst, piece_sem.at[len(copies)])
        copy.start()
        copies.append(copy)

    fetch(mine, ap.at[c])
    fetch(other, ap.at[1 - c])
    major = jnp.where(c == 0, x, y)
    for k, ref in enumerate((g0, g1, g2, g3)):
        source = lax.rem(major + 4 - k, 4)
        middle = jnp.logical_or(source == 1, source == 2).astype(jnp.int32)
        for j in range(2):
            panel = jnp.where(c == 0, middle, j)
            start = jnp.where(c == 0, (source // 2) * 1024 + 512 * j, source * 512)
            fetch(ref.at[j], dq.at[panel, :, pl.ds(pl.multiple_of(start, 512), 512)])
    loads = []
    for j in range(chunks):
        copy = pltpu.make_async_copy(
            mat.at[:, pl.ds(j * CHUNK, CHUNK)], m.at[:, pl.ds(j * CHUNK, CHUNK)], in_sem.at[j]
        )
        copy.start()
        loads.append(copy)

    for copy in copies[:2]:
        copy.wait()
    v00 = halves(v00_ref[...])
    v10 = halves(v10_ref[...])
    v11 = halves(v11_ref[...])
    for i in range(rows // TILE):
        at = pl.ds(i * TILE, TILE)
        a0 = halves(ap[0, at, :])
        a1 = halves(ap[1, at, :])
        first = dot3(a0, v00, NT)
        second = dot3(a0, v10, NT) + dot3(a1, v11, NT)
        lp[at, 0:TILE] = first
        lp[at, TILE:] = second
        lph[at, 0:TILE], lpl[at, 0:TILE] = halves(first)
        lph[at, TILE:], lpl[at, TILE:] = halves(second)
    for copy in copies[2:]:
        copy.wait()
    stores = []
    for j in range(chunks):
        at = pl.ds(j * CHUNK, CHUNK)
        d0 = halves(dq[0, :, at])
        d1 = halves(dq[1, :, at])
        lqh[0:TILE, :], lql[0:TILE, :] = halves(dot3(v00, d0, NN))
        lqh[TILE:, :], lql[TILE:, :] = halves(dot3(v10, d0, NN) + dot3(v11, d1, NN))
        loads[j].wait()
        for i in range(rows // TILE):
            r = pl.ds(i * TILE, TILE)
            o[r, at] = m[r, at] - dot3(
                (lph[r, :], lpl[r, :]), (lqh[...], lql[...]), NN
            )

        @pl.when(row < 2)
        def _():
            o[0:TILE, at] = jnp.zeros((TILE, CHUNK), F32)

        if j == 0:
            @pl.when(col == 0)
            def _():
                o[:, 0:TILE] = lp[:, 0:TILE]

                @pl.when(row == 0)
                def _():
                    o[0:TILE, 0:TILE] = l00[...]

            @pl.when(col == 1)
            def _():
                o[:, 0:TILE] = lp[:, TILE:]

                @pl.when(row == 0)
                def _():
                    o[0:TILE, 0:TILE] = jnp.zeros((TILE, TILE), F32)

                @pl.when(row == 1)
                def _():
                    o[0:TILE, 0:TILE] = l11[...]

        copy = pltpu.make_async_copy(o.at[:, at], out.at[:, at], out_sem.at[j])
        copy.start()
        stores.append(copy)
    for copy in stores:
        copy.wait()


def update(place, mat, v00, v10, v11, l00, l11, mine, other, pieces):
    rows, cols = mat.shape
    n = 2 * TILE
    chunks = cols // CHUNK
    hbm = pl.BlockSpec(memory_space=pl.ANY)
    vmem = pl.BlockSpec(memory_space=pltpu.VMEM)
    smem = pl.BlockSpec(memory_space=pltpu.SMEM)
    return pl.pallas_call(
        update_kernel,
        out_shape=jax.ShapeDtypeStruct((rows, cols), F32),
        in_specs=[smem, hbm] + [vmem] * 5 + [hbm] * 6,
        out_specs=hbm,
        scratch_shapes=[
            pltpu.VMEM((rows, cols), F32),
            pltpu.VMEM((rows, cols), F32),
            pltpu.VMEM((2, rows, TILE), F32),
            pltpu.VMEM((2, TILE, cols), F32),
            pltpu.VMEM((rows, n), F32),
            pltpu.VMEM((rows, n), BF16),
            pltpu.VMEM((rows, n), BF16),
            pltpu.VMEM((n, CHUNK), BF16),
            pltpu.VMEM((n, CHUNK), BF16),
            pltpu.SemaphoreType.DMA((chunks,)),
            pltpu.SemaphoreType.DMA((10,)),
            pltpu.SemaphoreType.DMA((chunks,)),
        ],
        compiler_params=pltpu.CompilerParams(vmem_limit_bytes=48 * 2**20),
        cost_estimate=pl.CostEstimate(
            flops=10 * 10**9, bytes_accessed=24 * 2**20, transcendentals=0
        ),
    )(place, mat, v00, v10, v11, l00, l11, mine, other, *pieces)


def along(axis, table, core, fixed=None):
    fixed = fixed or {}
    moves = []
    spans = [fixed.get(k, R4) for k in "yxz"]
    at = "yxz".index(axis)
    for a, b in table:
        spans[at] = (a,)
        for y in spans[0]:
            for x in spans[1]:
                for z in spans[2]:
                    dst = [y, x, z, core]
                    dst[at] = b
                    moves.append(((y, x, z, core), tuple(dst)))
    return moves


def swap_cores(value):
    return send(value, [((y, x, z, c), (y, x, z, 1 - c)) for y in R4 for x in R4 for z in R4 for c in R2])


def chain(value, place, root, orders, turns):
    c = place["c"]
    fixed = [{k: (root[k],) for k in "yxz"} for _ in R2]
    for step in range(3):
        axes = [orders[core][step] for core in R2]
        spots = []
        for core in R2:
            s, t = root[axes[core]], turns[core]
            spots.append((s, (s + t) % 4, (s - t) % 4, (s + 2) % 4))
        here = jnp.where(c == 0, place[axes[0]], place[axes[1]])

        def at(k):
            return here == jnp.where(c == 0, spots[0][k], spots[1][k])

        moves = []
        for core in R2:
            s, near, far, opposite = spots[core]
            moves += along(axes[core], [(s, near)], core, fixed[core])
        value = jnp.where(at(1), send(value, moves), value)
        moves = []
        for core in R2:
            s, near, far, opposite = spots[core]
            moves += along(axes[core], [(s, far), (near, opposite)], core, fixed[core])
        value = jnp.where(at(2) | at(3), send(value, moves), value)
        for core in R2:
            fixed[core][axes[core]] = R4
    return value


def shards(matrix):
    row = lax.axis_index("row")
    col = lax.axis_index("col")
    y, x = row // 4, row % 4
    z, c = col // 2, col % 2
    place = {"y": y, "x": x, "z": z, "c": c}
    zero_core = c == 0
    half = TILE // 2

    tile = matrix[0:TILE, 0:TILE]
    lower = send(tile[half:], [((0, 0, 0, 0), (0, 0, 0, 1))])
    part = jnp.where(zero_core, tile[:half], lower)
    part = chain(part, place, {"y": 0, "x": 0, "z": 0}, ("xyz", "yzx"), (1, 1))
    rest = swap_cores(part)
    d00 = jnp.concatenate([jnp.where(zero_core, part, rest), jnp.where(zero_core, rest, part)], axis=0)
    next_part = chain(tile, place, {"y": 0, "x": 1, "z": 0}, ("zxy", "zyx"), (1, -1))
    next_rest = swap_cores(next_part)
    d10 = jnp.where(zero_core, next_part, next_rest)
    d11 = jnp.where(zero_core, next_rest, next_part)

    v00, l00 = factor_call(first_kernel, 2, d00)
    v10, v11, l11 = factor_call(second_kernel, 3, d10, d11, v00)

    strip = matrix[:, 0:TILE]
    r1 = send(strip, along("z", [(0, 1)], 0) + along("z", [(0, 3)], 1))
    first_stop = jnp.where(zero_core, 1, 3)
    mine = jnp.where(z == first_stop, r1, strip)
    r2 = send(mine, along("z", [(0, 3), (1, 2)], 0) + along("z", [(0, 1), (3, 2)], 1))
    mine = jnp.where((z == 0) | (z == first_stop), mine, r2)
    other = swap_cores(mine)

    pick = lambda a, b: jnp.where(zero_core, a, b)
    quarters = [matrix[0:TILE, 512 * i : 512 * (i + 1)] for i in R4]
    top = {"y": (0,)}
    out0 = along("x", [(0, 3), (1, 2)], 0, top)
    sides = {"x": (0, 1)}
    a1 = send(pick(quarters[2], quarters[1]), out0 + along("y", [(0, 1)], 1, sides))
    a2 = send(pick(quarters[3], quarters[2]), out0 + along("y", [(0, 2)], 1, sides))
    a3 = send(quarters[3], along("y", [(0, 3)], 1, sides))
    qa = jnp.where(x < 2, quarters[0], a1)
    qb = jnp.where(x < 2, quarters[1], a2)
    s = jnp.where(y == 0, quarters[0], jnp.where(y == 1, a1, jnp.where(y == 2, a2, a3)))
    b1 = send(pick(qa, s), along("y", [(0, 1)], 0) + along("x", [(0, 1), (1, 0)], 1))
    b2 = send(pick(qb, s), along("y", [(0, 3)], 0) + along("x", [(0, 3), (1, 2)], 1))
    b3 = send(
        pick(jnp.where(y == 0, qa, b1), b2),
        along("y", [(0, 3), (1, 2)], 0) + along("x", [(3, 2), (2, 3)], 1),
    )
    b4 = send(jnp.where(y == 0, qb, b2), along("y", [(0, 1), (3, 2)], 0))
    qa = jnp.where(y == 0, qa, jnp.where(y == 1, b1, b3))
    qb = jnp.where(y == 0, qb, jnp.where(y == 3, b2, b4))
    p0 = jnp.where(x == 0, s, jnp.where(x == 1, b1, jnp.where(x == 2, b3, b2)))
    p1 = jnp.where(x == 0, b1, jnp.where(x == 1, s, jnp.where(x == 2, b2, b3)))
    both = jnp.stack([pick(qa, p0), pick(qb, p1)])
    pieces = [both]
    for k in (1, 2, 3):
        turn = [(i, (i + k) % 4) for i in R4]
        pieces.append(send(both, along("x", turn, 0) + along("y", turn, 1)))

    where = jnp.stack([row, col]).astype(jnp.int32)
    return update(where, matrix, v00, v10, v11, l00, l11, mine, other, pieces)


def solution(mesh):
    return jax.shard_map(
        shards,
        mesh=mesh,
        in_specs=(P("row", "col"),),
        out_specs=P("row", "col"),
        check_vma=False,
    )
```

time: 181 us -> 129 us (0.71)
  the two profiles are of different devices: /device:TPU:1 before, /device:TPU:101 now
where the time goes in v2:
time: 129 us; the launch traced here: 128 us
  Pallas kernels  43.5 us (34%)
  waiting for transfers between devices  42.9 us (33%)
  starting transfers between devices  27 us (21%)
  other arithmetic  9.21 us (7%)
  local copies, waits for them, and re-layouts  4.46 us (3%)
    ppermute x28, waiting for transfers between devices, send(): return lax.ppermute(value, ('row', 'col'), pairs(moves))  42.9 us
    ppermute x28, starting transfers between devices, send(): return lax.ppermute(value, ('row', 'col'), pairs(moves))  27 us
    pallas_call x2, Pallas kernels, factor_call(): pl.pallas_call(kernel, out_shape=[jax.ShapeDtypeStruct((TILE, TILE), F32)...  26.3 us
    pallas_call x1, Pallas kernels, update(): pl.pallas_call(update_kernel, out_shape=jax.ShapeDtypeStruct((rows, cols)...  17.2 us
    select_n x2, other arithmetic, shards(): pick = lambda a, b: jnp.where(zero_core, a, b)  3.02 us
  transfers between devices with their start and end apart: 28, of which 4 were waited for; matrix products, arithmetic and copies ran while one was open for 8% of the time, Pallas kernels for 21%

profile of v2, /device:TPU:101, one launch (start us, length us, event | category | flops | bytes accessed | tf_op | source)
XLA Modules:
  0.0 127.8 jit_solution(5295335414684081080)
XLA Ops:
  0.0 0.9 slice.27
  1.6 0.9 slice_select_fusion.4
  3.2 1.0 slice.28
  4.2 0.7 collective-permute-start.8
  5.6 1.6 %fusion = (f32[256,512]{1,0:T(8,128)S(1)}, f32[256,512]{1,0:T(8,128)S(1)}, f32[256,512]{1,0:T(8,128)S(1)}) fusion(f32[1024,2048]{1,0:T(8,128)} %mat.1, pred[]{:T(512)S(6)} %eq.57), kind=kLoop, calls=%fused_computation.33 | loop fusion | flops 262144 | bytes 3145729 | tf_op jit(solution)/shard_map/slice | solution.py:367
  7.2 1.5 %collective-permute-start.20 = (f32[256,512]{1,0:T(8,128)S(1)}, f32[256,512]{1,0:T(8,128)}, u32[]{:S(2)}, u32[]{:S(2)}) collective-permute-start(f32[256,512]{1,0:T(8,128)S(1)} %get-tuple-element.20), channel_id=1, source_target_pairs={{1,97},{3,99},{5,101},{7,103},{9,105},{11,107},{13,109},{15,111}} | collective-permute-start | bytes 1572872 | tf_op jit(solution)/shard_map/ppermute | solution.py:28
  8.7 0.7 collective-permute-start.18
  9.4 1.5 %collective-permute-start.19 = (f32[256,512]{1,0:T(8,128)S(1)}, f32[256,512]{1,0:T(8,128)}, u32[]{:S(2)}, u32[]{:S(2)}) collective-permute-start(f32[256,512]{1,0:T(8,128)S(1)} %get-tuple-element.22), channel_id=1, source_target_pairs={{0,24},{2,26},{4,28},{6,30},{8,16},{10,18},{12,20},{14,22},{1,65},... | collective-permute-start | bytes 1572872 | tf_op jit(solution)/shard_map/ppermute | solution.py:28
  10.9 1.3 %collective-permute-start.3 = (f32[128,256]{1,0:T(8,128)S(1)}, f32[128,256]{1,0:T(8,128)}, u32[]{:S(2)}, u32[]{:S(2)}) collective-permute-start(f32[128,256]{1,0:T(8,128)S(1)} %broadcast_select_fusion.14), channel_id=1, source_target_pairs={{0,32},{8,40},{16,48},{24,56},{1,3},{33,35},{65,67},{97,99}} | collective-permute-start | bytes 393224 | tf_op jit(solution)/shard_map/ppermute | solution.py:28
  12.2 1.0 broadcast_select_fusion.5
  13.2 1.4 %collective-permute-start.9 = (f32[256,256]{1,0:T(8,128)S(1)}, f32[256,256]{1,0:T(8,128)}, u32[]{:S(2)}, u32[]{:S(2)}) collective-permute-start(f32[256,256]{1,0:T(8,128)S(1)} %broadcast_select_fusion.5), channel_id=1, source_target_pairs={{8,14},{10,12},{9,11},{15,13}} | collective-permute-start | bytes 786440 | tf_op jit(solution)/shard_map/ppermute | solution.py:28
  14.6 1.3 %slice.29 = f32[1024,256]{1,0:T(8,128)S(1)} slice(f32[1024,2048]{1,0:T(8,128)} %mat.1), slice={[0:1024], [0:256]} | slice | bytes 2097152 | tf_op jit(solution)/shard_map/slice | solution.py:358
  16.0 1.3 %collective-permute-start.15 = (f32[1024,256]{1,0:T(8,128)S(1)}, f32[1024,256]{1,0:T(8,128)S(1)}, u32[]{:S(2)}, u32[]{:S(2)}) collective-permute-start(f32[1024,256]{1,0:T(8,128)S(1)} %slice.29), channel_id=1, source_target_pairs={{0,2},{8,10},{16,18},{24,26},{32,34},{40,42},{48,50},{56,58},{64,6... | collective-permute-start | bytes 3145736 | tf_op jit(solution)/shard_map/ppermute | solution.py:28
  18.8 1.8 %broadcast_select_fusion.3 = (f32[256,512]{1,0:T(8,128)S(1)}, f32[256,512]{1,0:T(8,128)S(1)}, f32[256,512]{1,0:T(8,128)S(1)}) fusion(pred[]{:T(512)S(6)} %eq.57, f32[256,512]{1,0:T(8,128)} %collective-permute-done.19, f32[1024,2048]{1,0:T(8,128)} %mat.1, pred[]{:T(512)S(6)} %lt.16, f32[256,512]{1,0:T(8,128)S(1)} %collective-permute-done.18, ...), kind=kLoop, calls=%fused_computation.13 | loop fusion | flops 655360 | bytes 4194309 | tf_op jit(solution)/shard_map/jit(_where)/select_n | solution.py:366
  22.1 1.3 %collective-permute-start.6 = (f32[128,256]{1,0:T(8,128)S(1)}, f32[128,256]{1,0:T(8,128)S(1)}, u32[]{:S(2)}, u32[]{:S(2)}) collective-permute-start(f32[128,256]{1,0:T(8,128)S(1)} %broadcast_select_fusion.17), channel_id=1, source_target_pairs={{0,6},{8,14},{16,22},{24,30},{32,38},{40,46},{48,54},{56,62},{64,7... | collective-permute-start | bytes 393224 | tf_op jit(solution)/shard_map/ppermute | solution.py:28
  23.4 1.2 broadcast_select_fusion.4
  24.6 0.7 collective-permute-start.21
  25.3 1.3 %collective-permute-start.22 = (f32[256,512]{1,0:T(8,128)S(1)}, f32[256,512]{1,0:T(8,128)S(1)}, u32[]{:S(2)}, u32[]{:S(2)}) collective-permute-start(f32[256,512]{1,0:T(8,128)S(1)} %get-tuple-element.15), channel_id=1, source_target_pairs={{0,96},{2,98},{4,100},{6,102},{8,104},{10,106},{12,108},{14,110},{... | collective-permute-start | bytes 1572872 | tf_op jit(solution)/shard_map/ppermute | solution.py:28
  26.6 20.9 %collective-permute-done.6 = f32[128,256]{1,0:T(8,128)S(1)} collective-permute-done((f32[128,256]{1,0:T(8,128)S(1)}, f32[128,256]{1,0:T(8,128)S(1)}, u32[]{:S(2)}, u32[]{:S(2)}) %collective-permute-start.6) | collective-permute-done | bytes 131104 | tf_op jit(solution)/shard_map/ppermute | solution.py:28
  48.3 1.3 %broadcast_select_fusion = f32[1024,256]{1,0:T(8,128)S(1)} fusion(f32[1024,256]{1,0:T(8,128)S(1)} %collective-permute-done.15, pred[]{:T(512)S(6)} %eq.136, f32[1024,2048]{1,0:T(8,128)} %mat.1), kind=kLoop, calls=%fused_computation.5 | loop fusion | flops 262144 | bytes 3145729 | tf_op jit(solution)/shard_map/jit(_where)/select_n | solution.py:361
  49.7 1.4 %collective-permute-start.16 = (f32[1024,256]{1,0:T(8,128)S(1)}, f32[1024,256]{1,0:T(8,128)S(1)}, u32[]{:S(2)}, u32[]{:S(2)}) collective-permute-start(f32[1024,256]{1,0:T(8,128)S(1)} %broadcast_select_fusion), channel_id=1, source_target_pairs={{0,6},{8,14},{16,22},{24,30},{32,38},{40,46},{48,54},{56,62},{64,7... | collective-permute-start | bytes 3145736 | tf_op jit(solution)/shard_map/ppermute | solution.py:28
  51.1 5.1 %collective-permute-done.22 = f32[256,512]{1,0:T(8,128)S(1)} collective-permute-done((f32[256,512]{1,0:T(8,128)S(1)}, f32[256,512]{1,0:T(8,128)S(1)}, u32[]{:S(2)}, u32[]{:S(2)}) %collective-permute-start.22) | collective-permute-done | bytes 524320 | tf_op jit(solution)/shard_map/ppermute | solution.py:28
  56.3 0.7 collective-permute-start.24
  57.0 4.3 %collective-permute-start.23 = (f32[256,512]{1,0:T(8,128)S(1)}, f32[256,512]{1,0:T(8,128)S(1)}, u32[]{:S(2)}, u32[]{:S(2)}) collective-permute-start(f32[256,512]{1,0:T(8,128)S(1)} %get-tuple-element.26), channel_id=1, source_target_pairs={{0,96},{2,98},{4,100},{6,102},{8,104},{10,106},{12,108},{14,110},{... | collective-permute-start | bytes 1572872 | tf_op jit(solution)/shard_map/ppermute | solution.py:28
  61.4 12.4 %shard_map.17 = (f32[256,256]{1,0:T(8,128)S(1)}, f32[256,256]{1,0:T(8,128)S(1)}) custom-call(f32[256,256]{1,0:T(8,128)S(1)} %pad_maximum_fusion.1.d00), custom_call_target="tpu_custom_call" | custom-call | flops 10000000000 | bytes 1048576 | tf_op jit(solution)/shard_map/pallas_call | solution.py:124
  73.8 1.3 %collective-permute-start.13 = (f32[256,256]{1,0:T(8,128)S(1)}, f32[256,256]{1,0:T(8,128)S(1)}, u32[]{:S(2)}, u32[]{:S(2)}) collective-permute-start(f32[256,256]{1,0:T(8,128)S(1)} %broadcast_select_fusion.9), channel_id=1, source_target_pairs={{0,96},{2,98},{4,100},{6,102},{8,104},{10,106},{12,108},{14,110},{... | collective-permute-start | bytes 786440 | tf_op jit(solution)/shard_map/ppermute | solution.py:28
  75.8 1.4 %collective-permute-start.25 = (f32[2,256,512]{2,1,0:T(8,128)S(1)}, f32[2,256,512]{2,1,0:T(8,128)S(1)}, u32[]{:S(2)}, u32[]{:S(2)}) collective-permute-start(f32[2,256,512]{2,1,0:T(8,128)S(1)} %pad_maximum_fusion.g0), channel_id=1, source_target_pairs={{0,8},{2,10},{4,12},{6,14},{32,40},{34,42},{36,44},{38,46},{64,72}... | collective-permute-start | bytes 3145736 | tf_op jit(solution)/shard_map/ppermute | solution.py:28
  77.2 16.3 %collective-permute-done.13 = f32[256,256]{1,0:T(8,128)S(1)} collective-permute-done((f32[256,256]{1,0:T(8,128)S(1)}, f32[256,256]{1,0:T(8,128)S(1)}, u32[]{:S(2)}, u32[]{:S(2)}) %collective-permute-start.13) | collective-permute-done | bytes 262176 | tf_op jit(solution)/shard_map/ppermute | solution.py:28
  93.8 0.7 collective-permute-start.17
  95.2 14.0 %shard_map.18 = (f32[256,256]{1,0:T(8,128)S(1)}, f32[256,256]{1,0:T(8,128)S(1)}, f32[256,256]{1,0:T(8,128)S(1)}) custom-call(f32[256,256]{1,0:T(8,128)S(1)} %get-tuple-element.28.d10, f32[256,256]{1,0:T(8,128)S(1)} %get-tuple-element.27.d11, f32[256,256]{1,0:T(8,128)S(1)} %get-tuple-element.10.v00.v00_ref), custom_call_target="tpu_custom_call" | custom-call | flops 10000000000 | bytes 1048576 | tf_op jit(solution)/shard_map/pallas_call | solution.py:124
  109.2 0.9 copy-done
  110.5 17.2 %shard_map.19 = f32[1024,2048]{1,0:T(8,128)} custom-call(s32[2]{0:T(128)S(1)} %pad_add_fusion.place, f32[1024,2048]{1,0:T(8,128)} %mat.1, f32[256,256]{1,0:T(8,128)S(1)} %get-tuple-element.10.v00.v00_ref, f32[256,256]{1,0:T(8,128)S(1)} %get-tuple-element.11.v10_ref, f32[256,256]{1,0:T(8,128)S(1)} %get-tuple-element.12.v11_ref, ...), custom_call_target="tpu_custom_call" | custom-call | flops 10000000000 | bytes 25165824 | tf_op jit(solution)/shard_map/pallas_call | solution.py:260
  (59 shorter events, 8.1 us)
Async XLA Ops:
  0.9 0.7 collective-permute-start
  2.5 2.4 %collective-permute-start.1 = (f32[128,256]{1,0:T(8,128)S(1)}, f32[128,256]{1,0:T(8,128)S(1)}, u32[]{:S(2)}, u32[]{:S(2)}) collective-permute-start(f32[128,256]{1,0:T(8,128)S(1)} %slice_select_fusion.4), channel_id=1, source_target_pairs={{0,8},{1,33}} | collective-permute-start | bytes 393224 | tf_op jit(solution)/shard_map/ppermute | solution.py:28
  4.2 8.0 %collective-permute-start.8 = (f32[256,256]{1,0:T(8,128)S(1)}, f32[256,256]{1,0:T(8,128)S(1)}, u32[]{:S(2)}, u32[]{:S(2)}) collective-permute-start(f32[256,256]{1,0:T(8,128)S(1)} %slice.28), channel_id=1, source_target_pairs={{8,10},{9,15}} | collective-permute-start | bytes 786440 | tf_op jit(solution)/shard_map/ppermute | solution.py:28
  4.9 5.9 %collective-permute-start.2 = (f32[128,256]{1,0:T(8,128)S(1)}, f32[128,256]{1,0:T(8,128)S(1)}, u32[]{:S(2)}, u32[]{:S(2)}) collective-permute-start(f32[128,256]{1,0:T(8,128)S(1)} %broadcast_select_fusion.13), channel_id=1, source_target_pairs={{0,24},{8,16},{1,97},{33,65}} | collective-permute-start | bytes 393224 | tf_op jit(solution)/shard_map/ppermute | solution.py:28
  7.2 10.9 %collective-permute-start.20 = (f32[256,512]{1,0:T(8,128)S(1)}, f32[256,512]{1,0:T(8,128)}, u32[]{:S(2)}, u32[]{:S(2)}) collective-permute-start(f32[256,512]{1,0:T(8,128)S(1)} %get-tuple-element.20), channel_id=1, source_target_pairs={{1,97},{3,99},{5,101},{7,103},{9,105},{11,107},{13,109},{15,111}} | collective-permute-start | bytes 1572872 | tf_op jit(solution)/shard_map/ppermute | solution.py:28
  8.7 10.1 %collective-permute-start.18 = (f32[256,512]{1,0:T(8,128)S(1)}, f32[256,512]{1,0:T(8,128)S(1)}, u32[]{:S(2)}, u32[]{:S(2)}) collective-permute-start(f32[256,512]{1,0:T(8,128)S(1)} %get-tuple-element.21), channel_id=1, source_target_pairs={{0,24},{2,26},{4,28},{6,30},{8,16},{10,18},{12,20},{14,22},{1,33},... | collective-permute-start | bytes 1572872 | tf_op jit(solution)/shard_map/ppermute | solution.py:28
  9.4 9.4 %collective-permute-start.19 = (f32[256,512]{1,0:T(8,128)S(1)}, f32[256,512]{1,0:T(8,128)}, u32[]{:S(2)}, u32[]{:S(2)}) collective-permute-start(f32[256,512]{1,0:T(8,128)S(1)} %get-tuple-element.22), channel_id=1, source_target_pairs={{0,24},{2,26},{4,28},{6,30},{8,16},{10,18},{12,20},{14,22},{1,65},... | collective-permute-start | bytes 1572872 | tf_op jit(solution)/shard_map/ppermute | solution.py:28
  10.9 5.1 %collective-permute-start.3 = (f32[128,256]{1,0:T(8,128)S(1)}, f32[128,256]{1,0:T(8,128)}, u32[]{:S(2)}, u32[]{:S(2)}) collective-permute-start(f32[128,256]{1,0:T(8,128)S(1)} %broadcast_select_fusion.14), channel_id=1, source_target_pairs={{0,32},{8,40},{16,48},{24,56},{1,3},{33,35},{65,67},{97,99}} | collective-permute-start | bytes 393224 | tf_op jit(solution)/shard_map/ppermute | solution.py:28
  13.2 4.1 %collective-permute-start.9 = (f32[256,256]{1,0:T(8,128)S(1)}, f32[256,256]{1,0:T(8,128)}, u32[]{:S(2)}, u32[]{:S(2)}) collective-permute-start(f32[256,256]{1,0:T(8,128)S(1)} %broadcast_select_fusion.5), channel_id=1, source_target_pairs={{8,14},{10,12},{9,11},{15,13}} | collective-permute-start | bytes 786440 | tf_op jit(solution)/shard_map/ppermute | solution.py:28
  16.0 32.4 %collective-permute-start.15 = (f32[1024,256]{1,0:T(8,128)S(1)}, f32[1024,256]{1,0:T(8,128)S(1)}, u32[]{:S(2)}, u32[]{:S(2)}) collective-permute-start(f32[1024,256]{1,0:T(8,128)S(1)} %slice.29), channel_id=1, source_target_pairs={{0,2},{8,10},{16,18},{24,26},{32,34},{40,42},{48,50},{56,58},{64,6... | collective-permute-start | bytes 3145736 | tf_op jit(solution)/shard_map/ppermute | solution.py:28
  17.3 3.3 %collective-permute-start.4 = (f32[128,256]{1,0:T(8,128)S(1)}, f32[128,256]{1,0:T(8,128)S(1)}, u32[]{:S(2)}, u32[]{:S(2)}) collective-permute-start(f32[128,256]{1,0:T(8,128)S(1)} %broadcast_select_fusion.15), channel_id=1, source_target_pairs={{0,96},{8,104},{16,112},{24,120},{32,64},{40,72},{48,80},{56,88},{... | collective-permute-start | bytes 393224 | tf_op jit(solution)/shard_map/ppermute | solution.py:28
  18.1 3.3 %collective-permute-start.10 = (f32[256,256]{1,0:T(8,128)S(1)}, f32[256,256]{1,0:T(8,128)S(1)}, u32[]{:S(2)}, u32[]{:S(2)}) collective-permute-start(f32[256,256]{1,0:T(8,128)S(1)} %broadcast_select_fusion.6), channel_id=1, source_target_pairs={{8,16},{10,18},{12,20},{14,22},{9,105},{11,107},{13,109},{15,111}} | collective-permute-start | bytes 786440 | tf_op jit(solution)/shard_map/ppermute | solution.py:28
  20.7 1.4 %collective-permute-start.5 = (f32[128,256]{1,0:T(8,128)S(1)}, f32[128,256]{1,0:T(8,128)S(1)}, u32[]{:S(2)}, u32[]{:S(2)}) collective-permute-start(f32[128,256]{1,0:T(8,128)S(1)} %broadcast_select_fusion.16), channel_id=1, source_target_pairs={{0,2},{8,10},{16,18},{24,26},{32,34},{40,42},{48,50},{56,58},{64,6... | collective-permute-start | bytes 393224 | tf_op jit(solution)/shard_map/ppermute | solution.py:28
  21.4 26.2 %collective-permute-start.11 = (f32[256,256]{1,0:T(8,128)S(1)}, f32[256,256]{1,0:T(8,128)S(1)}, u32[]{:S(2)}, u32[]{:S(2)}) collective-permute-start(f32[256,256]{1,0:T(8,128)S(1)} %broadcast_select_fusion.7), channel_id=1, source_target_pairs={{8,0},{10,2},{12,4},{14,6},{16,24},{18,26},{20,28},{22,30},{9,41},... | collective-permute-start | bytes 786440 | tf_op jit(solution)/shard_map/ppermute | solution.py:28
  22.1 25.4 %collective-permute-start.6 = (f32[128,256]{1,0:T(8,128)S(1)}, f32[128,256]{1,0:T(8,128)S(1)}, u32[]{:S(2)}, u32[]{:S(2)}) collective-permute-start(f32[128,256]{1,0:T(8,128)S(1)} %broadcast_select_fusion.17), channel_id=1, source_target_pairs={{0,6},{8,14},{16,22},{24,30},{32,38},{40,46},{48,54},{56,62},{64,7... | collective-permute-start | bytes 393224 | tf_op jit(solution)/shard_map/ppermute | solution.py:28
  24.6 26.5 %collective-permute-start.21 = (f32[256,512]{1,0:T(8,128)S(1)}, f32[256,512]{1,0:T(8,128)S(1)}, u32[]{:S(2)}, u32[]{:S(2)}) collective-permute-start(f32[256,512]{1,0:T(8,128)S(1)} %get-tuple-element.18), channel_id=1, source_target_pairs={{0,32},{2,34},{4,36},{6,38},{8,40},{10,42},{12,44},{14,46},{16,48}... | collective-permute-start | bytes 1572872 | tf_op jit(solution)/shard_map/ppermute | solution.py:28
  25.3 30.8 %collective-permute-start.22 = (f32[256,512]{1,0:T(8,128)S(1)}, f32[256,512]{1,0:T(8,128)S(1)}, u32[]{:S(2)}, u32[]{:S(2)}) collective-permute-start(f32[256,512]{1,0:T(8,128)S(1)} %get-tuple-element.15), channel_id=1, source_target_pairs={{0,96},{2,98},{4,100},{6,102},{8,104},{10,106},{12,108},{14,110},{... | collective-permute-start | bytes 1572872 | tf_op jit(solution)/shard_map/ppermute | solution.py:28
  47.5 13.8 %collective-permute-start.7 = (f32[128,256]{1,0:T(8,128)S(1)}, f32[128,256]{1,0:T(8,128)S(1)}, u32[]{:S(2)}, u32[]{:S(2)}) collective-permute-start(f32[128,256]{1,0:T(8,128)S(1)} %broadcast_select_fusion.18), channel_id=1, source_target_pairs={{0,1},{1,0},{2,3},{3,2},{4,5},{5,4},{6,7},{7,6},{8,9},{9,8},{10,11... | collective-permute-start | bytes 393224 | tf_op jit(solution)/shard_map/ppermute | solution.py:28
  47.7 26.1 %collective-permute-start.12 = (f32[256,256]{1,0:T(8,128)S(1)}, f32[256,256]{1,0:T(8,128)S(1)}, u32[]{:S(2)}, u32[]{:S(2)}) collective-permute-start(f32[256,256]{1,0:T(8,128)S(1)} %broadcast_select_fusion.8), channel_id=1, source_target_pairs={{0,32},{2,34},{4,36},{6,38},{8,40},{10,42},{12,44},{14,46},{16,48}... | collective-permute-start | bytes 786440 | tf_op jit(solution)/shard_map/ppermute | solution.py:28
  49.7 43.9 %collective-permute-start.16 = (f32[1024,256]{1,0:T(8,128)S(1)}, f32[1024,256]{1,0:T(8,128)S(1)}, u32[]{:S(2)}, u32[]{:S(2)}) collective-permute-start(f32[1024,256]{1,0:T(8,128)S(1)} %broadcast_select_fusion), channel_id=1, source_target_pairs={{0,6},{8,14},{16,22},{24,30},{32,38},{40,46},{48,54},{56,62},{64,7... | collective-permute-start | bytes 3145736 | tf_op jit(solution)/shard_map/ppermute | solution.py:28
  56.3 18.8 %collective-permute-start.24 = (f32[256,512]{1,0:T(8,128)S(1)}, f32[256,512]{1,0:T(8,128)S(1)}, u32[]{:S(2)}, u32[]{:S(2)}) collective-permute-start(f32[256,512]{1,0:T(8,128)S(1)} %get-tuple-element.25), channel_id=1, source_target_pairs={{0,32},{2,34},{4,36},{6,38},{8,40},{10,42},{12,44},{14,46},{16,48}... | collective-permute-start | bytes 1572872 | tf_op jit(solution)/shard_map/ppermute | solution.py:28
  57.0 18.1 %collective-permute-start.23 = (f32[256,512]{1,0:T(8,128)S(1)}, f32[256,512]{1,0:T(8,128)S(1)}, u32[]{:S(2)}, u32[]{:S(2)}) collective-permute-start(f32[256,512]{1,0:T(8,128)S(1)} %get-tuple-element.26), channel_id=1, source_target_pairs={{0,96},{2,98},{4,100},{6,102},{8,104},{10,106},{12,108},{14,110},{... | collective-permute-start | bytes 1572872 | tf_op jit(solution)/shard_map/ppermute | solution.py:28
  73.8 19.7 %collective-permute-start.13 = (f32[256,256]{1,0:T(8,128)S(1)}, f32[256,256]{1,0:T(8,128)S(1)}, u32[]{:S(2)}, u32[]{:S(2)}) collective-permute-start(f32[256,256]{1,0:T(8,128)S(1)} %broadcast_select_fusion.9), channel_id=1, source_target_pairs={{0,96},{2,98},{4,100},{6,102},{8,104},{10,106},{12,108},{14,110},{... | collective-permute-start | bytes 786440 | tf_op jit(solution)/shard_map/ppermute | solution.py:28
  75.7 33.5 %collective-permute-start.27 = (f32[2,256,512]{2,1,0:T(8,128)S(1)}, f32[2,256,512]{2,1,0:T(8,128)S(1)}, u32[]{:S(2)}, u32[]{:S(2)}) collective-permute-start(f32[2,256,512]{2,1,0:T(8,128)S(1)} %pad_maximum_fusion.g0), channel_id=1, source_target_pairs={{0,24},{2,26},{4,28},{6,30},{32,56},{34,58},{36,60},{38,62},{64,88... | collective-permute-start | bytes 3145736 | tf_op jit(solution)/shard_map/ppermute | solution.py:28
  75.7 33.4 %collective-permute-start.26 = (f32[2,256,512]{2,1,0:T(8,128)S(1)}, f32[2,256,512]{2,1,0:T(8,128)S(1)}, u32[]{:S(2)}, u32[]{:S(2)}) collective-permute-start(f32[2,256,512]{2,1,0:T(8,128)S(1)} %pad_maximum_fusion.g0), channel_id=1, source_target_pairs={{0,16},{2,18},{4,20},{6,22},{32,48},{34,50},{36,52},{38,54},{64,80... | collective-permute-start | bytes 3145736 | tf_op jit(solution)/shard_map/ppermute | solution.py:28
  75.8 33.3 %collective-permute-start.25 = (f32[2,256,512]{2,1,0:T(8,128)S(1)}, f32[2,256,512]{2,1,0:T(8,128)S(1)}, u32[]{:S(2)}, u32[]{:S(2)}) collective-permute-start(f32[2,256,512]{2,1,0:T(8,128)S(1)} %pad_maximum_fusion.g0), channel_id=1, source_target_pairs={{0,8},{2,10},{4,12},{6,14},{32,40},{34,42},{36,44},{38,46},{64,72}... | collective-permute-start | bytes 3145736 | tf_op jit(solution)/shard_map/ppermute | solution.py:28
  93.5 1.6 %collective-permute-start.14 = (f32[256,256]{1,0:T(8,128)S(1)}, f32[256,256]{1,0:T(8,128)S(1)}, u32[]{:S(2)}, u32[]{:S(2)}) collective-permute-start(f32[256,256]{1,0:T(8,128)S(1)} %broadcast_select_fusion.10), channel_id=1, source_target_pairs={{0,1},{1,0},{2,3},{3,2},{4,5},{5,4},{6,7},{7,6},{8,9},{9,8},{10,11... | collective-permute-start | bytes 786440 | tf_op jit(solution)/shard_map/ppermute | solution.py:28
  93.8 15.4 %collective-permute-start.17 = (f32[1024,256]{1,0:T(8,128)S(1)}, f32[1024,256]{1,0:T(8,128)S(1)}, u32[]{:S(2)}, u32[]{:S(2)}) collective-permute-start(f32[1024,256]{1,0:T(8,128)S(1)} %broadcast_select_fusion.1.mine), channel_id=1, source_target_pairs={{0,1},{1,0},{2,3},{3,2},{4,5},{5,4},{6,7},{7,6},{8,9},{9,8},{10,11... | collective-permute-start | bytes 3145736 | tf_op jit(solution)/shard_map/ppermute | solution.py:28
  109.1 1.0 copy-start
  109.2 1.3 %copy-start.1 = (f32[2,256,512]{2,1,0:T(8,128)}, f32[2,256,512]{2,1,0:T(8,128)S(1)}, u32[]{:S(2)}) copy-start(f32[2,256,512]{2,1,0:T(8,128)S(1)} %collective-permute-done.26.g2) | copy-start | bytes 3145732

commit v3 on v2

v3 whole, which is shorter than its diff:
```python
import functools

import jax
import jax.numpy as jnp
from jax import lax
from jax.experimental import pallas as pl
from jax.experimental.pallas import tpu as pltpu
from jax.sharding import PartitionSpec as P

TILE = 256
BLOCK = 128
F32 = jnp.float32
BF16 = jnp.bfloat16
HIGHEST = lax.Precision.HIGHEST


def device_id(y, x, z, c):
    return ((4 * y + x) * 4 + z) * 2 + c


def pairs(moves):
    return [(device_id(*a), device_id(*b)) for a, b in moves]


R4 = range(4)
R2 = range(2)


def send(value, moves):
    return lax.ppermute(value, ("row", "col"), pairs(moves))


def split3(x):
    hi = x.astype(BF16).astype(F32)
    rest = x - hi
    mid = rest.astype(BF16).astype(F32)
    return hi, mid, rest - mid


def stacked(x, left):
    hi, mid, lo = split3(x)
    parts = [hi, hi, mid, hi, lo, mid] if left else [hi, mid, hi, lo, hi, mid]
    return jnp.concatenate(parts, axis=0).astype(BF16)


def dot_tn(a, b, precision=None):
    return lax.dot_general(
        a, b, (((0,), (0,)), ((), ())), precision=precision, preferred_element_type=F32
    )


def spread(x):
    return jnp.broadcast_to(x, (8, BLOCK))


def factor_block(rows):
    groups, per = BLOCK // 8, 2
    width = 8 * per
    sub = lax.broadcasted_iota(jnp.int32, (8, BLOCK), 0)
    lane = lax.broadcasted_iota(jnp.int32, (8, BLOCK), 1)
    a = list(rows)
    w = [jnp.where(lane == sub + 8 * g, 1.0, 0.0).astype(F32) for g in range(groups)]
    upper, inverse = [], []
    for g in range(0, groups, per):
        r, v = a[g : g + per], w[g : g + per]
        cols = [[spread(x[:, 8 * g + i : 8 * g + i + 1]) for x in r] for i in range(width)]
        pivots = [None] * per
        for i in range(width):
            at, s = divmod(i, 8)
            p = spread(cols[i][at][s : s + 1, :])
            pivots[at] = p if s == 0 else jnp.where(sub == s, p, pivots[at])
            inverted = 1.0 / p
            row_r, row_v = spread(r[at][s : s + 1, :]), spread(v[at][s : s + 1, :])
            heads = [spread(cols[j][at][s : s + 1, :]) for j in range(i + 1, width)]
            for k in range(at, per):
                if k == at and s == 7:
                    continue
                m = cols[i][k] * inverted
                if k == at:
                    m = jnp.where(sub > s, m, 0.0)
                r[k] = r[k] - m * row_r
                v[k] = v[k] - m * row_v
                for j in range(i + 1, width):
                    cols[j][k] = cols[j][k] - m * heads[j - i - 1]
        for k in range(per):
            s = lax.rsqrt(pivots[k])
            s = s * (1.5 - 0.5 * pivots[k] * s * s)
            upper.append(jnp.where(lane >= sub + 8 * (g + k), r[k] * s, 0.0))
            inverse.append(v[k] * s)
        if g + per < groups:
            right = jnp.concatenate(upper[g:], axis=0)
            both = jnp.concatenate([right, jnp.concatenate(inverse[g:], axis=0)], axis=1)
            t = dot_tn(stacked(right, True), stacked(both, False))
            for h in range(g + per, groups):
                a[h] = a[h] - t[8 * h : 8 * h + 8, :BLOCK]
                w[h] = w[h] - t[8 * h : 8 * h + 8, BLOCK:]
    return jnp.concatenate(upper, axis=0), jnp.concatenate(inverse, axis=0)


def factor_tile(m, v_ref, l_ref):
    b = BLOCK
    u0, v0 = factor_block([m[8 * g : 8 * g + 8, 0:b] for g in range(b // 8)])
    u01 = jnp.dot(v0, m[0:b, b:], precision=HIGHEST, preferred_element_type=F32)
    m[b:, b:] = m[b:, b:] - dot_tn(u01, u01, HIGHEST)
    u1, v1 = factor_block([m[b + 8 * g : b + 8 * g + 8, b:] for g in range(b // 8)])
    w = dot_tn(u01, v0, HIGHEST)
    zeros = jnp.zeros((b, b), F32)
    v_ref[0:b, 0:b] = v0
    v_ref[0:b, b:] = zeros
    v_ref[b:, 0:b] = -jnp.dot(v1, w, precision=HIGHEST, preferred_element_type=F32)
    v_ref[b:, b:] = v1
    l_ref[0:b, 0:b] = u0.T
    l_ref[0:b, b:] = zeros
    l_ref[b:, 0:b] = u01.T
    l_ref[b:, b:] = u1.T


def first_kernel(d00, v00, l00, m):
    m[...] = d00[...]
    factor_tile(m, v00, l00)


def second_kernel(d10, d11, v00, v10, v11, l11, m):
    u01 = lax.dot_general(
        v00[...], d10[...], (((1,), (1,)), ((), ())), precision=HIGHEST, preferred_element_type=F32
    )
    m[...] = d11[...] - dot_tn(u01, u01, HIGHEST)
    factor_tile(m, v11, l11)
    w = dot_tn(u01, v00[...], HIGHEST)
    v10[...] = -jnp.dot(v11[...], w, precision=HIGHEST, preferred_element_type=F32)


def factor_call(kernel, sizes, args, scratch=()):
    vmem = pl.BlockSpec(memory_space=pltpu.VMEM)
    return pl.pallas_call(
        kernel,
        out_shape=[jax.ShapeDtypeStruct((n, n), F32) for n in sizes],
        in_specs=[vmem] * len(args),
        out_specs=[vmem] * len(sizes),
        scratch_shapes=list(scratch),
        compiler_params=pltpu.CompilerParams(vmem_limit_bytes=8 * 2**20),
        cost_estimate=pl.CostEstimate(
            flops=6 * 10**9, bytes_accessed=2**20, transcendentals=0
        ),
    )(*args)


def halves(x):
    hi = x.astype(BF16)
    return hi, (x - hi.astype(F32)).astype(BF16)


def dot3(a, b, dims):
    ah, al = a
    bh, bl = b
    d = (dims, ((), ()))
    out = lax.dot_general(ah, bh, d, preferred_element_type=F32)
    out = out + lax.dot_general(ah, bl, d, preferred_element_type=F32)
    return out + lax.dot_general(al, bh, d, preferred_element_type=F32)


NT = ((1,), (1,))
NN = ((1,), (0,))
CHUNK = 512


def update_kernel(shifts, solve, place, mat, v00_ref, v10_ref, v11_ref, l00, l11, *refs):
    if solve:
        mine, other, *pieces = refs[: 2 + len(shifts)]
        out, lph, lpl = refs[2 + len(shifts) : 5 + len(shifts)]
    else:
        lph, lpl, *pieces = refs[: 2 + len(shifts)]
        out = refs[3 + len(shifts)]
    m, o, lqh, lql, in_sem, out_sem = refs[-6:]
    row, col = place[0], place[1]
    zero_core = col % 2 == 0
    major = jnp.where(zero_core, row % 4, row // 4)
    rows = mat.shape[0]
    count = len(shifts)
    sources = [lax.rem(major + 4 - k, 4) for k in shifts]
    spans = [pl.ds(pl.multiple_of(i * CHUNK, CHUNK), CHUNK) for i in sources]
    loads = []
    for k in range(count):
        copy = pltpu.make_async_copy(mat.at[:, spans[k]], m.at[k], in_sem.at[k])
        copy.start()
        loads.append(copy)

    v00 = halves(v00_ref[...])
    v10 = halves(v10_ref[...])
    v11 = halves(v11_ref[...])

    for i in range(rows // TILE if solve else 0):
        at = pl.ds(i * TILE, TILE)
        a_mine, a_other = mine[at, :], other[at, :]
        a0 = halves(jnp.where(zero_core, a_mine, a_other))
        a1 = halves(jnp.where(zero_core, a_other, a_mine))
        lph[at, 0:TILE], lpl[at, 0:TILE] = halves(dot3(a0, v00, NT))
        lph[at, TILE:], lpl[at, TILE:] = halves(dot3(a0, v10, NT) + dot3(a1, v11, NT))

    stores = []
    for k in range(count):
        piece = pieces[k]
        slot = k
        d0 = halves(piece[0])
        d1 = halves(piece[1])
        lqh[0:TILE, :], lql[0:TILE, :] = halves(dot3(v00, d0, NN))
        lqh[TILE:, :], lql[TILE:, :] = halves(dot3(v10, d0, NN) + dot3(v11, d1, NN))
        loads[k].wait()
        for i in range(rows // TILE):
            r = pl.ds(i * TILE, TILE)
            o[slot, r, :] = m[k, r, :] - dot3(
                (lph[r, :], lpl[r, :]), (lqh[...], lql[...]), NN
            )

        @pl.when(row < 2)
        def _():
            o[slot, 0:TILE, :] = jnp.zeros((TILE, CHUNK), F32)

        @pl.when((sources[k] == 0) & (col < 2))
        def _():
            for j in range(2):
                side = pl.ds(j * TILE, TILE)

                @pl.when(col == j)
                def _():
                    o[slot, :, 0:TILE] = lph[:, side].astype(F32) + lpl[:, side].astype(F32)

            @pl.when((row == 0) & (col == 0))
            def _():
                o[slot, 0:TILE, 0:TILE] = l00[...]

            @pl.when((row == 0) & (col == 1))
            def _():
                o[slot, 0:TILE, 0:TILE] = jnp.zeros((TILE, TILE), F32)

            @pl.when((row == 1) & (col == 1))
            def _():
                o[slot, 0:TILE, 0:TILE] = l11[...]

        copy = pltpu.make_async_copy(o.at[slot], out.at[:, spans[k]], out_sem.at[k])
        copy.start()
        stores.append(copy)
    for copy in stores:
        copy.wait()


def update_call(shifts, place, mat, factors, pieces, rows_in=None, solved=None, out=None):
    rows, cols = mat.shape
    n = 2 * TILE
    solve = rows_in is not None
    count = len(shifts)
    hbm = pl.BlockSpec(memory_space=pl.ANY)
    vmem = pl.BlockSpec(memory_space=pltpu.VMEM)
    smem = pl.BlockSpec(memory_space=pltpu.SMEM)
    whole = jax.ShapeDtypeStruct((rows, cols), F32)
    half_rows = jax.ShapeDtypeStruct((rows, n), BF16)
    args = (place, mat, *factors, *(rows_in if solve else solved), *pieces)
    in_specs = [smem, hbm] + [vmem] * (len(args) - 2)
    if not solve:
        args += (out,)
        in_specs.append(hbm)
    return pl.pallas_call(
        functools.partial(update_kernel, shifts, solve),
        out_shape=[whole, half_rows, half_rows] if solve else whole,
        in_specs=in_specs,
        out_specs=[hbm, vmem, vmem] if solve else hbm,
        scratch_shapes=[
            pltpu.VMEM((count, rows, CHUNK), F32),
            pltpu.VMEM((count, rows, CHUNK), F32),
            pltpu.VMEM((n, CHUNK), BF16),
            pltpu.VMEM((n, CHUNK), BF16),
            pltpu.SemaphoreType.DMA((count,)),
            pltpu.SemaphoreType.DMA((count,)),
        ],
        input_output_aliases={} if solve else {len(args) - 1: 0},
        compiler_params=pltpu.CompilerParams(vmem_limit_bytes=26 * 2**20),
        cost_estimate=pl.CostEstimate(
            flops=3 * 10**9 * count, bytes_accessed=6 * 2**20 * count, transcendentals=0
        ),
    )(*args)


def along(axis, table, core, fixed=None):
    fixed = fixed or {}
    moves = []
    spans = [fixed.get(k, R4) for k in "yxz"]
    at = "yxz".index(axis)
    for a, b in table:
        spans[at] = (a,)
        for y in spans[0]:
            for x in spans[1]:
                for z in spans[2]:
                    dst = [y, x, z, core]
                    dst[at] = b
                    moves.append(((y, x, z, core), tuple(dst)))
    return moves


def swap_cores(value):
    return send(value, [((y, x, z, c), (y, x, z, 1 - c)) for y in R4 for x in R4 for z in R4 for c in R2])


def tied(values, *after):
    return lax.optimization_barrier((values, after))[0]


def shards(matrix):
    row = lax.axis_index("row")
    col = lax.axis_index("col")
    y, x = row // 4, row % 4
    z, c = col // 2, col % 2
    place = {"y": y, "x": x, "z": z, "c": c}
    zero_core = c == 0
    half = TILE // 2

    def pick(a, b):
        return jnp.where(zero_core, a, b)

    def columns(i):
        return lax.dynamic_slice(matrix, (0, i * CHUNK), (TILE, CHUNK))

    def among(index, *values):
        out = values[-1]
        for i in reversed(range(len(values) - 1)):
            out = jnp.where(index == i, values[i], out)
        return out

    tile = matrix[0:TILE, 0:TILE]
    strip = matrix[:, 0:TILE]

    first_stop = pick(1, 3)
    turns = (
        along("z", [(0, 1)], 0) + along("z", [(0, 3)], 1),
        along("z", [(0, 3), (1, 2)], 0) + along("z", [(0, 1), (3, 2)], 1),
    )
    spots = [((y0, x0, 0, c0), (y0, x0, k, c0)) for k in (2, 1, 3) for y0, x0, c0 in ((0, 0, 0), (0, 1, 0), (0, 1, 1))]
    t2, t1, t3 = [send(tile, spots[i : i + 3]) for i in (0, 3, 6)]
    tile = among(z, tile, t1, t2, t3)

    edge = {"y": (0,)}
    sides = {"x": (0, 1)}
    hops = (
        along("x", [(0, 1), (1, 0)], 0, edge) + along("y", [(0, 1)], 1, sides),
        along("x", [(0, 3), (1, 2)], 0, edge) + along("y", [(0, 2)], 1, sides),
        along("x", [(0, 2), (1, 3)], 0, edge) + along("y", [(0, 3)], 1, sides),
    )
    q0, *rest = [columns(i) for i in (
        pick(jnp.minimum(x, 1), 0),
        pick(1 - jnp.minimum(x, 1), 1),
        pick(jnp.where(x == 0, 3, 2), 2),
        pick(jnp.where(x == 0, 2, 3), 3),
    )]
    came = [send(q, moves) for q, moves in zip(rest, hops)]
    tiles = [send(tile, moves) for moves in hops]
    q0 = jnp.concatenate([q0, tile], axis=1)
    a1, a2, a3 = [jnp.concatenate(both, axis=1) for both in zip(came, tiles)]
    top = among(pick(x, y), q0, a1, pick(a3, a2), pick(a2, a3))
    low = among(pick(x, y), pick(a1, q0), pick(q0, a1), a2, a3)
    b1 = send(top, along("y", [(0, 1)], 0) + along("x", [(0, 1), (1, 0)], 1))
    b2 = send(low, along("y", [(0, 3)], 0) + along("x", [(0, 3), (1, 2)], 1))
    b3 = send(
        pick(jnp.where(y == 0, top, b1), b2),
        along("y", [(0, 3), (1, 2)], 0) + along("x", [(3, 2), (2, 3)], 1),
    )
    b4 = send(jnp.where(y == 0, low, b2), along("y", [(0, 1), (3, 2)], 0))
    first = among(pick(y, x), top, b1, b3, pick(b3, b2))
    second = among(pick(y, x), pick(low, b1), pick(b4, low), pick(b4, b2), pick(b2, b3))
    diagonal = jnp.stack([first[:, CHUNK:], second[:, CHUNK:]])
    both = jnp.stack([first[:, :CHUNK], second[:, :CHUNK]])
    diagonal_rest = swap_cores(diagonal)
    pieces = [both]
    for k in (1, 2, 3):
        turn = [(i, (i + k) % 4) for i in R4]
        pieces.append(send(both, along("x", turn, 0) + along("y", turn, 1)))
    d00 = pick(diagonal[0], diagonal_rest[0])
    d10 = pick(diagonal[1], diagonal_rest[1])
    d11 = pick(diagonal_rest[1], diagonal[1])
    scratch = [pltpu.VMEM((TILE, TILE), F32)]
    v00, l00 = factor_call(first_kernel, [TILE] * 2, (d00,), scratch)
    v10, v11, l11 = factor_call(second_kernel, [TILE] * 3, (d10, d11, v00), scratch)

    r1 = send(tied(strip, t2), turns[0])
    strip = jnp.where(z == first_stop, r1, strip)
    r2 = send(strip, turns[1])
    mine = jnp.where((z == 0) | (z == first_stop), strip, r2)
    other = swap_cores(mine)

    where = jnp.stack([row, col]).astype(jnp.int32)
    factors = (v00, v10, v11, l00, l11)
    out, high, rest = update_call((0,), where, matrix, factors, pieces[:1], rows_in=(mine, other))
    return update_call(
        (1, 3, 2), where, matrix, factors, (pieces[1], pieces[3], pieces[2]), solved=(high, rest), out=out
    )


def solution(mesh):
    return jax.shard_map(
        shards,
        mesh=mesh,
        in_specs=(P("row", "col"),),
        out_specs=P("row", "col"),
        check_vma=False,
    )
```

time: 129 us -> 114 us (0.88)
  the two profiles are of different devices: /device:TPU:101 before, /device:TPU:81 now
where the time goes in v3:
time: 114 us; the launch traced here: 113 us
  starting transfers between devices  37.9 us (33%)
  Pallas kernels  34.2 us (30%)
  waiting for transfers between devices  26.4 us (23%)
  local copies, waits for them, and re-layouts  7.79 us (7%)
  other arithmetic  6.23 us (5%)
    ppermute x20, starting transfers between devices, send(): return lax.ppermute(value, ('row', 'col'), pairs(moves))  37.9 us
    ppermute x20, waiting for transfers between devices, send(): return lax.ppermute(value, ('row', 'col'), pairs(moves))  26.4 us
    pallas_call x2, Pallas kernels, factor_call(): pl.pallas_call(kernel, out_shape=[jax.ShapeDtypeStruct((n, n), F32) for n...  17.2 us
    pallas_call x2, Pallas kernels, update_call(): pl.pallas_call(functools.partial(update_kernel, shifts, solve), out_shape...  17 us
    select_n x3, other arithmetic, among(): out = jnp.where(index == i, values[i], out)  3.13 us
    dynamic_slice x1, local copies, waits for them, and re-layouts, columns(): return lax.dynamic_slice(matrix, (0, i * CHUNK), (TILE, CHUNK))  2.58 us
  transfers between devices with their start and end apart: 20, of which 5 were waited for; matrix products, arithmetic and copies ran while one was open for 11% of the time, Pallas kernels for 21%

profile of v3, /device:TPU:81, one launch (start us, length us, event | category | flops | bytes accessed | tf_op | source)
XLA Modules:
  0.0 113.1 jit_solution(12468067858264076776)
XLA Ops:
  0.0 1.0 slice.25
  1.7 1.4 %collective-permute-start.1 = (f32[256,256]{1,0:T(8,128)S(1)}, f32[256,256]{1,0:T(8,128)}, u32[]{:S(2)}, u32[]{:S(2)}) collective-permute-start(f32[256,256]{1,0:T(8,128)S(1)} %slice.25), channel_id=1, source_target_pairs={{0,4},{8,12},{9,13}} | collective-permute-start | bytes 786440 | tf_op jit(solution)/shard_map/ppermute | solution.py:30
  3.0 1.4 %collective-permute-start = (f32[256,256]{1,0:T(8,128)S(1)}, f32[256,256]{1,0:T(8,128)}, u32[]{:S(2)}, u32[]{:S(2)}) collective-permute-start(f32[256,256]{1,0:T(8,128)S(1)} %slice.25), channel_id=1, source_target_pairs={{0,2},{8,10},{9,11}} | collective-permute-start | bytes 786440 | tf_op jit(solution)/shard_map/ppermute | solution.py:30
  4.4 2.6 %constant_dynamic-slice_fusion.3 = (f32[256,512]{1,0:T(8,128)S(1)}, f32[256,512]{1,0:T(8,128)}, f32[256,512]{1,0:T(8,128)S(1)}, f32[256,512]{1,0:T(8,128)S(1)}) fusion(f32[1024,2048]{1,0:T(8,128)} %mat.3, s32[]{:T(128)S(6)} %select_n.233, s32[]{:T(128)S(6)} %select_n.251, s32[]{:T(128)S(6)} %select_n.248, s32[]{:T(128)S(6)} %select_n.243), kind=kLoop, calls=%fused_computation.32 | loop fusion | bytes 4194320 | tf_op jit(solution)/shard_map/dynamic_slice | solution.py:320
  7.0 1.3 %collective-permute-start.7 = (f32[256,512]{1,0:T(8,128)}, f32[256,512]{1,0:T(8,128)S(1)}, u32[]{:S(2)}, u32[]{:S(2)}) collective-permute-start(f32[256,512]{1,0:T(8,128)} %get-tuple-element.24), channel_id=1, source_target_pairs={{0,24},{2,26},{4,28},{6,30},{8,16},{10,18},{12,20},{14,22},{1,65},... | collective-permute-start | bytes 1572872 | tf_op jit(solution)/shard_map/ppermute | solution.py:30
  8.2 0.7 collective-permute-start.5
  9.0 0.7 copy-done
  9.7 0.7 collective-permute-start.3
  10.4 1.1 select_select_fusion.5
  11.5 1.3 %collective-permute-start.8 = (f32[256,256]{1,0:T(8,128)S(1)}, f32[256,256]{1,0:T(8,128)}, u32[]{:S(2)}, u32[]{:S(2)}) collective-permute-start(f32[256,256]{1,0:T(8,128)S(1)} %select_select_fusion.5), channel_id=1, source_target_pairs={{0,24},{2,26},{4,28},{6,30},{8,16},{10,18},{12,20},{14,22},{1,65},... | collective-permute-start | bytes 786440 | tf_op jit(solution)/shard_map/ppermute | solution.py:30
  13.5 5.1 %collective-permute-done.7 = f32[256,512]{1,0:T(8,128)S(1)} collective-permute-done((f32[256,512]{1,0:T(8,128)}, f32[256,512]{1,0:T(8,128)S(1)}, u32[]{:S(2)}, u32[]{:S(2)}) %collective-permute-start.7) | collective-permute-done | bytes 524320 | tf_op jit(solution)/shard_map/ppermute | solution.py:30
  19.4 7.8 %collective-permute-done.8 = f32[256,256]{1,0:T(8,128)} collective-permute-done((f32[256,256]{1,0:T(8,128)S(1)}, f32[256,256]{1,0:T(8,128)}, u32[]{:S(2)}, u32[]{:S(2)}) %collective-permute-start.8) | collective-permute-done | bytes 262176 | tf_op jit(solution)/shard_map/ppermute | solution.py:30
  27.1 1.0 constant_dynamic-update-slice_fusion.4
  28.6 3.1 %collective-permute-start.9 = (f32[256,768]{1,0:T(8,128)S(1)}, f32[256,768]{1,0:T(8,128)S(1)}, u32[]{:S(2)}, u32[]{:S(2)}) collective-permute-start(f32[256,768]{1,0:T(8,128)S(1)} %get-tuple-element.27), channel_id=1, source_target_pairs={{0,32},{2,34},{4,36},{6,38},{8,40},{10,42},{12,44},{14,46},{16,48}... | collective-permute-start | bytes 2359304 | tf_op jit(solution)/shard_map/ppermute | solution.py:30
  31.7 1.3 %collective-permute-start.10 = (f32[256,768]{1,0:T(8,128)S(1)}, f32[256,768]{1,0:T(8,128)S(1)}, u32[]{:S(2)}, u32[]{:S(2)}) collective-permute-start(f32[256,768]{1,0:T(8,128)S(1)} %get-tuple-element.28), channel_id=1, source_target_pairs={{0,96},{2,98},{4,100},{6,102},{8,104},{10,106},{12,108},{14,110},{... | collective-permute-start | bytes 2359304 | tf_op jit(solution)/shard_map/ppermute | solution.py:30
  33.0 2.3 %slice.30 = f32[1024,256]{1,0:T(8,128)} slice(f32[1024,2048]{1,0:T(8,128)} %mat.3), slice={[0:1024], [0:256]} | slice | bytes 2097152 | tf_op jit(solution)/shard_map/slice | solution.py:329
  35.3 1.6 %collective-permute-start.14 = (f32[1024,256]{1,0:T(8,128)}, f32[1024,256]{1,0:T(8,128)}, u32[]{:S(2)}, u32[]{:S(2)}) collective-permute-start(f32[1024,256]{1,0:T(8,128)} %slice.30), channel_id=1, source_target_pairs={{0,2},{8,10},{16,18},{24,26},{32,34},{40,42},{48,50},{56,58},{64,6... | collective-permute-start | bytes 3145736 | tf_op jit(solution)/shard_map/ppermute | solution.py:30
  36.9 4.6 %collective-permute-done.9 = f32[256,768]{1,0:T(8,128)S(1)} collective-permute-done((f32[256,768]{1,0:T(8,128)S(1)}, f32[256,768]{1,0:T(8,128)S(1)}, u32[]{:S(2)}, u32[]{:S(2)}) %collective-permute-start.9) | collective-permute-done | bytes 786464 | tf_op jit(solution)/shard_map/ppermute | solution.py:30
  41.9 1.4 %broadcast_select_fusion.2 = (f32[256,768]{1,0:T(8,128)}, f32[256,768]{1,0:T(8,128)}) fusion(f32[256,768]{1,0:T(8,128)S(1)} %get-tuple-element.28, f32[256,768]{1,0:T(8,128)S(1)} %collective-permute-done.10, pred[]{:T(512)S(6)} %eq.63, f32[256,768]{1,0:T(8,128)S(1)} %get-tuple-element.27, f32[256,768]{1,0:T(8,128)S(1)} %collective-permute-done.9, pred[]{:T(512)S(6)} %eq.52), kind=kLoop, calls=%fused_computation.14 | loop fusion | flops 589824 | bytes 4718594 | tf_op jit(solution)/shard_map/jit(_where)/select_n | solution.py:365
  43.3 1.5 %collective-permute-start.12 = (f32[256,768]{1,0:T(8,128)}, f32[256,768]{1,0:T(8,128)}, u32[]{:S(2)}, u32[]{:S(2)}) collective-permute-start(f32[256,768]{1,0:T(8,128)} %get-tuple-element.33), channel_id=1, source_target_pairs={{0,32},{2,34},{4,36},{6,38},{8,40},{10,42},{12,44},{14,46},{16,48}... | collective-permute-start | bytes 2359304 | tf_op jit(solution)/shard_map/ppermute | solution.py:30
  44.8 1.5 %collective-permute-start.11 = (f32[256,768]{1,0:T(8,128)}, f32[256,768]{1,0:T(8,128)}, u32[]{:S(2)}, u32[]{:S(2)}) collective-permute-start(f32[256,768]{1,0:T(8,128)} %get-tuple-element.34), channel_id=1, source_target_pairs={{0,96},{2,98},{4,100},{6,102},{8,104},{10,106},{12,108},{14,110},{... | collective-permute-start | bytes 2359304 | tf_op jit(solution)/shard_map/ppermute | solution.py:30
  46.4 1.4 %broadcast_select_fusion = f32[1024,256]{1,0:T(8,128)S(1)} fusion(f32[1024,256]{1,0:T(8,128)} %collective-permute-done.14, pred[]{:T(512)S(6)} %eq.64, f32[1024,2048]{1,0:T(8,128)} %mat.3), kind=kLoop, calls=%fused_computation.12 | loop fusion | flops 262144 | bytes 3145729 | tf_op jit(solution)/shard_map/jit(_where)/select_n | solution.py:383
  47.8 1.3 %collective-permute-start.15 = (f32[1024,256]{1,0:T(8,128)S(1)}, f32[1024,256]{1,0:T(8,128)S(1)}, u32[]{:S(2)}, u32[]{:S(2)}) collective-permute-start(f32[1024,256]{1,0:T(8,128)S(1)} %broadcast_select_fusion), channel_id=1, source_target_pairs={{0,6},{8,14},{16,22},{24,30},{32,38},{40,46},{48,54},{56,62},{64,7... | collective-permute-start | bytes 3145736 | tf_op jit(solution)/shard_map/ppermute | solution.py:30
  49.1 1.7 %fusion.1 = (f32[256,768]{1,0:T(8,128)S(1)}, f32[256,768]{1,0:T(8,128)S(1)}) fusion(f32[256,768]{1,0:T(8,128)S(1)} %get-tuple-element.27, f32[256,768]{1,0:T(8,128)S(1)} %collective-permute-done.9, f32[256,768]{1,0:T(8,128)} %collective-permute-done.11, f32[256,768]{1,0:T(8,128)S(1)} %collective-permute-done.10, pred[]{:T(512)S(6)} %eq.62, pred[]{:T(512)S(6)} %eq.61, ...), kind=kLoop, calls=%fused_computation.3 | loop fusion | flops 2162688 | bytes 6291460 | tf_op jit(solution)/shard_map/jit(_where)/select_n | solution.py:325
  50.9 11.5 %collective-permute-start.13 = (f32[2,256,256]{2,1,0:T(8,128)S(1)}, f32[2,256,256]{2,1,0:T(8,128)S(1)}, u32[]{:S(2)}, u32[]{:S(2)}) collective-permute-start(f32[2,256,256]{2,1,0:T(8,128)S(1)} %pad_maximum_fusion.2), channel_id=1, source_target_pairs={{0,1},{1,0},{2,3},{3,2},{4,5},{5,4},{6,7},{7,6},{8,9},{9,8},{10,11... | collective-permute-start | bytes 1572872 | tf_op jit(solution)/shard_map/ppermute | solution.py:30
  62.6 4.2 %collective-permute-start.19 = (f32[2,256,512]{2,1,0:T(8,128)S(1)}, f32[2,256,512]{2,1,0:T(8,128)S(1)}, u32[]{:S(2)}, u32[]{:S(2)}) collective-permute-start(f32[2,256,512]{2,1,0:T(8,128)S(1)} %pad_maximum_fusion.refs_2_), channel_id=1, source_target_pairs={{0,16},{2,18},{4,20},{6,22},{32,48},{34,50},{36,52},{38,54},{64,80... | collective-permute-start | bytes 3145736 | tf_op jit(solution)/shard_map/ppermute | solution.py:30
  66.8 2.8 %collective-permute-start.18 = (f32[2,256,512]{2,1,0:T(8,128)S(1)}, f32[2,256,512]{2,1,0:T(8,128)S(1)}, u32[]{:S(2)}, u32[]{:S(2)}) collective-permute-start(f32[2,256,512]{2,1,0:T(8,128)S(1)} %pad_maximum_fusion.refs_2_), channel_id=1, source_target_pairs={{0,24},{2,26},{4,28},{6,30},{32,56},{34,58},{36,60},{38,62},{64,88... | collective-permute-start | bytes 3145736 | tf_op jit(solution)/shard_map/ppermute | solution.py:30
  69.6 8.5 %collective-permute-done.15 = f32[1024,256]{1,0:T(8,128)S(1)} collective-permute-done((f32[1024,256]{1,0:T(8,128)S(1)}, f32[1024,256]{1,0:T(8,128)S(1)}, u32[]{:S(2)}, u32[]{:S(2)}) %collective-permute-start.15) | collective-permute-done | bytes 1048608 | tf_op jit(solution)/shard_map/ppermute | solution.py:30
  78.6 7.8 %shard_map.17 = (f32[256,256]{1,0:T(8,128)S(1)}, f32[256,256]{1,0:T(8,128)S(1)}) custom-call(f32[256,256]{1,0:T(8,128)S(1)} %get-tuple-element.35.d00), custom_call_target="tpu_custom_call" | custom-call | flops 6000000000 | bytes 1048576 | tf_op jit(solution)/shard_map/pallas_call | solution.py:135
  86.5 9.4 %shard_map.18 = (f32[256,256]{1,0:T(8,128)S(1)}, f32[256,256]{1,0:T(8,128)S(1)}, f32[256,256]{1,0:T(8,128)S(1)}) custom-call(f32[256,256]{1,0:T(8,128)S(1)} %get-tuple-element.32.d10, f32[256,256]{1,0:T(8,128)S(1)} %get-tuple-element.31.d11, f32[256,256]{1,0:T(8,128)S(1)} %get-tuple-element.14.v00.v00_ref), custom_call_target="tpu_custom_call" | custom-call | flops 6000000000 | bytes 1048576 | tf_op jit(solution)/shard_map/pallas_call | solution.py:135
  95.9 6.3 %shard_map.19 = (f32[1024,2048]{1,0:T(8,128)}, bf16[1024,512]{1,0:T(8,128)(2,1)S(1)}, bf16[1024,512]{1,0:T(8,128)(2,1)S(1)}) custom-call(s32[2]{0:T(128)S(1)} %pad_add_fusion.place, f32[1024,2048]{1,0:T(8,128)S(1)} %bitcast.21, f32[256,256]{1,0:T(8,128)S(1)} %get-tuple-element.14.v00.v00_ref, f32[256,256]{1,0:T(8,128)S(1)} %get-tuple-element.15.v10_ref, ...), custom_call_target="tpu_custom_call" | custom-call | flops 3000000000 | bytes 6291456 | tf_op jit(solution)/shard_map/pallas_call | solution.py:262
  102.3 10.6 %shard_map.20 = f32[1024,2048]{1,0:T(8,128)} custom-call(s32[2]{0:T(128)S(1)} %pad_add_fusion.place, f32[1024,2048]{1,0:T(8,128)S(1)} %bitcast.21, f32[256,256]{1,0:T(8,128)S(1)} %get-tuple-element.14.v00.v00_ref, f32[256,256]{1,0:T(8,128)S(1)} %get-tuple-element.15.v10_ref, ...), custom_call_target="tpu_custom_call", output_to_operand_aliasing={{}: (12, {})} | custom-call | flops 8999999488 | bytes 18874368 | tf_op jit(solution)/shard_map/pallas_call | solution.py:262
  (40 shorter events, 3.7 us)
Async XLA Ops:
  1.0 8.0 %collective-permute-start.2 = (f32[256,256]{1,0:T(8,128)S(1)}, f32[256,256]{1,0:T(8,128)S(1)}, u32[]{:S(2)}, u32[]{:S(2)}) collective-permute-start(f32[256,256]{1,0:T(8,128)S(1)} %slice.25), channel_id=1, source_target_pairs={{0,6},{8,14},{9,15}} | collective-permute-start | bytes 786440 | tf_op jit(solution)/shard_map/ppermute | solution.py:30
  1.7 8.7 %collective-permute-start.1 = (f32[256,256]{1,0:T(8,128)S(1)}, f32[256,256]{1,0:T(8,128)}, u32[]{:S(2)}, u32[]{:S(2)}) collective-permute-start(f32[256,256]{1,0:T(8,128)S(1)} %slice.25), channel_id=1, source_target_pairs={{0,4},{8,12},{9,13}} | collective-permute-start | bytes 786440 | tf_op jit(solution)/shard_map/ppermute | solution.py:30
  3.0 7.4 %collective-permute-start = (f32[256,256]{1,0:T(8,128)S(1)}, f32[256,256]{1,0:T(8,128)}, u32[]{:S(2)}, u32[]{:S(2)}) collective-permute-start(f32[256,256]{1,0:T(8,128)S(1)} %slice.25), channel_id=1, source_target_pairs={{0,2},{8,10},{9,11}} | collective-permute-start | bytes 786440 | tf_op jit(solution)/shard_map/ppermute | solution.py:30
  7.0 11.6 %collective-permute-start.7 = (f32[256,512]{1,0:T(8,128)}, f32[256,512]{1,0:T(8,128)S(1)}, u32[]{:S(2)}, u32[]{:S(2)}) collective-permute-start(f32[256,512]{1,0:T(8,128)} %get-tuple-element.24), channel_id=1, source_target_pairs={{0,24},{2,26},{4,28},{6,30},{8,16},{10,18},{12,20},{14,22},{1,65},... | collective-permute-start | bytes 1572872 | tf_op jit(solution)/shard_map/ppermute | solution.py:30
  8.2 11.1 %collective-permute-start.5 = (f32[256,512]{1,0:T(8,128)S(1)}, f32[256,512]{1,0:T(8,128)S(1)}, u32[]{:S(2)}, u32[]{:S(2)}) collective-permute-start(f32[256,512]{1,0:T(8,128)S(1)} %get-tuple-element.25), channel_id=1, source_target_pairs={{0,16},{2,18},{4,20},{6,22},{8,24},{10,26},{12,28},{14,30},{1,97},... | collective-permute-start | bytes 1572872 | tf_op jit(solution)/shard_map/ppermute | solution.py:30
  9.0 0.7 copy-start
  9.7 18.4 %collective-permute-start.3 = (f32[256,512]{1,0:T(8,128)S(1)}, f32[256,512]{1,0:T(8,128)S(1)}, u32[]{:S(2)}, u32[]{:S(2)}) collective-permute-start(f32[256,512]{1,0:T(8,128)S(1)} %get-tuple-element.26), channel_id=1, source_target_pairs={{0,8},{2,10},{4,12},{6,14},{8,0},{10,2},{12,4},{14,6},{1,33},{3,35... | collective-permute-start | bytes 1572872 | tf_op jit(solution)/shard_map/ppermute | solution.py:30
  11.5 15.6 %collective-permute-start.8 = (f32[256,256]{1,0:T(8,128)S(1)}, f32[256,256]{1,0:T(8,128)}, u32[]{:S(2)}, u32[]{:S(2)}) collective-permute-start(f32[256,256]{1,0:T(8,128)S(1)} %select_select_fusion.5), channel_id=1, source_target_pairs={{0,24},{2,26},{4,28},{6,30},{8,16},{10,18},{12,20},{14,22},{1,65},... | collective-permute-start | bytes 786440 | tf_op jit(solution)/shard_map/ppermute | solution.py:30
  12.8 15.3 %collective-permute-start.6 = (f32[256,256]{1,0:T(8,128)S(1)}, f32[256,256]{1,0:T(8,128)S(1)}, u32[]{:S(2)}, u32[]{:S(2)}) collective-permute-start(f32[256,256]{1,0:T(8,128)S(1)} %select_select_fusion.5), channel_id=1, source_target_pairs={{0,16},{2,18},{4,20},{6,22},{8,24},{10,26},{12,28},{14,30},{1,97},... | collective-permute-start | bytes 786440 | tf_op jit(solution)/shard_map/ppermute | solution.py:30
  18.6 9.6 %collective-permute-start.4 = (f32[256,256]{1,0:T(8,128)S(1)}, f32[256,256]{1,0:T(8,128)S(1)}, u32[]{:S(2)}, u32[]{:S(2)}) collective-permute-start(f32[256,256]{1,0:T(8,128)S(1)} %select_select_fusion.5), channel_id=1, source_target_pairs={{0,8},{2,10},{4,12},{6,14},{8,0},{10,2},{12,4},{14,6},{1,33},{3,35... | collective-permute-start | bytes 786440 | tf_op jit(solution)/shard_map/ppermute | solution.py:30
  28.6 13.0 %collective-permute-start.9 = (f32[256,768]{1,0:T(8,128)S(1)}, f32[256,768]{1,0:T(8,128)S(1)}, u32[]{:S(2)}, u32[]{:S(2)}) collective-permute-start(f32[256,768]{1,0:T(8,128)S(1)} %get-tuple-element.27), channel_id=1, source_target_pairs={{0,32},{2,34},{4,36},{6,38},{8,40},{10,42},{12,44},{14,46},{16,48}... | collective-permute-start | bytes 2359304 | tf_op jit(solution)/shard_map/ppermute | solution.py:30
  31.7 10.2 %collective-permute-start.10 = (f32[256,768]{1,0:T(8,128)S(1)}, f32[256,768]{1,0:T(8,128)S(1)}, u32[]{:S(2)}, u32[]{:S(2)}) collective-permute-start(f32[256,768]{1,0:T(8,128)S(1)} %get-tuple-element.28), channel_id=1, source_target_pairs={{0,96},{2,98},{4,100},{6,102},{8,104},{10,106},{12,108},{14,110},{... | collective-permute-start | bytes 2359304 | tf_op jit(solution)/shard_map/ppermute | solution.py:30
  35.3 11.1 %collective-permute-start.14 = (f32[1024,256]{1,0:T(8,128)}, f32[1024,256]{1,0:T(8,128)}, u32[]{:S(2)}, u32[]{:S(2)}) collective-permute-start(f32[1024,256]{1,0:T(8,128)} %slice.30), channel_id=1, source_target_pairs={{0,2},{8,10},{16,18},{24,26},{32,34},{40,42},{48,50},{56,58},{64,6... | collective-permute-start | bytes 3145736 | tf_op jit(solution)/shard_map/ppermute | solution.py:30
  43.3 5.8 %collective-permute-start.12 = (f32[256,768]{1,0:T(8,128)}, f32[256,768]{1,0:T(8,128)}, u32[]{:S(2)}, u32[]{:S(2)}) collective-permute-start(f32[256,768]{1,0:T(8,128)} %get-tuple-element.33), channel_id=1, source_target_pairs={{0,32},{2,34},{4,36},{6,38},{8,40},{10,42},{12,44},{14,46},{16,48}... | collective-permute-start | bytes 2359304 | tf_op jit(solution)/shard_map/ppermute | solution.py:30
  44.8 4.3 %collective-permute-start.11 = (f32[256,768]{1,0:T(8,128)}, f32[256,768]{1,0:T(8,128)}, u32[]{:S(2)}, u32[]{:S(2)}) collective-permute-start(f32[256,768]{1,0:T(8,128)} %get-tuple-element.34), channel_id=1, source_target_pairs={{0,96},{2,98},{4,100},{6,102},{8,104},{10,106},{12,108},{14,110},{... | collective-permute-start | bytes 2359304 | tf_op jit(solution)/shard_map/ppermute | solution.py:30
  47.8 30.3 %collective-permute-start.15 = (f32[1024,256]{1,0:T(8,128)S(1)}, f32[1024,256]{1,0:T(8,128)S(1)}, u32[]{:S(2)}, u32[]{:S(2)}) collective-permute-start(f32[1024,256]{1,0:T(8,128)S(1)} %broadcast_select_fusion), channel_id=1, source_target_pairs={{0,6},{8,14},{16,22},{24,30},{32,38},{40,46},{48,54},{56,62},{64,7... | collective-permute-start | bytes 3145736 | tf_op jit(solution)/shard_map/ppermute | solution.py:30
  50.9 27.7 %collective-permute-start.13 = (f32[2,256,256]{2,1,0:T(8,128)S(1)}, f32[2,256,256]{2,1,0:T(8,128)S(1)}, u32[]{:S(2)}, u32[]{:S(2)}) collective-permute-start(f32[2,256,256]{2,1,0:T(8,128)S(1)} %pad_maximum_fusion.2), channel_id=1, source_target_pairs={{0,1},{1,0},{2,3},{3,2},{4,5},{5,4},{6,7},{7,6},{8,9},{9,8},{10,11... | collective-permute-start | bytes 1572872 | tf_op jit(solution)/shard_map/ppermute | solution.py:30
  62.6 39.7 %collective-permute-start.19 = (f32[2,256,512]{2,1,0:T(8,128)S(1)}, f32[2,256,512]{2,1,0:T(8,128)S(1)}, u32[]{:S(2)}, u32[]{:S(2)}) collective-permute-start(f32[2,256,512]{2,1,0:T(8,128)S(1)} %pad_maximum_fusion.refs_2_), channel_id=1, source_target_pairs={{0,16},{2,18},{4,20},{6,22},{32,48},{34,50},{36,52},{38,54},{64,80... | collective-permute-start | bytes 3145736 | tf_op jit(solution)/shard_map/ppermute | solution.py:30
  66.8 35.5 %collective-permute-start.18 = (f32[2,256,512]{2,1,0:T(8,128)S(1)}, f32[2,256,512]{2,1,0:T(8,128)S(1)}, u32[]{:S(2)}, u32[]{:S(2)}) collective-permute-start(f32[2,256,512]{2,1,0:T(8,128)S(1)} %pad_maximum_fusion.refs_2_), channel_id=1, source_target_pairs={{0,24},{2,26},{4,28},{6,30},{32,56},{34,58},{36,60},{38,62},{64,88... | collective-permute-start | bytes 3145736 | tf_op jit(solution)/shard_map/ppermute | solution.py:30
  69.6 32.7 %collective-permute-start.17 = (f32[2,256,512]{2,1,0:T(8,128)S(1)}, f32[2,256,512]{2,1,0:T(8,128)S(1)}, u32[]{:S(2)}, u32[]{:S(2)}) collective-permute-start(f32[2,256,512]{2,1,0:T(8,128)S(1)} %pad_maximum_fusion.refs_2_), channel_id=1, source_target_pairs={{0,8},{2,10},{4,12},{6,14},{32,40},{34,42},{36,44},{38,46},{64,72}... | collective-permute-start | bytes 3145736 | tf_op jit(solution)/shard_map/ppermute | solution.py:30
  78.3 17.6 %collective-permute-start.16 = (f32[1024,256]{1,0:T(8,128)S(1)}, f32[1024,256]{1,0:T(8,128)S(1)}, u32[]{:S(2)}, u32[]{:S(2)}) collective-permute-start(f32[1024,256]{1,0:T(8,128)S(1)} %broadcast_select_fusion.1.refs_0_), channel_id=1, source_target_pairs={{0,1},{1,0},{2,3},{3,2},{4,5},{5,4},{6,7},{7,6},{8,9},{9,8},{10,11... | collective-permute-start | bytes 3145736 | tf_op jit(solution)/shard_map/ppermute | solution.py:30
  78.6 17.2 %slice-start = ((s8[8388608]{0:T(1024)(128)(4,1)}), s8[4194304]{0:T(1024)(128)(4,1)S(1)}, s32[]{:S(2)}) async-start(s8[8388608]{0:T(1024)(128)(4,1)} %bitcast.20), calls=%async_computation | async-start | bytes 8388608
  86.5 9.4 %slice-start.1 = ((s8[8388608]{0:T(1024)(128)(4,1)}), s8[4194304]{0:T(1024)(128)(4,1)S(1)}, s32[]{:S(2)}) async-start(s8[8388608]{0:T(1024)(128)(4,1)} %bitcast.20), calls=%async_computation.1 | async-start | bytes 8388608

commit v4 on v3

--- a/solution.py
+++ b/solution.py
@@ -334,6 +334,13 @@
         along("z", [(0, 3), (1, 2)], 0) + along("z", [(0, 1), (3, 2)], 1),
     )
     spots = [((y0, x0, 0, c0), (y0, x0, k, c0)) for k in (2, 1, 3) for y0, x0, c0 in ((0, 0, 0), (0, 1, 0), (0, 1, 1))]
+    q0, *rest = [columns(i) for i in (
+        pick(jnp.minimum(x, 1), 0),
+        pick(1 - jnp.minimum(x, 1), 1),
+        pick(jnp.where(x == 0, 3, 2), 2),
+        pick(jnp.where(x == 0, 2, 3), 3),
+    )]
+    tile = tied(tile, q0, *rest)
     t2, t1, t3 = [send(tile, spots[i : i + 3]) for i in (0, 3, 6)]
     tile = among(z, tile, t1, t2, t3)
 
@@ -344,12 +351,6 @@
         along("x", [(0, 3), (1, 2)], 0, edge) + along("y", [(0, 2)], 1, sides),
         along("x", [(0, 2), (1, 3)], 0, edge) + along("y", [(0, 3)], 1, sides),
     )
-    q0, *rest = [columns(i) for i in (
-        pick(jnp.minimum(x, 1), 0),
-        pick(1 - jnp.minimum(x, 1), 1),
-        pick(jnp.where(x == 0, 3, 2), 2),
-        pick(jnp.where(x == 0, 2, 3), 3),
-    )]
     came = [send(q, moves) for q, moves in zip(rest, hops)]
     tiles = [send(tile, moves) for moves in hops]
     q0 = jnp.concatenate([q0, tile], axis=1)
@@ -358,13 +359,12 @@
     low = among(pick(x, y), pick(a1, q0), pick(q0, a1), a2, a3)
     b1 = send(top, along("y", [(0, 1)], 0) + along("x", [(0, 1), (1, 0)], 1))
     b2 = send(low, along("y", [(0, 3)], 0) + along("x", [(0, 3), (1, 2)], 1))
-    b3 = send(
-        pick(jnp.where(y == 0, top, b1), b2),
-        along("y", [(0, 3), (1, 2)], 0) + along("x", [(3, 2), (2, 3)], 1),
-    )
-    b4 = send(jnp.where(y == 0, low, b2), along("y", [(0, 1), (3, 2)], 0))
-    first = among(pick(y, x), top, b1, b3, pick(b3, b2))
-    second = among(pick(y, x), pick(low, b1), pick(b4, low), pick(b4, b2), pick(b2, b3))
+    b3 = send(top, along("y", [(0, 3)], 0))
+    b4 = send(low, along("y", [(0, 1)], 0))
+    b5 = send(pick(b1, b2), along("y", [(1, 2)], 0) + along("x", [(3, 2), (2, 3)], 1))
+    b6 = send(b2, along("y", [(3, 2)], 0))
+    first = among(pick(y, x), top, b1, b5, pick(b3, b2))
+    second = among(pick(y, x), pick(low, b1), pick(b4, low), pick(b6, b2), pick(b2, b5))
     diagonal = jnp.stack([first[:, CHUNK:], second[:, CHUNK:]])
     both = jnp.stack([first[:, :CHUNK], second[:, :CHUNK]])
     diagonal_rest = swap_cores(diagonal)

time: 114 us -> 111 us (0.974)
  starting transfers between devices: 37.9 us -> 36.3 us
  local copies, waits for them, and re-layouts: 7.79 us -> 6.32 us
  waiting for transfers between devices: 26.4 us -> 27.8 us
    ppermute x20 -> x22, starting transfers between devices: 37.9 us -> 36.3 us  [send(): return lax.ppermute(value, ('row', 'col'), pairs(moves))]
    ppermute x20 -> x22, waiting for transfers between devices: 26.4 us -> 27.8 us  [send(): return lax.ppermute(value, ('row', 'col'), pairs(moves))]
    select_n x1 -> x0, other arithmetic: 1.35 us -> none  [shards(): b4 = send(jnp.where(y == 0, low, b2), along('y', [(0, 1), (3, 2)], 0))]
  transfers between devices with their start and end apart: 20 -> 22, of which waited for: 5 -> 5; matrix products, arithmetic and copies ran while one was open for 11% -> 7% of each run, Pallas kernels for 21% -> 21%
where the time goes in v4:
time: 111 us
  starting transfers between devices  36.3 us (33%)
  Pallas kernels  34 us (31%)
  waiting for transfers between devices  27.8 us (25%)
  local copies, waits for them, and re-layouts  6.32 us (6%)
  other arithmetic  5.63 us (5%)
    ppermute x22, starting transfers between devices, send(): return lax.ppermute(value, ('row', 'col'), pairs(moves))  36.3 us
    ppermute x22, waiting for transfers between devices, send(): return lax.ppermute(value, ('row', 'col'), pairs(moves))  27.8 us
    pallas_call x2, Pallas kernels, factor_call(): pl.pallas_call(kernel, out_shape=[jax.ShapeDtypeStruct((n, n), F32) for n...  17.2 us
    pallas_call x2, Pallas kernels, update_call(): pl.pallas_call(functools.partial(update_kernel, shifts, solve), out_shape...  16.8 us
    select_n x3, other arithmetic, among(): out = jnp.where(index == i, values[i], out)  2.9 us
    dynamic_slice x1, local copies, waits for them, and re-layouts, columns(): return lax.dynamic_slice(matrix, (0, i * CHUNK), (TILE, CHUNK))  2.76 us
    slice x1, local copies, waits for them, and re-layouts, shards(): strip = matrix[:, 0:TILE]  2.26 us
  transfers between devices with their start and end apart: 22, of which 5 were waited for; matrix products, arithmetic and copies ran while one was open for 7% of the time, Pallas kernels for 21%

profile of v4, /device:TPU:81, one launch (start us, length us, event | category | flops | bytes accessed | tf_op | source)
XLA Modules:
  0.0 110.7 jit_solution(7271329831791119593)
XLA Ops:
  0.0 1.0 slice.25
  1.0 2.8 %constant_dynamic-slice_fusion = (f32[256,512]{1,0:T(8,128)}, f32[256,512]{1,0:T(8,128)}, f32[256,512]{1,0:T(8,128)S(1)}, f32[256,512]{1,0:T(8,128)S(1)}) fusion(f32[1024,2048]{1,0:T(8,128)} %mat.3, s32[]{:T(128)S(6)} %select_n.233, s32[]{:T(128)S(6)} %select_n.230, s32[]{:T(128)S(6)} %select_n.227, s32[]{:T(128)S(6)} %select_n.223), kind=kLoop, calls=%fused_computation.26 | loop fusion | bytes 4194320 | tf_op jit(solution)/shard_map/dynamic_slice | solution.py:320
  4.4 1.4 %collective-permute-start.1 = (f32[256,256]{1,0:T(8,128)S(1)}, f32[256,256]{1,0:T(8,128)}, u32[]{:S(2)}, u32[]{:S(2)}) collective-permute-start(f32[256,256]{1,0:T(8,128)S(1)} %slice.25), channel_id=1, source_target_pairs={{0,4},{8,12},{9,13}} | collective-permute-start | bytes 786440 | tf_op jit(solution)/shard_map/ppermute | solution.py:30
  5.8 1.4 %collective-permute-start = (f32[256,256]{1,0:T(8,128)S(1)}, f32[256,256]{1,0:T(8,128)}, u32[]{:S(2)}, u32[]{:S(2)}) collective-permute-start(f32[256,256]{1,0:T(8,128)S(1)} %slice.25), channel_id=1, source_target_pairs={{0,2},{8,10},{9,11}} | collective-permute-start | bytes 786440 | tf_op jit(solution)/shard_map/ppermute | solution.py:30
  7.1 0.7 collective-permute-start.5
  7.8 1.3 %collective-permute-start.7 = (f32[256,512]{1,0:T(8,128)}, f32[256,512]{1,0:T(8,128)S(1)}, u32[]{:S(2)}, u32[]{:S(2)}) collective-permute-start(f32[256,512]{1,0:T(8,128)} %get-tuple-element.26), channel_id=1, source_target_pairs={{0,24},{2,26},{4,28},{6,30},{8,16},{10,18},{12,20},{14,22},{1,65},... | collective-permute-start | bytes 1572872 | tf_op jit(solution)/shard_map/ppermute | solution.py:30
  9.2 0.7 collective-permute-start.3
  9.9 1.0 select_select_fusion.4
  10.9 0.7 collective-permute-start.6
  11.6 1.3 %collective-permute-start.8 = (f32[256,256]{1,0:T(8,128)S(1)}, f32[256,256]{1,0:T(8,128)S(1)}, u32[]{:S(2)}, u32[]{:S(2)}) collective-permute-start(f32[256,256]{1,0:T(8,128)S(1)} %select_select_fusion.4), channel_id=1, source_target_pairs={{0,24},{2,26},{4,28},{6,30},{8,16},{10,18},{12,20},{14,22},{1,65},... | collective-permute-start | bytes 786440 | tf_op jit(solution)/shard_map/ppermute | solution.py:30
  13.7 6.3 %collective-permute-done.7 = f32[256,512]{1,0:T(8,128)S(1)} collective-permute-done((f32[256,512]{1,0:T(8,128)}, f32[256,512]{1,0:T(8,128)S(1)}, u32[]{:S(2)}, u32[]{:S(2)}) %collective-permute-start.7) | collective-permute-done | bytes 524320 | tf_op jit(solution)/shard_map/ppermute | solution.py:30
  20.0 8.3 %collective-permute-done.8 = f32[256,256]{1,0:T(8,128)S(1)} collective-permute-done((f32[256,256]{1,0:T(8,128)S(1)}, f32[256,256]{1,0:T(8,128)S(1)}, u32[]{:S(2)}, u32[]{:S(2)}) %collective-permute-start.8) | collective-permute-done | bytes 262176 | tf_op jit(solution)/shard_map/ppermute | solution.py:30
  28.8 3.1 %collective-permute-start.9 = (f32[256,768]{1,0:T(8,128)S(1)}, f32[256,768]{1,0:T(8,128)S(1)}, u32[]{:S(2)}, u32[]{:S(2)}) collective-permute-start(f32[256,768]{1,0:T(8,128)S(1)} %get-tuple-element.29), channel_id=1, source_target_pairs={{0,32},{2,34},{4,36},{6,38},{8,40},{10,42},{12,44},{14,46},{16,48}... | collective-permute-start | bytes 2359304 | tf_op jit(solution)/shard_map/ppermute | solution.py:30
  31.9 1.3 %collective-permute-start.10 = (f32[256,768]{1,0:T(8,128)S(1)}, f32[256,768]{1,0:T(8,128)S(1)}, u32[]{:S(2)}, u32[]{:S(2)}) collective-permute-start(f32[256,768]{1,0:T(8,128)S(1)} %get-tuple-element.30), channel_id=1, source_target_pairs={{0,96},{2,98},{4,100},{6,102},{8,104},{10,106},{12,108},{14,110},{... | collective-permute-start | bytes 2359304 | tf_op jit(solution)/shard_map/ppermute | solution.py:30
  33.3 2.3 %slice.30 = f32[1024,256]{1,0:T(8,128)} slice(f32[1024,2048]{1,0:T(8,128)} %mat.3), slice={[0:1024], [0:256]} | slice | bytes 2097152 | tf_op jit(solution)/shard_map/slice | solution.py:329
  35.5 1.6 %collective-permute-start.16 = (f32[1024,256]{1,0:T(8,128)}, f32[1024,256]{1,0:T(8,128)}, u32[]{:S(2)}, u32[]{:S(2)}) collective-permute-start(f32[1024,256]{1,0:T(8,128)} %slice.30), channel_id=1, source_target_pairs={{0,2},{8,10},{16,18},{24,26},{32,34},{40,42},{48,50},{56,58},{64,6... | collective-permute-start | bytes 3145736 | tf_op jit(solution)/shard_map/ppermute | solution.py:30
  37.2 1.6 %collective-permute-start.12 = (f32[256,768]{1,0:T(8,128)S(1)}, f32[256,768]{1,0:T(8,128)}, u32[]{:S(2)}, u32[]{:S(2)}) collective-permute-start(f32[256,768]{1,0:T(8,128)S(1)} %get-tuple-element.29), channel_id=1, source_target_pairs={{0,96},{2,98},{4,100},{6,102},{8,104},{10,106},{12,108},{14,110},{... | collective-permute-start | bytes 2359304 | tf_op jit(solution)/shard_map/ppermute | solution.py:30
  38.7 1.6 %collective-permute-start.13 = (f32[256,768]{1,0:T(8,128)S(1)}, f32[256,768]{1,0:T(8,128)}, u32[]{:S(2)}, u32[]{:S(2)}) collective-permute-start(f32[256,768]{1,0:T(8,128)S(1)} %get-tuple-element.30), channel_id=1, source_target_pairs={{0,32},{2,34},{4,36},{6,38},{8,40},{10,42},{12,44},{14,46},{16,48}... | collective-permute-start | bytes 2359304 | tf_op jit(solution)/shard_map/ppermute | solution.py:30
  40.3 1.5 %collective-permute-done.9 = f32[256,768]{1,0:T(8,128)S(1)} collective-permute-done((f32[256,768]{1,0:T(8,128)S(1)}, f32[256,768]{1,0:T(8,128)S(1)}, u32[]{:S(2)}, u32[]{:S(2)}) %collective-permute-start.9) | collective-permute-done | bytes 786464 | tf_op jit(solution)/shard_map/ppermute | solution.py:30
  42.1 1.0 broadcast_select_fusion.2
  43.1 1.5 %collective-permute-start.11 = (f32[256,768]{1,0:T(8,128)}, f32[256,768]{1,0:T(8,128)}, u32[]{:S(2)}, u32[]{:S(2)}) collective-permute-start(f32[256,768]{1,0:T(8,128)} %broadcast_select_fusion.2), channel_id=1, source_target_pairs={{32,64},{34,66},{36,68},{38,70},{40,72},{42,74},{44,76},{46,78},{4... | collective-permute-start | bytes 2359304 | tf_op jit(solution)/shard_map/ppermute | solution.py:30
  44.7 1.5 %collective-permute-start.14 = (f32[256,768]{1,0:T(8,128)S(1)}, f32[256,768]{1,0:T(8,128)}, u32[]{:S(2)}, u32[]{:S(2)}) collective-permute-start(f32[256,768]{1,0:T(8,128)S(1)} %collective-permute-done.10), channel_id=1, source_target_pairs={{96,64},{98,66},{100,68},{102,70},{104,72},{106,74},{108,76},{110,... | collective-permute-start | bytes 2359304 | tf_op jit(solution)/shard_map/ppermute | solution.py:30
  46.3 1.4 %broadcast_select_fusion = f32[1024,256]{1,0:T(8,128)S(1)} fusion(f32[1024,256]{1,0:T(8,128)} %collective-permute-done.16, pred[]{:T(512)S(6)} %eq.59, f32[1024,2048]{1,0:T(8,128)} %mat.3), kind=kLoop, calls=%fused_computation.9 | loop fusion | flops 262144 | bytes 3145729 | tf_op jit(solution)/shard_map/jit(_where)/select_n | solution.py:383
  47.6 1.3 %collective-permute-start.17 = (f32[1024,256]{1,0:T(8,128)S(1)}, f32[1024,256]{1,0:T(8,128)S(1)}, u32[]{:S(2)}, u32[]{:S(2)}) collective-permute-start(f32[1024,256]{1,0:T(8,128)S(1)} %broadcast_select_fusion), channel_id=1, source_target_pairs={{0,6},{8,14},{16,22},{24,30},{32,38},{40,46},{48,54},{56,62},{64,7... | collective-permute-start | bytes 3145736 | tf_op jit(solution)/shard_map/ppermute | solution.py:30
  49.0 1.5 %select_select_fusion.1 = (f32[256,768]{1,0:T(8,128)S(1)}, f32[256,768]{1,0:T(8,128)S(1)}) fusion(f32[256,768]{1,0:T(8,128)S(1)} %get-tuple-element.29, f32[256,768]{1,0:T(8,128)S(1)} %collective-permute-done.9, f32[256,768]{1,0:T(8,128)} %collective-permute-done.11, f32[256,768]{1,0:T(8,128)} %collective-permute-done.12, ...), kind=kLoop, calls=%fused_computation.3 | loop fusion | flops 2162688 | bytes 7864324 | tf_op jit(solution)/shard_map/jit(_where)/select_n | solution.py:325
  50.6 12.1 %collective-permute-start.15 = (f32[2,256,256]{2,1,0:T(8,128)S(1)}, f32[2,256,256]{2,1,0:T(8,128)S(1)}, u32[]{:S(2)}, u32[]{:S(2)}) collective-permute-start(f32[2,256,256]{2,1,0:T(8,128)S(1)} %pad_maximum_fusion.2), channel_id=1, source_target_pairs={{0,1},{1,0},{2,3},{3,2},{4,5},{5,4},{6,7},{7,6},{8,9},{9,8},{10,11... | collective-permute-start | bytes 1572872 | tf_op jit(solution)/shard_map/ppermute | solution.py:30
  63.3 1.2 %collective-permute-start.19 = (f32[2,256,512]{2,1,0:T(8,128)S(1)}, f32[2,256,512]{2,1,0:T(8,128)S(1)}, u32[]{:S(2)}, u32[]{:S(2)}) collective-permute-start(f32[2,256,512]{2,1,0:T(8,128)S(1)} %pad_maximum_fusion.refs_2_), channel_id=1, source_target_pairs={{0,8},{2,10},{4,12},{6,14},{32,40},{34,42},{36,44},{38,46},{64,72}... | collective-permute-start | bytes 3145736 | tf_op jit(solution)/shard_map/ppermute | solution.py:30
  64.5 11.3 %collective-permute-done.17 = f32[1024,256]{1,0:T(8,128)S(1)} collective-permute-done((f32[1024,256]{1,0:T(8,128)S(1)}, f32[1024,256]{1,0:T(8,128)S(1)}, u32[]{:S(2)}, u32[]{:S(2)}) %collective-permute-start.17) | collective-permute-done | bytes 1048608 | tf_op jit(solution)/shard_map/ppermute | solution.py:30
  76.4 7.8 %shard_map.17 = (f32[256,256]{1,0:T(8,128)S(1)}, f32[256,256]{1,0:T(8,128)S(1)}) custom-call(f32[256,256]{1,0:T(8,128)S(1)} %get-tuple-element.35.d00), custom_call_target="tpu_custom_call" | custom-call | flops 6000000000 | bytes 1048576 | tf_op jit(solution)/shard_map/pallas_call | solution.py:135
  84.2 9.4 %shard_map.18 = (f32[256,256]{1,0:T(8,128)S(1)}, f32[256,256]{1,0:T(8,128)S(1)}, f32[256,256]{1,0:T(8,128)S(1)}) custom-call(f32[256,256]{1,0:T(8,128)S(1)} %get-tuple-element.34.d10, f32[256,256]{1,0:T(8,128)S(1)} %get-tuple-element.33.d11, f32[256,256]{1,0:T(8,128)S(1)} %get-tuple-element.16.v00.v00_ref), custom_call_target="tpu_custom_call" | custom-call | flops 6000000000 | bytes 1048576 | tf_op jit(solution)/shard_map/pallas_call | solution.py:135
  93.6 6.2 %shard_map.19 = (f32[1024,2048]{1,0:T(8,128)}, bf16[1024,512]{1,0:T(8,128)(2,1)S(1)}, bf16[1024,512]{1,0:T(8,128)(2,1)S(1)}) custom-call(s32[2]{0:T(128)S(1)} %pad_add_fusion.place, f32[1024,2048]{1,0:T(8,128)S(1)} %bitcast.21, f32[256,256]{1,0:T(8,128)S(1)} %get-tuple-element.16.v00.v00_ref, f32[256,256]{1,0:T(8,128)S(1)} %get-tuple-element.17.v10_ref, ...), custom_call_target="tpu_custom_call" | custom-call | flops 3000000000 | bytes 6291456 | tf_op jit(solution)/shard_map/pallas_call | solution.py:262
  99.9 10.6 %shard_map.20 = f32[1024,2048]{1,0:T(8,128)} custom-call(s32[2]{0:T(128)S(1)} %pad_add_fusion.place, f32[1024,2048]{1,0:T(8,128)S(1)} %bitcast.21, f32[256,256]{1,0:T(8,128)S(1)} %get-tuple-element.16.v00.v00_ref, f32[256,256]{1,0:T(8,128)S(1)} %get-tuple-element.17.v10_ref, ...), custom_call_target="tpu_custom_call", output_to_operand_aliasing={{}: (12, {})} | custom-call | flops 8999999488 | bytes 18874368 | tf_op jit(solution)/shard_map/pallas_call | solution.py:262
  (42 shorter events, 3.4 us)
Async XLA Ops:
  3.7 5.4 %collective-permute-start.2 = (f32[256,256]{1,0:T(8,128)S(1)}, f32[256,256]{1,0:T(8,128)S(1)}, u32[]{:S(2)}, u32[]{:S(2)}) collective-permute-start(f32[256,256]{1,0:T(8,128)S(1)} %slice.25), channel_id=1, source_target_pairs={{0,6},{8,14},{9,15}} | collective-permute-start | bytes 786440 | tf_op jit(solution)/shard_map/ppermute | solution.py:30
  4.4 5.5 %collective-permute-start.1 = (f32[256,256]{1,0:T(8,128)S(1)}, f32[256,256]{1,0:T(8,128)}, u32[]{:S(2)}, u32[]{:S(2)}) collective-permute-start(f32[256,256]{1,0:T(8,128)S(1)} %slice.25), channel_id=1, source_target_pairs={{0,4},{8,12},{9,13}} | collective-permute-start | bytes 786440 | tf_op jit(solution)/shard_map/ppermute | solution.py:30
  5.8 4.1 %collective-permute-start = (f32[256,256]{1,0:T(8,128)S(1)}, f32[256,256]{1,0:T(8,128)}, u32[]{:S(2)}, u32[]{:S(2)}) collective-permute-start(f32[256,256]{1,0:T(8,128)S(1)} %slice.25), channel_id=1, source_target_pairs={{0,2},{8,10},{9,11}} | collective-permute-start | bytes 786440 | tf_op jit(solution)/shard_map/ppermute | solution.py:30
  7.1 5.8 %collective-permute-start.5 = (f32[256,512]{1,0:T(8,128)}, f32[256,512]{1,0:T(8,128)S(1)}, u32[]{:S(2)}, u32[]{:S(2)}) collective-permute-start(f32[256,512]{1,0:T(8,128)} %get-tuple-element.25), channel_id=1, source_target_pairs={{0,16},{2,18},{4,20},{6,22},{8,24},{10,26},{12,28},{14,30},{1,97},... | collective-permute-start | bytes 1572872 | tf_op jit(solution)/shard_map/ppermute | solution.py:30
  7.8 12.1 %collective-permute-start.7 = (f32[256,512]{1,0:T(8,128)}, f32[256,512]{1,0:T(8,128)S(1)}, u32[]{:S(2)}, u32[]{:S(2)}) collective-permute-start(f32[256,512]{1,0:T(8,128)} %get-tuple-element.26), channel_id=1, source_target_pairs={{0,24},{2,26},{4,28},{6,30},{8,16},{10,18},{12,20},{14,22},{1,65},... | collective-permute-start | bytes 1572872 | tf_op jit(solution)/shard_map/ppermute | solution.py:30
  9.2 19.2 %collective-permute-start.3 = (f32[256,512]{1,0:T(8,128)S(1)}, f32[256,512]{1,0:T(8,128)S(1)}, u32[]{:S(2)}, u32[]{:S(2)}) collective-permute-start(f32[256,512]{1,0:T(8,128)S(1)} %get-tuple-element.27), channel_id=1, source_target_pairs={{0,8},{2,10},{4,12},{6,14},{8,0},{10,2},{12,4},{14,6},{1,33},{3,35... | collective-permute-start | bytes 1572872 | tf_op jit(solution)/shard_map/ppermute | solution.py:30
  10.9 9.0 %collective-permute-start.6 = (f32[256,256]{1,0:T(8,128)S(1)}, f32[256,256]{1,0:T(8,128)S(1)}, u32[]{:S(2)}, u32[]{:S(2)}) collective-permute-start(f32[256,256]{1,0:T(8,128)S(1)} %select_select_fusion.4), channel_id=1, source_target_pairs={{0,16},{2,18},{4,20},{6,22},{8,24},{10,26},{12,28},{14,30},{1,97},... | collective-permute-start | bytes 786440 | tf_op jit(solution)/shard_map/ppermute | solution.py:30
  11.6 16.7 %collective-permute-start.8 = (f32[256,256]{1,0:T(8,128)S(1)}, f32[256,256]{1,0:T(8,128)S(1)}, u32[]{:S(2)}, u32[]{:S(2)}) collective-permute-start(f32[256,256]{1,0:T(8,128)S(1)} %select_select_fusion.4), channel_id=1, source_target_pairs={{0,24},{2,26},{4,28},{6,30},{8,16},{10,18},{12,20},{14,22},{1,65},... | collective-permute-start | bytes 786440 | tf_op jit(solution)/shard_map/ppermute | solution.py:30
  12.9 15.5 %collective-permute-start.4 = (f32[256,256]{1,0:T(8,128)S(1)}, f32[256,256]{1,0:T(8,128)S(1)}, u32[]{:S(2)}, u32[]{:S(2)}) collective-permute-start(f32[256,256]{1,0:T(8,128)S(1)} %select_select_fusion.4), channel_id=1, source_target_pairs={{0,8},{2,10},{4,12},{6,14},{8,0},{10,2},{12,4},{14,6},{1,33},{3,35... | collective-permute-start | bytes 786440 | tf_op jit(solution)/shard_map/ppermute | solution.py:30
  28.8 13.0 %collective-permute-start.9 = (f32[256,768]{1,0:T(8,128)S(1)}, f32[256,768]{1,0:T(8,128)S(1)}, u32[]{:S(2)}, u32[]{:S(2)}) collective-permute-start(f32[256,768]{1,0:T(8,128)S(1)} %get-tuple-element.29), channel_id=1, source_target_pairs={{0,32},{2,34},{4,36},{6,38},{8,40},{10,42},{12,44},{14,46},{16,48}... | collective-permute-start | bytes 2359304 | tf_op jit(solution)/shard_map/ppermute | solution.py:30
  31.9 10.2 %collective-permute-start.10 = (f32[256,768]{1,0:T(8,128)S(1)}, f32[256,768]{1,0:T(8,128)S(1)}, u32[]{:S(2)}, u32[]{:S(2)}) collective-permute-start(f32[256,768]{1,0:T(8,128)S(1)} %get-tuple-element.30), channel_id=1, source_target_pairs={{0,96},{2,98},{4,100},{6,102},{8,104},{10,106},{12,108},{14,110},{... | collective-permute-start | bytes 2359304 | tf_op jit(solution)/shard_map/ppermute | solution.py:30
  35.5 10.7 %collective-permute-start.16 = (f32[1024,256]{1,0:T(8,128)}, f32[1024,256]{1,0:T(8,128)}, u32[]{:S(2)}, u32[]{:S(2)}) collective-permute-start(f32[1024,256]{1,0:T(8,128)} %slice.30), channel_id=1, source_target_pairs={{0,2},{8,10},{16,18},{24,26},{32,34},{40,42},{48,50},{56,58},{64,6... | collective-permute-start | bytes 3145736 | tf_op jit(solution)/shard_map/ppermute | solution.py:30
  37.2 11.8 %collective-permute-start.12 = (f32[256,768]{1,0:T(8,128)S(1)}, f32[256,768]{1,0:T(8,128)}, u32[]{:S(2)}, u32[]{:S(2)}) collective-permute-start(f32[256,768]{1,0:T(8,128)S(1)} %get-tuple-element.29), channel_id=1, source_target_pairs={{0,96},{2,98},{4,100},{6,102},{8,104},{10,106},{12,108},{14,110},{... | collective-permute-start | bytes 2359304 | tf_op jit(solution)/shard_map/ppermute | solution.py:30
  38.7 10.2 %collective-permute-start.13 = (f32[256,768]{1,0:T(8,128)S(1)}, f32[256,768]{1,0:T(8,128)}, u32[]{:S(2)}, u32[]{:S(2)}) collective-permute-start(f32[256,768]{1,0:T(8,128)S(1)} %get-tuple-element.30), channel_id=1, source_target_pairs={{0,32},{2,34},{4,36},{6,38},{8,40},{10,42},{12,44},{14,46},{16,48}... | collective-permute-start | bytes 2359304 | tf_op jit(solution)/shard_map/ppermute | solution.py:30
  43.1 5.8 %collective-permute-start.11 = (f32[256,768]{1,0:T(8,128)}, f32[256,768]{1,0:T(8,128)}, u32[]{:S(2)}, u32[]{:S(2)}) collective-permute-start(f32[256,768]{1,0:T(8,128)} %broadcast_select_fusion.2), channel_id=1, source_target_pairs={{32,64},{34,66},{36,68},{38,70},{40,72},{42,74},{44,76},{46,78},{4... | collective-permute-start | bytes 2359304 | tf_op jit(solution)/shard_map/ppermute | solution.py:30
  44.7 4.3 %collective-permute-start.14 = (f32[256,768]{1,0:T(8,128)S(1)}, f32[256,768]{1,0:T(8,128)}, u32[]{:S(2)}, u32[]{:S(2)}) collective-permute-start(f32[256,768]{1,0:T(8,128)S(1)} %collective-permute-done.10), channel_id=1, source_target_pairs={{96,64},{98,66},{100,68},{102,70},{104,72},{106,74},{108,76},{110,... | collective-permute-start | bytes 2359304 | tf_op jit(solution)/shard_map/ppermute | solution.py:30
  47.6 28.2 %collective-permute-start.17 = (f32[1024,256]{1,0:T(8,128)S(1)}, f32[1024,256]{1,0:T(8,128)S(1)}, u32[]{:S(2)}, u32[]{:S(2)}) collective-permute-start(f32[1024,256]{1,0:T(8,128)S(1)} %broadcast_select_fusion), channel_id=1, source_target_pairs={{0,6},{8,14},{16,22},{24,30},{32,38},{40,46},{48,54},{56,62},{64,7... | collective-permute-start | bytes 3145736 | tf_op jit(solution)/shard_map/ppermute | solution.py:30
  50.6 25.7 %collective-permute-start.15 = (f32[2,256,256]{2,1,0:T(8,128)S(1)}, f32[2,256,256]{2,1,0:T(8,128)S(1)}, u32[]{:S(2)}, u32[]{:S(2)}) collective-permute-start(f32[2,256,256]{2,1,0:T(8,128)S(1)} %pad_maximum_fusion.2), channel_id=1, source_target_pairs={{0,1},{1,0},{2,3},{3,2},{4,5},{5,4},{6,7},{7,6},{8,9},{9,8},{10,11... | collective-permute-start | bytes 1572872 | tf_op jit(solution)/shard_map/ppermute | solution.py:30
  62.9 37.0 %collective-permute-start.21 = (f32[2,256,512]{2,1,0:T(8,128)S(1)}, f32[2,256,512]{2,1,0:T(8,128)S(1)}, u32[]{:S(2)}, u32[]{:S(2)}) collective-permute-start(f32[2,256,512]{2,1,0:T(8,128)S(1)} %pad_maximum_fusion.refs_2_), channel_id=1, source_target_pairs={{0,16},{2,18},{4,20},{6,22},{32,48},{34,50},{36,52},{38,54},{64,80... | collective-permute-start | bytes 3145736 | tf_op jit(solution)/shard_map/ppermute | solution.py:30
  63.0 36.9 %collective-permute-start.20 = (f32[2,256,512]{2,1,0:T(8,128)S(1)}, f32[2,256,512]{2,1,0:T(8,128)S(1)}, u32[]{:S(2)}, u32[]{:S(2)}) collective-permute-start(f32[2,256,512]{2,1,0:T(8,128)S(1)} %pad_maximum_fusion.refs_2_), channel_id=1, source_target_pairs={{0,24},{2,26},{4,28},{6,30},{32,56},{34,58},{36,60},{38,62},{64,88... | collective-permute-start | bytes 3145736 | tf_op jit(solution)/shard_map/ppermute | solution.py:30
  63.3 36.6 %collective-permute-start.19 = (f32[2,256,512]{2,1,0:T(8,128)S(1)}, f32[2,256,512]{2,1,0:T(8,128)S(1)}, u32[]{:S(2)}, u32[]{:S(2)}) collective-permute-start(f32[2,256,512]{2,1,0:T(8,128)S(1)} %pad_maximum_fusion.refs_2_), channel_id=1, source_target_pairs={{0,8},{2,10},{4,12},{6,14},{32,40},{34,42},{36,44},{38,46},{64,72}... | collective-permute-start | bytes 3145736 | tf_op jit(solution)/shard_map/ppermute | solution.py:30
  76.0 17.6 %collective-permute-start.18 = (f32[1024,256]{1,0:T(8,128)S(1)}, f32[1024,256]{1,0:T(8,128)S(1)}, u32[]{:S(2)}, u32[]{:S(2)}) collective-permute-start(f32[1024,256]{1,0:T(8,128)S(1)} %broadcast_select_fusion.1.refs_0_), channel_id=1, source_target_pairs={{0,1},{1,0},{2,3},{3,2},{4,5},{5,4},{6,7},{7,6},{8,9},{9,8},{10,11... | collective-permute-start | bytes 3145736 | tf_op jit(solution)/shard_map/ppermute | solution.py:30
  76.4 17.2 %slice-start = ((s8[8388608]{0:T(1024)(128)(4,1)}), s8[4194304]{0:T(1024)(128)(4,1)S(1)}, s32[]{:S(2)}) async-start(s8[8388608]{0:T(1024)(128)(4,1)} %bitcast.20), calls=%async_computation | async-start | bytes 8388608
  84.2 9.4 %slice-start.1 = ((s8[8388608]{0:T(1024)(128)(4,1)}), s8[4194304]{0:T(1024)(128)(4,1)S(1)}, s32[]{:S(2)}) async-start(s8[8388608]{0:T(1024)(128)(4,1)} %bitcast.20), calls=%async_computation.1 | async-start | bytes 8388608

commit v5 on v4

--- a/solution.py
+++ b/solution.py
@@ -103,11 +103,11 @@
     u01 = jnp.dot(v0, m[0:b, b:], precision=HIGHEST, preferred_element_type=F32)
     m[b:, b:] = m[b:, b:] - dot_tn(u01, u01, HIGHEST)
     u1, v1 = factor_block([m[b + 8 * g : b + 8 * g + 8, b:] for g in range(b // 8)])
-    w = dot_tn(u01, v0, HIGHEST)
+    w = dot3(halves(u01), halves(v0), TN)
     zeros = jnp.zeros((b, b), F32)
     v_ref[0:b, 0:b] = v0
     v_ref[0:b, b:] = zeros
-    v_ref[b:, 0:b] = -jnp.dot(v1, w, precision=HIGHEST, preferred_element_type=F32)
+    v_ref[b:, 0:b] = -dot3(halves(v1), halves(w), NN)
     v_ref[b:, b:] = v1
     l_ref[0:b, 0:b] = u0.T
     l_ref[0:b, b:] = zeros
@@ -126,8 +126,8 @@
     )
     m[...] = d11[...] - dot_tn(u01, u01, HIGHEST)
     factor_tile(m, v11, l11)
-    w = dot_tn(u01, v00[...], HIGHEST)
-    v10[...] = -jnp.dot(v11[...], w, precision=HIGHEST, preferred_element_type=F32)
+    w = dot3(halves(u01), halves(v00[...]), TN)
+    v10[...] = -dot3(halves(v11[...]), halves(w), NN)
 
 
 def factor_call(kernel, sizes, args, scratch=()):
@@ -159,6 +159,7 @@
     return out + lax.dot_general(al, bh, d, preferred_element_type=F32)
 
 
+TN = ((0,), (0,))
 NT = ((1,), (1,))
 NN = ((1,), (0,))
 CHUNK = 512
@@ -333,7 +334,7 @@
         along("z", [(0, 1)], 0) + along("z", [(0, 3)], 1),
         along("z", [(0, 3), (1, 2)], 0) + along("z", [(0, 1), (3, 2)], 1),
     )
-    spots = [((y0, x0, 0, c0), (y0, x0, k, c0)) for k in (2, 1, 3) for y0, x0, c0 in ((0, 0, 0), (0, 1, 0), (0, 1, 1))]
+    spots = [((y0, x0, 0, c0), (y0, x0, k, c0)) for k in (3, 2, 1) for y0, x0, c0 in ((0, 0, 0), (0, 1, 0), (0, 1, 1))]
     q0, *rest = [columns(i) for i in (
         pick(jnp.minimum(x, 1), 0),
         pick(1 - jnp.minimum(x, 1), 1),
@@ -341,7 +342,7 @@
         pick(jnp.where(x == 0, 2, 3), 3),
     )]
     tile = tied(tile, q0, *rest)
-    t2, t1, t3 = [send(tile, spots[i : i + 3]) for i in (0, 3, 6)]
+    t3, t2, t1 = [send(tile, spots[i : i + 3]) for i in (0, 3, 6)]
     tile = among(z, tile, t1, t2, t3)
 
     edge = {"y": (0,)}
@@ -379,7 +380,7 @@
     v00, l00 = factor_call(first_kernel, [TILE] * 2, (d00,), scratch)
     v10, v11, l11 = factor_call(second_kernel, [TILE] * 3, (d10, d11, v00), scratch)
 
-    r1 = send(tied(strip, t2), turns[0])
+    r1 = send(tied(strip, t1), turns[0])
     strip = jnp.where(z == first_stop, r1, strip)
     r2 = send(strip, turns[1])
     mine = jnp.where((z == 0) | (z == first_stop), strip, r2)

time: 111 us -> 111 us (level)
  no operation moved by 1% of the time
where the time goes in v5:
time: 111 us; the launch traced here: 110 us
  starting transfers between devices  36.3 us (33%)
  Pallas kernels  33.7 us (30%)
  waiting for transfers between devices  27.8 us (25%)
  local copies, waits for them, and re-layouts  6.32 us (6%)
  other arithmetic  5.63 us (5%)
    ppermute x22, starting transfers between devices, send(): return lax.ppermute(value, ('row', 'col'), pairs(moves))  36.3 us
    ppermute x22, waiting for transfers between devices, send(): return lax.ppermute(value, ('row', 'col'), pairs(moves))  27.8 us
    pallas_call x2, Pallas kernels, factor_call(): pl.pallas_call(kernel, out_shape=[jax.ShapeDtypeStruct((n, n), F32) for n...  16.9 us
    pallas_call x2, Pallas kernels, update_call(): pl.pallas_call(functools.partial(update_kernel, shifts, solve), out_shape...  16.8 us
    select_n x3, other arithmetic, among(): out = jnp.where(index == i, values[i], out)  2.9 us
    dynamic_slice x1, local copies, waits for them, and re-layouts, columns(): return lax.dynamic_slice(matrix, (0, i * CHUNK), (TILE, CHUNK))  2.76 us
    slice x1, local copies, waits for them, and re-layouts, shards(): strip = matrix[:, 0:TILE]  2.26 us
  transfers between devices with their start and end apart: 22, of which 5 were waited for; matrix products, arithmetic and copies ran while one was open for 7% of the time, Pallas kernels for 21%

profile of v5, /device:TPU:81, one launch (start us, length us, event | category | flops | bytes accessed | tf_op | source)
XLA Modules:
  0.0 110.4 jit_solution(16300021141474268732)
XLA Ops:
  0.0 1.0 slice.25
  1.0 2.8 %constant_dynamic-slice_fusion = (f32[256,512]{1,0:T(8,128)}, f32[256,512]{1,0:T(8,128)}, f32[256,512]{1,0:T(8,128)S(1)}, f32[256,512]{1,0:T(8,128)S(1)}) fusion(f32[1024,2048]{1,0:T(8,128)} %mat.3, s32[]{:T(128)S(6)} %select_n.233, s32[]{:T(128)S(6)} %select_n.230, s32[]{:T(128)S(6)} %select_n.227, s32[]{:T(128)S(6)} %select_n.223), kind=kLoop, calls=%fused_computation.26 | loop fusion | bytes 4194320 | tf_op jit(solution)/shard_map/dynamic_slice | solution.py:321
  4.4 1.4 %collective-permute-start.1 = (f32[256,256]{1,0:T(8,128)S(1)}, f32[256,256]{1,0:T(8,128)}, u32[]{:S(2)}, u32[]{:S(2)}) collective-permute-start(f32[256,256]{1,0:T(8,128)S(1)} %slice.25), channel_id=1, source_target_pairs={{0,4},{8,12},{9,13}} | collective-permute-start | bytes 786440 | tf_op jit(solution)/shard_map/ppermute | solution.py:30
  5.8 1.4 %collective-permute-start = (f32[256,256]{1,0:T(8,128)S(1)}, f32[256,256]{1,0:T(8,128)}, u32[]{:S(2)}, u32[]{:S(2)}) collective-permute-start(f32[256,256]{1,0:T(8,128)S(1)} %slice.25), channel_id=1, source_target_pairs={{0,2},{8,10},{9,11}} | collective-permute-start | bytes 786440 | tf_op jit(solution)/shard_map/ppermute | solution.py:30
  7.1 0.7 collective-permute-start.5
  7.8 1.3 %collective-permute-start.7 = (f32[256,512]{1,0:T(8,128)}, f32[256,512]{1,0:T(8,128)S(1)}, u32[]{:S(2)}, u32[]{:S(2)}) collective-permute-start(f32[256,512]{1,0:T(8,128)} %get-tuple-element.26), channel_id=1, source_target_pairs={{0,24},{2,26},{4,28},{6,30},{8,16},{10,18},{12,20},{14,22},{1,65},... | collective-permute-start | bytes 1572872 | tf_op jit(solution)/shard_map/ppermute | solution.py:30
  9.2 0.7 collective-permute-start.3
  9.9 1.0 select_select_fusion.4
  10.9 0.7 collective-permute-start.6
  11.6 1.3 %collective-permute-start.8 = (f32[256,256]{1,0:T(8,128)S(1)}, f32[256,256]{1,0:T(8,128)S(1)}, u32[]{:S(2)}, u32[]{:S(2)}) collective-permute-start(f32[256,256]{1,0:T(8,128)S(1)} %select_select_fusion.4), channel_id=1, source_target_pairs={{0,24},{2,26},{4,28},{6,30},{8,16},{10,18},{12,20},{14,22},{1,65},... | collective-permute-start | bytes 786440 | tf_op jit(solution)/shard_map/ppermute | solution.py:30
  13.7 6.3 %collective-permute-done.7 = f32[256,512]{1,0:T(8,128)S(1)} collective-permute-done((f32[256,512]{1,0:T(8,128)}, f32[256,512]{1,0:T(8,128)S(1)}, u32[]{:S(2)}, u32[]{:S(2)}) %collective-permute-start.7) | collective-permute-done | bytes 524320 | tf_op jit(solution)/shard_map/ppermute | solution.py:30
  20.0 8.3 %collective-permute-done.8 = f32[256,256]{1,0:T(8,128)S(1)} collective-permute-done((f32[256,256]{1,0:T(8,128)S(1)}, f32[256,256]{1,0:T(8,128)S(1)}, u32[]{:S(2)}, u32[]{:S(2)}) %collective-permute-start.8) | collective-permute-done | bytes 262176 | tf_op jit(solution)/shard_map/ppermute | solution.py:30
  28.8 3.1 %collective-permute-start.9 = (f32[256,768]{1,0:T(8,128)S(1)}, f32[256,768]{1,0:T(8,128)S(1)}, u32[]{:S(2)}, u32[]{:S(2)}) collective-permute-start(f32[256,768]{1,0:T(8,128)S(1)} %get-tuple-element.29), channel_id=1, source_target_pairs={{0,32},{2,34},{4,36},{6,38},{8,40},{10,42},{12,44},{14,46},{16,48}... | collective-permute-start | bytes 2359304 | tf_op jit(solution)/shard_map/ppermute | solution.py:30
  31.9 1.3 %collective-permute-start.10 = (f32[256,768]{1,0:T(8,128)S(1)}, f32[256,768]{1,0:T(8,128)S(1)}, u32[]{:S(2)}, u32[]{:S(2)}) collective-permute-start(f32[256,768]{1,0:T(8,128)S(1)} %get-tuple-element.30), channel_id=1, source_target_pairs={{0,96},{2,98},{4,100},{6,102},{8,104},{10,106},{12,108},{14,110},{... | collective-permute-start | bytes 2359304 | tf_op jit(solution)/shard_map/ppermute | solution.py:30
  33.3 2.3 %slice.30 = f32[1024,256]{1,0:T(8,128)} slice(f32[1024,2048]{1,0:T(8,128)} %mat.3), slice={[0:1024], [0:256]} | slice | bytes 2097152 | tf_op jit(solution)/shard_map/slice | solution.py:330
  35.5 1.6 %collective-permute-start.16 = (f32[1024,256]{1,0:T(8,128)}, f32[1024,256]{1,0:T(8,128)}, u32[]{:S(2)}, u32[]{:S(2)}) collective-permute-start(f32[1024,256]{1,0:T(8,128)} %slice.30), channel_id=1, source_target_pairs={{0,2},{8,10},{16,18},{24,26},{32,34},{40,42},{48,50},{56,58},{64,6... | collective-permute-start | bytes 3145736 | tf_op jit(solution)/shard_map/ppermute | solution.py:30
  37.2 1.6 %collective-permute-start.12 = (f32[256,768]{1,0:T(8,128)S(1)}, f32[256,768]{1,0:T(8,128)}, u32[]{:S(2)}, u32[]{:S(2)}) collective-permute-start(f32[256,768]{1,0:T(8,128)S(1)} %get-tuple-element.29), channel_id=1, source_target_pairs={{0,96},{2,98},{4,100},{6,102},{8,104},{10,106},{12,108},{14,110},{... | collective-permute-start | bytes 2359304 | tf_op jit(solution)/shard_map/ppermute | solution.py:30
  38.7 1.6 %collective-permute-start.13 = (f32[256,768]{1,0:T(8,128)S(1)}, f32[256,768]{1,0:T(8,128)}, u32[]{:S(2)}, u32[]{:S(2)}) collective-permute-start(f32[256,768]{1,0:T(8,128)S(1)} %get-tuple-element.30), channel_id=1, source_target_pairs={{0,32},{2,34},{4,36},{6,38},{8,40},{10,42},{12,44},{14,46},{16,48}... | collective-permute-start | bytes 2359304 | tf_op jit(solution)/shard_map/ppermute | solution.py:30
  40.3 1.5 %collective-permute-done.9 = f32[256,768]{1,0:T(8,128)S(1)} collective-permute-done((f32[256,768]{1,0:T(8,128)S(1)}, f32[256,768]{1,0:T(8,128)S(1)}, u32[]{:S(2)}, u32[]{:S(2)}) %collective-permute-start.9) | collective-permute-done | bytes 786464 | tf_op jit(solution)/shard_map/ppermute | solution.py:30
  42.1 1.0 broadcast_select_fusion.2
  43.1 1.5 %collective-permute-start.11 = (f32[256,768]{1,0:T(8,128)}, f32[256,768]{1,0:T(8,128)}, u32[]{:S(2)}, u32[]{:S(2)}) collective-permute-start(f32[256,768]{1,0:T(8,128)} %broadcast_select_fusion.2), channel_id=1, source_target_pairs={{32,64},{34,66},{36,68},{38,70},{40,72},{42,74},{44,76},{46,78},{4... | collective-permute-start | bytes 2359304 | tf_op jit(solution)/shard_map/ppermute | solution.py:30
  44.7 1.5 %collective-permute-start.14 = (f32[256,768]{1,0:T(8,128)S(1)}, f32[256,768]{1,0:T(8,128)}, u32[]{:S(2)}, u32[]{:S(2)}) collective-permute-start(f32[256,768]{1,0:T(8,128)S(1)} %collective-permute-done.10), channel_id=1, source_target_pairs={{96,64},{98,66},{100,68},{102,70},{104,72},{106,74},{108,76},{110,... | collective-permute-start | bytes 2359304 | tf_op jit(solution)/shard_map/ppermute | solution.py:30
  46.3 1.4 %broadcast_select_fusion = f32[1024,256]{1,0:T(8,128)S(1)} fusion(f32[1024,256]{1,0:T(8,128)} %collective-permute-done.16, pred[]{:T(512)S(6)} %eq.59, f32[1024,2048]{1,0:T(8,128)} %mat.3), kind=kLoop, calls=%fused_computation.9 | loop fusion | flops 262144 | bytes 3145729 | tf_op jit(solution)/shard_map/jit(_where)/select_n | solution.py:384
  47.6 1.3 %collective-permute-start.17 = (f32[1024,256]{1,0:T(8,128)S(1)}, f32[1024,256]{1,0:T(8,128)S(1)}, u32[]{:S(2)}, u32[]{:S(2)}) collective-permute-start(f32[1024,256]{1,0:T(8,128)S(1)} %broadcast_select_fusion), channel_id=1, source_target_pairs={{0,6},{8,14},{16,22},{24,30},{32,38},{40,46},{48,54},{56,62},{64,7... | collective-permute-start | bytes 3145736 | tf_op jit(solution)/shard_map/ppermute | solution.py:30
  49.0 1.5 %select_select_fusion.1 = (f32[256,768]{1,0:T(8,128)S(1)}, f32[256,768]{1,0:T(8,128)S(1)}) fusion(f32[256,768]{1,0:T(8,128)S(1)} %get-tuple-element.29, f32[256,768]{1,0:T(8,128)S(1)} %collective-permute-done.9, f32[256,768]{1,0:T(8,128)} %collective-permute-done.11, f32[256,768]{1,0:T(8,128)} %collective-permute-done.12, ...), kind=kLoop, calls=%fused_computation.3 | loop fusion | flops 2162688 | bytes 7864324 | tf_op jit(solution)/shard_map/jit(_where)/select_n | solution.py:326
  50.6 12.1 %collective-permute-start.15 = (f32[2,256,256]{2,1,0:T(8,128)S(1)}, f32[2,256,256]{2,1,0:T(8,128)S(1)}, u32[]{:S(2)}, u32[]{:S(2)}) collective-permute-start(f32[2,256,256]{2,1,0:T(8,128)S(1)} %pad_maximum_fusion.2), channel_id=1, source_target_pairs={{0,1},{1,0},{2,3},{3,2},{4,5},{5,4},{6,7},{7,6},{8,9},{9,8},{10,11... | collective-permute-start | bytes 1572872 | tf_op jit(solution)/shard_map/ppermute | solution.py:30
  63.3 1.2 %collective-permute-start.19 = (f32[2,256,512]{2,1,0:T(8,128)S(1)}, f32[2,256,512]{2,1,0:T(8,128)S(1)}, u32[]{:S(2)}, u32[]{:S(2)}) collective-permute-start(f32[2,256,512]{2,1,0:T(8,128)S(1)} %pad_maximum_fusion.refs_2_), channel_id=1, source_target_pairs={{0,8},{2,10},{4,12},{6,14},{32,40},{34,42},{36,44},{38,46},{64,72}... | collective-permute-start | bytes 3145736 | tf_op jit(solution)/shard_map/ppermute | solution.py:30
  64.5 11.3 %collective-permute-done.17 = f32[1024,256]{1,0:T(8,128)S(1)} collective-permute-done((f32[1024,256]{1,0:T(8,128)S(1)}, f32[1024,256]{1,0:T(8,128)S(1)}, u32[]{:S(2)}, u32[]{:S(2)}) %collective-permute-start.17) | collective-permute-done | bytes 1048608 | tf_op jit(solution)/shard_map/ppermute | solution.py:30
  76.4 7.7 %shard_map.17 = (f32[256,256]{1,0:T(8,128)S(1)}, f32[256,256]{1,0:T(8,128)S(1)}) custom-call(f32[256,256]{1,0:T(8,128)S(1)} %get-tuple-element.35.d00), custom_call_target="tpu_custom_call" | custom-call | flops 6000000000 | bytes 1048576 | tf_op jit(solution)/shard_map/pallas_call | solution.py:135
  84.2 9.2 %shard_map.18 = (f32[256,256]{1,0:T(8,128)S(1)}, f32[256,256]{1,0:T(8,128)S(1)}, f32[256,256]{1,0:T(8,128)S(1)}) custom-call(f32[256,256]{1,0:T(8,128)S(1)} %get-tuple-element.34.d10, f32[256,256]{1,0:T(8,128)S(1)} %get-tuple-element.33.d11, f32[256,256]{1,0:T(8,128)S(1)} %get-tuple-element.16.v00.v00_ref), custom_call_target="tpu_custom_call" | custom-call | flops 6000000000 | bytes 1048576 | tf_op jit(solution)/shard_map/pallas_call | solution.py:135
  93.4 6.2 %shard_map.19 = (f32[1024,2048]{1,0:T(8,128)}, bf16[1024,512]{1,0:T(8,128)(2,1)S(1)}, bf16[1024,512]{1,0:T(8,128)(2,1)S(1)}) custom-call(s32[2]{0:T(128)S(1)} %pad_add_fusion.place, f32[1024,2048]{1,0:T(8,128)S(1)} %bitcast.21, f32[256,256]{1,0:T(8,128)S(1)} %get-tuple-element.16.v00.v00_ref, f32[256,256]{1,0:T(8,128)S(1)} %get-tuple-element.17.v10_ref, ...), custom_call_target="tpu_custom_call" | custom-call | flops 3000000000 | bytes 6291456 | tf_op jit(solution)/shard_map/pallas_call | solution.py:263
  99.6 10.6 %shard_map.20 = f32[1024,2048]{1,0:T(8,128)} custom-call(s32[2]{0:T(128)S(1)} %pad_add_fusion.place, f32[1024,2048]{1,0:T(8,128)S(1)} %bitcast.21, f32[256,256]{1,0:T(8,128)S(1)} %get-tuple-element.16.v00.v00_ref, f32[256,256]{1,0:T(8,128)S(1)} %get-tuple-element.17.v10_ref, ...), custom_call_target="tpu_custom_call", output_to_operand_aliasing={{}: (12, {})} | custom-call | flops 8999999488 | bytes 18874368 | tf_op jit(solution)/shard_map/pallas_call | solution.py:263
  (42 shorter events, 3.4 us)
Async XLA Ops:
  3.7 5.4 %collective-permute-start.2 = (f32[256,256]{1,0:T(8,128)S(1)}, f32[256,256]{1,0:T(8,128)S(1)}, u32[]{:S(2)}, u32[]{:S(2)}) collective-permute-start(f32[256,256]{1,0:T(8,128)S(1)} %slice.25), channel_id=1, source_target_pairs={{0,6},{8,14},{9,15}} | collective-permute-start | bytes 786440 | tf_op jit(solution)/shard_map/ppermute | solution.py:30
  4.4 5.5 %collective-permute-start.1 = (f32[256,256]{1,0:T(8,128)S(1)}, f32[256,256]{1,0:T(8,128)}, u32[]{:S(2)}, u32[]{:S(2)}) collective-permute-start(f32[256,256]{1,0:T(8,128)S(1)} %slice.25), channel_id=1, source_target_pairs={{0,4},{8,12},{9,13}} | collective-permute-start | bytes 786440 | tf_op jit(solution)/shard_map/ppermute | solution.py:30
  5.8 4.1 %collective-permute-start = (f32[256,256]{1,0:T(8,128)S(1)}, f32[256,256]{1,0:T(8,128)}, u32[]{:S(2)}, u32[]{:S(2)}) collective-permute-start(f32[256,256]{1,0:T(8,128)S(1)} %slice.25), channel_id=1, source_target_pairs={{0,2},{8,10},{9,11}} | collective-permute-start | bytes 786440 | tf_op jit(solution)/shard_map/ppermute | solution.py:30
  7.1 5.8 %collective-permute-start.5 = (f32[256,512]{1,0:T(8,128)}, f32[256,512]{1,0:T(8,128)S(1)}, u32[]{:S(2)}, u32[]{:S(2)}) collective-permute-start(f32[256,512]{1,0:T(8,128)} %get-tuple-element.25), channel_id=1, source_target_pairs={{0,16},{2,18},{4,20},{6,22},{8,24},{10,26},{12,28},{14,30},{1,97},... | collective-permute-start | bytes 1572872 | tf_op jit(solution)/shard_map/ppermute | solution.py:30
  7.8 12.1 %collective-permute-start.7 = (f32[256,512]{1,0:T(8,128)}, f32[256,512]{1,0:T(8,128)S(1)}, u32[]{:S(2)}, u32[]{:S(2)}) collective-permute-start(f32[256,512]{1,0:T(8,128)} %get-tuple-element.26), channel_id=1, source_target_pairs={{0,24},{2,26},{4,28},{6,30},{8,16},{10,18},{12,20},{14,22},{1,65},... | collective-permute-start | bytes 1572872 | tf_op jit(solution)/shard_map/ppermute | solution.py:30
  9.2 19.2 %collective-permute-start.3 = (f32[256,512]{1,0:T(8,128)S(1)}, f32[256,512]{1,0:T(8,128)S(1)}, u32[]{:S(2)}, u32[]{:S(2)}) collective-permute-start(f32[256,512]{1,0:T(8,128)S(1)} %get-tuple-element.27), channel_id=1, source_target_pairs={{0,8},{2,10},{4,12},{6,14},{8,0},{10,2},{12,4},{14,6},{1,33},{3,35... | collective-permute-start | bytes 1572872 | tf_op jit(solution)/shard_map/ppermute | solution.py:30
  10.9 9.0 %collective-permute-start.6 = (f32[256,256]{1,0:T(8,128)S(1)}, f32[256,256]{1,0:T(8,128)S(1)}, u32[]{:S(2)}, u32[]{:S(2)}) collective-permute-start(f32[256,256]{1,0:T(8,128)S(1)} %select_select_fusion.4), channel_id=1, source_target_pairs={{0,16},{2,18},{4,20},{6,22},{8,24},{10,26},{12,28},{14,30},{1,97},... | collective-permute-start | bytes 786440 | tf_op jit(solution)/shard_map/ppermute | solution.py:30
  11.6 16.7 %collective-permute-start.8 = (f32[256,256]{1,0:T(8,128)S(1)}, f32[256,256]{1,0:T(8,128)S(1)}, u32[]{:S(2)}, u32[]{:S(2)}) collective-permute-start(f32[256,256]{1,0:T(8,128)S(1)} %select_select_fusion.4), channel_id=1, source_target_pairs={{0,24},{2,26},{4,28},{6,30},{8,16},{10,18},{12,20},{14,22},{1,65},... | collective-permute-start | bytes 786440 | tf_op jit(solution)/shard_map/ppermute | solution.py:30
  12.9 15.5 %collective-permute-start.4 = (f32[256,256]{1,0:T(8,128)S(1)}, f32[256,256]{1,0:T(8,128)S(1)}, u32[]{:S(2)}, u32[]{:S(2)}) collective-permute-start(f32[256,256]{1,0:T(8,128)S(1)} %select_select_fusion.4), channel_id=1, source_target_pairs={{0,8},{2,10},{4,12},{6,14},{8,0},{10,2},{12,4},{14,6},{1,33},{3,35... | collective-permute-start | bytes 786440 | tf_op jit(solution)/shard_map/ppermute | solution.py:30
  28.8 13.0 %collective-permute-start.9 = (f32[256,768]{1,0:T(8,128)S(1)}, f32[256,768]{1,0:T(8,128)S(1)}, u32[]{:S(2)}, u32[]{:S(2)}) collective-permute-start(f32[256,768]{1,0:T(8,128)S(1)} %get-tuple-element.29), channel_id=1, source_target_pairs={{0,32},{2,34},{4,36},{6,38},{8,40},{10,42},{12,44},{14,46},{16,48}... | collective-permute-start | bytes 2359304 | tf_op jit(solution)/shard_map/ppermute | solution.py:30
  31.9 10.2 %collective-permute-start.10 = (f32[256,768]{1,0:T(8,128)S(1)}, f32[256,768]{1,0:T(8,128)S(1)}, u32[]{:S(2)}, u32[]{:S(2)}) collective-permute-start(f32[256,768]{1,0:T(8,128)S(1)} %get-tuple-element.30), channel_id=1, source_target_pairs={{0,96},{2,98},{4,100},{6,102},{8,104},{10,106},{12,108},{14,110},{... | collective-permute-start | bytes 2359304 | tf_op jit(solution)/shard_map/ppermute | solution.py:30
  35.5 10.7 %collective-permute-start.16 = (f32[1024,256]{1,0:T(8,128)}, f32[1024,256]{1,0:T(8,128)}, u32[]{:S(2)}, u32[]{:S(2)}) collective-permute-start(f32[1024,256]{1,0:T(8,128)} %slice.30), channel_id=1, source_target_pairs={{0,2},{8,10},{16,18},{24,26},{32,34},{40,42},{48,50},{56,58},{64,6... | collective-permute-start | bytes 3145736 | tf_op jit(solution)/shard_map/ppermute | solution.py:30
  37.2 11.8 %collective-permute-start.12 = (f32[256,768]{1,0:T(8,128)S(1)}, f32[256,768]{1,0:T(8,128)}, u32[]{:S(2)}, u32[]{:S(2)}) collective-permute-start(f32[256,768]{1,0:T(8,128)S(1)} %get-tuple-element.29), channel_id=1, source_target_pairs={{0,96},{2,98},{4,100},{6,102},{8,104},{10,106},{12,108},{14,110},{... | collective-permute-start | bytes 2359304 | tf_op jit(solution)/shard_map/ppermute | solution.py:30
  38.7 10.2 %collective-permute-start.13 = (f32[256,768]{1,0:T(8,128)S(1)}, f32[256,768]{1,0:T(8,128)}, u32[]{:S(2)}, u32[]{:S(2)}) collective-permute-start(f32[256,768]{1,0:T(8,128)S(1)} %get-tuple-element.30), channel_id=1, source_target_pairs={{0,32},{2,34},{4,36},{6,38},{8,40},{10,42},{12,44},{14,46},{16,48}... | collective-permute-start | bytes 2359304 | tf_op jit(solution)/shard_map/ppermute | solution.py:30
  43.1 5.8 %collective-permute-start.11 = (f32[256,768]{1,0:T(8,128)}, f32[256,768]{1,0:T(8,128)}, u32[]{:S(2)}, u32[]{:S(2)}) collective-permute-start(f32[256,768]{1,0:T(8,128)} %broadcast_select_fusion.2), channel_id=1, source_target_pairs={{32,64},{34,66},{36,68},{38,70},{40,72},{42,74},{44,76},{46,78},{4... | collective-permute-start | bytes 2359304 | tf_op jit(solution)/shard_map/ppermute | solution.py:30
  44.7 4.3 %collective-permute-start.14 = (f32[256,768]{1,0:T(8,128)S(1)}, f32[256,768]{1,0:T(8,128)}, u32[]{:S(2)}, u32[]{:S(2)}) collective-permute-start(f32[256,768]{1,0:T(8,128)S(1)} %collective-permute-done.10), channel_id=1, source_target_pairs={{96,64},{98,66},{100,68},{102,70},{104,72},{106,74},{108,76},{110,... | collective-permute-start | bytes 2359304 | tf_op jit(solution)/shard_map/ppermute | solution.py:30
  47.6 28.2 %collective-permute-start.17 = (f32[1024,256]{1,0:T(8,128)S(1)}, f32[1024,256]{1,0:T(8,128)S(1)}, u32[]{:S(2)}, u32[]{:S(2)}) collective-permute-start(f32[1024,256]{1,0:T(8,128)S(1)} %broadcast_select_fusion), channel_id=1, source_target_pairs={{0,6},{8,14},{16,22},{24,30},{32,38},{40,46},{48,54},{56,62},{64,7... | collective-permute-start | bytes 3145736 | tf_op jit(solution)/shard_map/ppermute | solution.py:30
  50.6 25.7 %collective-permute-start.15 = (f32[2,256,256]{2,1,0:T(8,128)S(1)}, f32[2,256,256]{2,1,0:T(8,128)S(1)}, u32[]{:S(2)}, u32[]{:S(2)}) collective-permute-start(f32[2,256,256]{2,1,0:T(8,128)S(1)} %pad_maximum_fusion.2), channel_id=1, source_target_pairs={{0,1},{1,0},{2,3},{3,2},{4,5},{5,4},{6,7},{7,6},{8,9},{9,8},{10,11... | collective-permute-start | bytes 1572872 | tf_op jit(solution)/shard_map/ppermute | solution.py:30
  62.9 36.7 %collective-permute-start.21 = (f32[2,256,512]{2,1,0:T(8,128)S(1)}, f32[2,256,512]{2,1,0:T(8,128)S(1)}, u32[]{:S(2)}, u32[]{:S(2)}) collective-permute-start(f32[2,256,512]{2,1,0:T(8,128)S(1)} %pad_maximum_fusion.refs_2_), channel_id=1, source_target_pairs={{0,16},{2,18},{4,20},{6,22},{32,48},{34,50},{36,52},{38,54},{64,80... | collective-permute-start | bytes 3145736 | tf_op jit(solution)/shard_map/ppermute | solution.py:30
  63.0 36.6 %collective-permute-start.20 = (f32[2,256,512]{2,1,0:T(8,128)S(1)}, f32[2,256,512]{2,1,0:T(8,128)S(1)}, u32[]{:S(2)}, u32[]{:S(2)}) collective-permute-start(f32[2,256,512]{2,1,0:T(8,128)S(1)} %pad_maximum_fusion.refs_2_), channel_id=1, source_target_pairs={{0,24},{2,26},{4,28},{6,30},{32,56},{34,58},{36,60},{38,62},{64,88... | collective-permute-start | bytes 3145736 | tf_op jit(solution)/shard_map/ppermute | solution.py:30
  63.3 36.3 %collective-permute-start.19 = (f32[2,256,512]{2,1,0:T(8,128)S(1)}, f32[2,256,512]{2,1,0:T(8,128)S(1)}, u32[]{:S(2)}, u32[]{:S(2)}) collective-permute-start(f32[2,256,512]{2,1,0:T(8,128)S(1)} %pad_maximum_fusion.refs_2_), channel_id=1, source_target_pairs={{0,8},{2,10},{4,12},{6,14},{32,40},{34,42},{36,44},{38,46},{64,72}... | collective-permute-start | bytes 3145736 | tf_op jit(solution)/shard_map/ppermute | solution.py:30
  76.0 17.3 %collective-permute-start.18 = (f32[1024,256]{1,0:T(8,128)S(1)}, f32[1024,256]{1,0:T(8,128)S(1)}, u32[]{:S(2)}, u32[]{:S(2)}) collective-permute-start(f32[1024,256]{1,0:T(8,128)S(1)} %broadcast_select_fusion.1.refs_0_), channel_id=1, source_target_pairs={{0,1},{1,0},{2,3},{3,2},{4,5},{5,4},{6,7},{7,6},{8,9},{9,8},{10,11... | collective-permute-start | bytes 3145736 | tf_op jit(solution)/shard_map/ppermute | solution.py:30
  76.4 16.9 %slice-start = ((s8[8388608]{0:T(1024)(128)(4,1)}), s8[4194304]{0:T(1024)(128)(4,1)S(1)}, s32[]{:S(2)}) async-start(s8[8388608]{0:T(1024)(128)(4,1)} %bitcast.20), calls=%async_computation | async-start | bytes 8388608
  84.1 9.2 %slice-start.1 = ((s8[8388608]{0:T(1024)(128)(4,1)}), s8[4194304]{0:T(1024)(128)(4,1)S(1)}, s32[]{:S(2)}) async-start(s8[8388608]{0:T(1024)(128)(4,1)} %bitcast.20), calls=%async_computation.1 | async-start | bytes 8388608
